TPU v7x, 32 devices: a whole 2x2x4 slice. The times are simulated.
32 devices in a mesh: prompt: 4 (over z), seq: 8 (over y, x, core).
Axes of the slice: x: 2, y: 2, z: 4, core: 2. Of those that a mesh axis runs over, the one named last changes fastest.
Arguments:
- queries: bfloat16 [4, 8, 2, 32, 128], P('prompt', 'seq'), may hold values from -160 to 160
- prompt_key_cache: bfloat16 [4, 4, 2048, 128], P('prompt', None, 'seq'), may hold values from -5 to 5
- prompt_value_cache: bfloat16 [4, 4, 2048, 128], P('prompt', None, 'seq'), may hold values from -6 to 6
- kept: int32 [4, 4, 8], P('prompt', None, 'seq'), may hold values from 1 to 2, as said below
- sample_keys: bfloat16 [4, 8, 4, 256, 128], P('prompt', 'seq'), may hold values from -6 to 6
- sample_values: bfloat16 [4, 8, 4, 256, 128], P('prompt', 'seq'), may hold values from -6 to 6
- suffix_len: int32 [4, 8], P('prompt', 'seq'), may hold values from 1 to 256, as said below
- decode_keys: bfloat16 [4, 8, 2, 4, 128], P('prompt', 'seq'), may hold values from -6 to 6
- decode_values: bfloat16 [4, 8, 2, 4, 128], P('prompt', 'seq'), may hold values from -6 to 6
- out_weight: bfloat16 [4096, 8192], P('seq', 'prompt'), may hold values from -0.1875 to 0.1875
Outputs:
- attn_out: bfloat16 [64, 8192], P('seq', 'prompt')
Inputs may be any that keep to these rules, and one draw needn't show every extreme that they name: `kept`: for every prompt and key-value head some seq index has all 2 slots live. `suffix_len`: in every prompt some sample has 256 generated tokens.
All inputs are finite; a program needn't handle non-finite values.
Results may differ from a plain program's by a relative error of at most 0.0048.
Values may be sent and summed in bfloat16 or wider, within the bound.
No kernel may reach another device: no remote copies, remote signals or barrier semaphores. Data moves between devices by JAX's collectives and lax.ppermute only.
A program may use at most 128 MiB of HBM per device.

v0:
```python
import math

import jax
import jax.numpy as jnp
from jax import lax
from jax.sharding import PartitionSpec as P

BLOCK_TOKENS = 128
KEPT_SLOTS = 2


NEGATIVE = -1e30


def joined(x, axis, combine):
    everything = jax.tree.map(lambda part: lax.all_gather(part, axis), x)
    initial = jax.tree.map(lambda part: part[0], everything)

    def lap(k, so_far):
        return combine(so_far, jax.tree.map(lambda part: part[k], everything))

    return lax.fori_loop(1, lax.axis_size(axis), lap, initial)


def combine(earlier, later):
    highest = jnp.maximum(earlier[0], later[0])
    early_factor = jnp.exp(earlier[0] - highest)
    late_factor = jnp.exp(later[0] - highest)
    softmax_total = earlier[1] * early_factor + later[1] * late_factor
    summed = earlier[2] * early_factor[..., None] + later[2] * late_factor[..., None]
    return (highest, softmax_total, summed)


def on_device(
    queries,
    prompt_key_cache,
    prompt_value_cache,
    kept,
    sample_keys,
    sample_values,
    suffix_len,
    decode_keys,
    decode_values,
    out_weight,
):
    seq_count = lax.axis_size("seq")
    seq_index = lax.axis_index("seq")
    own_count = queries.shape[1]
    step_count = queries.shape[2]
    head_count = queries.shape[3]
    head_dim = queries.shape[4]
    kv_count = prompt_key_cache.shape[1]
    group_size = head_count // kv_count
    logit_scale = 1.0 / math.sqrt(head_dim)
    gathered = lax.all_gather(queries, "seq", axis=1, tiled=True)
    sample_count = gathered.shape[1]
    grouped_queries = gathered[0].reshape(sample_count, step_count, kv_count, group_size, head_dim)
    query_rows = jnp.transpose(grouped_queries, (2, 0, 1, 3, 4)).reshape(
        kv_count, sample_count * step_count * group_size, head_dim
    )
    key_cache_store = prompt_key_cache[0].reshape(kv_count, KEPT_SLOTS, BLOCK_TOKENS, head_dim)
    value_cache_store = prompt_value_cache[0].reshape(kv_count, KEPT_SLOTS, BLOCK_TOKENS, head_dim)
    kept_block_counts = kept[0, :, 0]
    active_mask = jnp.arange(KEPT_SLOTS, dtype=jnp.int32)[None, :] < kept_block_counts[:, None]

    def one_head(pieces):
        head_row_block, key_block_list, value_block_list, live_blocks = pieces
        logit_scores = (
            jnp.einsum(
                "eg,mxg->emx", head_row_block, key_block_list, preferred_element_type=jnp.float32
            )
            * logit_scale
        )
        block_max = jnp.where(live_blocks[None, :], jnp.max(logit_scores, axis=2), NEGATIVE)
        attention_weights = jnp.where(
            live_blocks[None, :, None], jnp.exp(logit_scores - block_max[:, :, None]), 0.0
        )
        block_sum = jnp.sum(attention_weights, axis=2)
        block_output = jnp.einsum(
            "yaf,afi->yai",
            attention_weights.astype(jnp.bfloat16),
            value_block_list,
            preferred_element_type=jnp.float32,
        )
        highest = jnp.max(block_max, axis=1)
        factor = jnp.exp(block_max - highest[:, None])
        return (
            highest,
            jnp.sum(factor * block_sum, axis=1),
            jnp.sum(factor[:, :, None] * block_output, axis=1),
        )

    prompt_maximum, prompt_sum, prompt_output = lax.map(
        one_head, (query_rows, key_cache_store, value_cache_store, active_mask)
    )
    own_queries = queries[0].reshape(own_count, step_count, kv_count, group_size, head_dim)
    suffix_scores = (
        jnp.einsum(
            "nthgd,nhid->nhtgi", own_queries, sample_keys[0], preferred_element_type=jnp.float32
        )
        * logit_scale
    )
    fresh_scores = (
        jnp.einsum(
            "nthgd,nuhd->nhtgu", own_queries, decode_keys[0], preferred_element_type=jnp.float32
        )
        * logit_scale
    )
    position = jnp.arange(sample_keys.shape[3], dtype=jnp.int32)
    sample_token_mask = (position[None, :] < suffix_len[0][:, None])[:, None, None, None, :]
    step_index = jnp.arange(step_count, dtype=jnp.int32)
    newest_token_mask = (step_index[None, :] <= step_index[:, None])[None, None, :, None, :]
    tail_max = jnp.maximum(
        jnp.max(jnp.where(sample_token_mask, suffix_scores, NEGATIVE), axis=4),
        jnp.max(jnp.where(newest_token_mask, fresh_scores, NEGATIVE), axis=4),
    )
    suffix_weights = jnp.where(sample_token_mask, jnp.exp(suffix_scores - tail_max[..., None]), 0.0)
    fresh_weights = jnp.where(newest_token_mask, jnp.exp(fresh_scores - tail_max[..., None]), 0.0)
    tail_sum = jnp.sum(suffix_weights, axis=4) + jnp.sum(fresh_weights, axis=4)
    tail_out = jnp.einsum(
        "nhtgi,nhid->nhtgd",
        suffix_weights.astype(jnp.bfloat16),
        sample_values[0],
        preferred_element_type=jnp.float32,
    )
    tail_out = tail_out + jnp.einsum(
        "nhtgu,nuhd->nhtgd",
        fresh_weights.astype(jnp.bfloat16),
        decode_values[0],
        preferred_element_type=jnp.float32,
    )
    tail_part = (
        jnp.transpose(tail_max, (1, 0, 2, 3)),
        jnp.transpose(tail_sum, (1, 0, 2, 3)),
        jnp.transpose(tail_out, (1, 0, 2, 3, 4)),
    )
    prefix = (
        prompt_maximum.reshape(kv_count, sample_count, step_count, group_size),
        prompt_sum.reshape(kv_count, sample_count, step_count, group_size),
        prompt_output.reshape(kv_count, sample_count, step_count, group_size, head_dim),
    )
    offset = seq_index * own_count
    own_part = tuple((lax.dynamic_slice_in_dim(member, offset, own_count, 1) for member in prefix))
    merged = combine(own_part, tail_part)
    prefix = tuple(
        (
            lax.dynamic_update_slice_in_dim(member, update, offset, 1)
            for member, update in zip(prefix, merged)
        )
    )
    part_max = jnp.transpose(prefix[0], (1, 2, 0, 3)).reshape(sample_count, step_count, head_count)
    part_total = jnp.transpose(prefix[1], (1, 2, 0, 3)).reshape(
        sample_count, step_count, head_count
    )
    part_out = jnp.transpose(prefix[2], (1, 2, 0, 3, 4)).reshape(
        sample_count, step_count, head_count, head_dim
    )
    local_heads = head_count // seq_count
    highest, softmax_total, summed = joined((part_max, part_total, part_out), "seq", combine)
    highest = lax.dynamic_slice_in_dim(highest, seq_index * local_heads, local_heads, 2)
    softmax_total = lax.dynamic_slice_in_dim(softmax_total, seq_index * local_heads, local_heads, 2)
    summed = lax.dynamic_slice_in_dim(summed, seq_index * local_heads, local_heads, 2)
    head_out = (
        (summed / softmax_total[..., None])
        .astype(jnp.bfloat16)
        .reshape(sample_count * step_count, local_heads * head_dim)
    )
    all_rows = lax.all_gather(head_out, "prompt", axis=0, tiled=True)
    result = lax.psum_scatter(
        jnp.dot(all_rows, out_weight, preferred_element_type=jnp.float32),
        "seq",
        scatter_dimension=0,
        tiled=True,
    )
    return result.astype(jnp.bfloat16)


def solution(mesh):
    placed = (
        P("prompt", "seq", None, None, None),
        P("prompt", None, "seq", None),
        P("prompt", None, "seq", None),
        P("prompt", None, "seq"),
        P("prompt", "seq", None, None, None),
        P("prompt", "seq", None, None, None),
        P("prompt", "seq"),
        P("prompt", "seq", None, None, None),
        P("prompt", "seq", None, None, None),
        P("seq", "prompt"),
    )
    return jax.shard_map(
        on_device, mesh=mesh, in_specs=placed, out_specs=P("seq", "prompt"), check_vma=False
    )
```

profile of v0, /device:TPU:0, one launch (start us, length us, event | category | flops | bytes accessed | tf_op | source)
XLA Modules:
  0.0 127.1 jit_solution(7255105818194194087)
XLA Ops:
  6.5 0.0 copy-start
  6.5 0.0 all-gather.2.cloned.1.call-start
  7.4 0.7 iota_compare_fusion
  8.1 10.8 %all_gather.15 = bf16[1,8,2,32,128]{4,3,2,0,1:T(8,128)(2,1)S(1)} all-gather(bf16[1,1,2,32,128]{4,3,2,0,1:T(8,128)(2,1)} %bitcast.186), channel_id=1, replica_groups=mesh['prompt'=4,'seq'=8] {'seq'}, dimensions={1}, use_global_device_ids=true | all-gather | bytes 147456 | tf_op jit(solution)/shard_map/all_gather | solution.py:55
  19.0 0.0 copy-start.2
  19.0 0.0 copy-start.4
  19.0 0.0 copy-start.1
  19.0 0.0 copy-start.3
  19.0 0.0 copy-start.5
  19.0 10.2 %while.33 = (s32[]{:T(128)}, f32[4,128]{1,0:T(4,128)S(1)}, f32[4,128]{1,0:T(4,128)S(1)}, f32[4,128,128]{2,1,0:T(8,128)S(1)}, pred[4,2]{1,0:T(4,128)(4,1)S(1)}, /...) while((s32[]{:T(128)}, f32[4,128]{1,0:T(4,128)S(1)}, ...), condition=%wide.region_6.7_spmd, body=%wide.region_0.6_spmd.sunk | while | flops 17089024 | bytes 899723 | solution.py:93
  19.1 1.1 fusion.68
  20.1 0.1 fusion.69
  20.2 0.1 fusion.70
  20.4 1.1 fusion.71
  21.4 0.1 copy.106
  21.6 1.0 fusion.68
  22.7 0.1 fusion.69
  22.8 0.1 fusion.70
  22.9 1.1 fusion.71
  24.0 0.1 copy.106
  24.2 1.0 fusion.68
  25.2 0.1 fusion.69
  25.3 0.1 fusion.70
  25.4 1.1 fusion.71
  26.5 0.1 copy.106
  26.7 1.0 fusion.68
  27.7 0.1 fusion.69
  27.8 0.1 fusion.70
  28.0 1.1 fusion.71
  29.0 0.1 copy.106
  29.2 0.1 reshape.196
  29.3 0.0 copy-done.2
  29.3 0.0 copy-done.4
  29.4 0.2 select_reduce_fusion.1
  29.6 0.3 select_reduce_fusion
  29.9 0.1 fusion.45
  30.0 0.2 fusion.30
  30.1 0.2 fusion.26
  30.4 0.1 reshape.200
  30.5 0.2 fusion.25
  30.8 0.8 copy_bitcast_fusion.2
  31.5 0.0 all-gather.2.cloned.1.call-update
  31.6 0.0 reduce-scatter.2.cloned.1.call-start
  31.6 0.1 all_gather_reshape.10
  31.7 0.1 all_gather_reshape.9
  31.8 9.0 %all_gather.16 = f32[8,8,2,32]{3,1,2,0:T(8,128)S(1)} all-gather(f32[1,8,2,32]{3,1,2,0:T(8,128)S(1)} %all_gather_reshape.9), channel_id=1, replica_groups=mesh['prompt'=4,'seq'=8] {'seq'}, dimensions={0}, use_global_device_ids=true | all-gather | bytes 18432 | tf_op jit(solution)/shard_map/all_gather | solution.py:16
  40.9 8.4 %all_gather.17 = f32[8,8,2,32]{3,1,2,0:T(8,128)S(1)} all-gather(f32[1,8,2,32]{3,1,2,0:T(8,128)S(1)} %all_gather_reshape.10), channel_id=1, replica_groups=mesh['prompt'=4,'seq'=8] {'seq'}, dimensions={0}, use_global_device_ids=true | all-gather | bytes 18432 | tf_op jit(solution)/shard_map/all_gather | solution.py:16
  49.3 10.6 %all-gather.2.cloned.1.call-done = f32[8,8,2,32,128]{4,3,2,1,0:T(8,128)} async-done(((f32[1,8,2,32,128]{4,3,2,1,0:T(8,128)}), f32[8,8,2,32,128]{4,3,2,1,0:T(8,128)}) %all-gather.2.cloned.1.call-update) | async-done | bytes 2097168 | tf_op jit(solution)/shard_map/all_gather | solution.py:16
  59.9 1.0 slice_bitcast_fusion
  60.9 9.0 %while.34 = (s32[]{:T(128)}, f32[8,2,32]{2,1,0:T(2,128)S(1)}, f32[8,2,32]{2,1,0:T(2,128)S(1)}, f32[8,2,32,128]{3,2,1,0:T(8,128)S(1)}, f32[8,8,2,32]{3,1,2,0:T(8,...) while((s32[]{:T(128)}, f32[8,2,32]{2,1,0:T(2,128)S(1)}, ...), condition=%wide.region_12.13_spmd, body=%wide.region_11.12_spmd.sunk | while | flops 199685 | bytes 815247 | solution.py:22
  61.0 1.2 fusion.73
  62.3 1.2 fusion.73
  63.6 1.2 fusion.73
  64.8 1.2 fusion.73
  66.1 1.2 fusion.73
  67.4 1.2 fusion.73
  68.7 1.2 fusion.73
  69.9 0.1 constant_dynamic-slice_fusion.3
  70.0 0.1 fusion.34
  70.1 13.2 %all_gather.19 = bf16[64,512]{1,0:T(8,128)(2,1)S(1)} all-gather(bf16[16,512]{1,0:T(8,128)(2,1)S(1)} %bitcast.188), channel_id=1, replica_groups=mesh['prompt'=4,'seq'=8] {'prompt'}, dimensions={0}, use_global_device_ids=true | all-gather | bytes 81920 | tf_op jit(solution)/shard_map/all_gather | solution.py:168
  83.4 1.3 fusion.52
  84.6 0.0 reduce-scatter.2.cloned.1.call-update
  84.7 34.2 %reduce-scatter.2.cloned.1.call-done = f32[8,2048]{1,0:T(8,128)} async-done(((f32[64,2048]{1,0:T(8,128)}), f32[8,2048]{1,0:T(8,128)}) %reduce-scatter.2.cloned.1.call-update) | async-done | bytes 65552 | tf_op jit(solution)/shard_map/reduce_scatter | solution.py:169
  118.9 1.5 %convert_element_type.20 = bf16[8,2048]{1,0:T(8,128)(2,1)} convert(f32[8,2048]{1,0:T(8,128)} %reduce-scatter.2.cloned.1.call-done) | non-fusion elementwise | flops 16384 | bytes 98304 | tf_op jit(solution)/shard_map/convert_element_type | solution.py:175
  (54 shorter events, 0.9 us)
Async XLA Ops:
  6.5 76.8 %copy-start = (bf16[512,2048]{1,0:T(8,128)(2,1)S(1)}, bf16[512,2048]{1,0:T(8,128)(2,1)}, u32[]{:S(2)}) copy-start(bf16[512,2048]{1,0:T(8,128)(2,1)} %param.23) | copy-start | bytes 6291460
  6.5 53.4 %all-gather.2.cloned.1.call-start = ((), (), s32[]{:S(2)}) async-start(), calls=%async_computation.1 | async-start | bytes 2359296 | tf_op jit(solution)/shard_map/all_gather | solution.py:16
  19.0 10.4 %copy-start.2 = (bf16[1,1,2,32,128]{4,3,2,1,0:T(8,128)(2,1)S(1)}, bf16[1,1,2,32,128]{4,3,2,1,0:T(8,128)(2,1)}, u32[]{:S(2)}) copy-start(bf16[1,1,2,32,128]{4,3,2,1,0:T(8,128)(2,1)} %param.14) | copy-start | bytes 49156
  19.0 10.4 %copy-start.4 = (bf16[1,1,2,4,128]{4,3,2,1,0:T(4,128)(2,1)S(1)}, bf16[1,1,2,4,128]{4,3,2,1,0:T(4,128)(2,1)}, u32[]{:S(2)}) copy-start(bf16[1,1,2,4,128]{4,3,2,1,0:T(4,128)(2,1)} %param.21) | copy-start | bytes 6148
  19.0 10.6 %copy-start.1 = (bf16[1,1,4,256,128]{4,3,2,1,0:T(8,128)(2,1)S(1)}, bf16[1,1,4,256,128]{4,3,2,1,0:T(8,128)(2,1)}, u32[]{:S(2)}) copy-start(bf16[1,1,4,256,128]{4,3,2,1,0:T(8,128)(2,1)} %param.18) | copy-start | bytes 786436
  19.0 11.1 %copy-start.3 = (bf16[1,1,4,256,128]{4,3,2,1,0:T(8,128)(2,1)S(1)}, bf16[1,1,4,256,128]{4,3,2,1,0:T(8,128)(2,1)}, u32[]{:S(2)}) copy-start(bf16[1,1,4,256,128]{4,3,2,1,0:T(8,128)(2,1)} %param.19) | copy-start | bytes 786436
  19.0 11.5 %copy-start.5 = (bf16[1,1,2,4,128]{4,3,2,1,0:T(4,128)(2,1)S(1)}, bf16[1,1,2,4,128]{4,3,2,1,0:T(4,128)(2,1)}, u32[]{:S(2)}) copy-start(bf16[1,1,2,4,128]{4,3,2,1,0:T(4,128)(2,1)} %param.22) | copy-start | bytes 6148
  31.6 87.3 %reduce-scatter.2.cloned.1.call-start = ((), (), s32[]{:S(2)}) async-start(), calls=%async_computation.2 | async-start | bytes 589824 | tf_op jit(solution)/shard_map/reduce_scatter | solution.py:169
Sparse Core Ops, SparseCore 0:
  31.7 28.2 all-gather.1
  84.8 34.0 reduce-scatter.1
where the time goes:
time: 128 us; the launch traced here: 127 us
  waiting for transfers between devices  44.9 us (35%)
  blocking collectives  41.5 us (32%)
  between operations  14.4 us (11%)
  other arithmetic  12.2 us (10%)
  matrix products  10.6 us (8%)
  local copies, waits for them, and re-layouts  3.1 us (2%)
    reduce_scatter x1, waiting for transfers between devices, on_device(): lax.psum_scatter(jnp.dot(all_rows, out_weight, preferred_element_type=jnp...  34.2 us
    all_gather x2, blocking collectives, joined(): everything = jax.tree.map(lambda part: lax.all_gather(part, axis), x)  17.4 us
    all_gather x1, blocking collectives, on_device(): all_rows = lax.all_gather(head_out, 'prompt', axis=0, tiled=True)  13.2 us
    all_gather x1, blocking collectives, on_device(): gathered = lax.all_gather(queries, 'seq', axis=1, tiled=True)  10.8 us
    all_gather x1, waiting for transfers between devices, joined(): everything = jax.tree.map(lambda part: lax.all_gather(part, axis), x)  10.6 us
    add x7, other arithmetic, combine(): earlier[2] * early_factor[..., None] + later[2] * late_factor[..., None]  8.48 us
    dot_general x4, matrix products, one_head(): jnp.einsum('yaf,afi->yai', attention_weights.astype(jnp.bfloat16), value_...  4.32 us
    dot_general x4, matrix products, one_head(): jnp.einsum('eg,mxg->emx', head_row_block, key_block_list, preferred_eleme...  4.14 us
  transfers between devices with their start and end apart: 2, of which 2 were waited for; matrix products, arithmetic and copies ran while one was open for 0% of the time, Pallas kernels for 0%

commit v1 on v0

v1 whole, which is shorter than its diff:
```python
import functools
import math

import jax
import jax.numpy as jnp
from jax import lax
from jax.experimental import pallas as pl
from jax.experimental.pallas import tpu as pltpu
from jax.sharding import PartitionSpec as P

BLOCK_TOKENS = 128
NEGATIVE = -1e30
F32 = jnp.float32
BF16 = jnp.bfloat16
VMEM_LIMIT = 16 * 1024 * 1024
MAX_LANE, SUM_LANE, SUM_REST_LANE, KEPT_LANE = 0, 1, 2, 3


def lanes_of(rows, width, values):
    lane = lax.broadcasted_iota(jnp.int32, (rows, width), 1)
    filled = jnp.zeros((rows, width), F32)
    for i, value in enumerate(values):
        filled = jnp.where(lane == i, value, filled)
    return filled


def dot_rows(a, b):
    return lax.dot_general(a, b, (((1,), (1,)), ((), ())), preferred_element_type=F32)


def message_kernel(
    shape, q_refs, key_ref, value_ref, kept_ref, tail_key_ref, tail_value_ref, len_ref,
    step_key_ref, step_value_ref, out_refs, small,
):
    heads, steps, group, dim, ranks, chunk = shape
    rows = steps * group
    scale = 1.0 / math.sqrt(dim)
    chip = lax.div(lax.axis_index("seq"), ranks)
    for x in range(heads):
        out_refs[x][0:chunk, :] = key_ref[chip ^ x]
        out_refs[x][chunk : 2 * chunk, :] = value_ref[chip ^ x]
    queries = [ref[...].astype(F32) for ref in q_refs]
    step_keys = step_key_ref[...].astype(F32)
    step_values = step_value_ref[...].astype(F32)
    length = len_ref[0]
    position = lax.broadcasted_iota(jnp.int32, (rows, tail_key_ref.shape[1]), 1)
    step_of_row = lax.div(lax.broadcasted_iota(jnp.int32, (rows, 1), 0), group)

    def of_head(whole, h):
        return jnp.concatenate(
            [
                whole[t * heads * group + h * group : t * heads * group + (h + 1) * group]
                for t in range(steps)
            ],
            axis=0,
        )

    for h in range(heads):
        q = of_head(queries[0], h)
        scores = dot_rows(q.astype(BF16), tail_key_ref[h]) * scale
        scores = jnp.where(position < length, scores, NEGATIVE)
        own = []
        for u in range(steps):
            score = jnp.sum(q * step_keys[u, h : h + 1], axis=1, keepdims=True) * scale
            own.append(jnp.where(step_of_row >= u, score, NEGATIVE))
        top = jnp.max(scores, axis=1, keepdims=True)
        for score in own:
            top = jnp.maximum(top, score)
        top = top.astype(BF16).astype(F32)
        weights = jnp.exp(scores - top)
        total = jnp.sum(weights, axis=1, keepdims=True)
        summed = jnp.dot(weights.astype(BF16), tail_value_ref[h], preferred_element_type=F32)
        for u, score in enumerate(own):
            weight = jnp.exp(score - top)
            total = total + weight
            summed = summed + weight.astype(BF16).astype(F32) * step_values[u, h : h + 1]
        summed_high = summed.astype(BF16)
        summed_rest = (summed - summed_high.astype(F32)).astype(BF16)
        total_high = total.astype(BF16).astype(F32)
        kept = kept_ref[h].astype(F32)
        stats = lanes_of(rows, dim, [top, total_high, total - total_high, kept])
        parts = [q.astype(BF16)] + [of_head(other, h).astype(BF16) for other in queries[1:]]
        parts += [summed_high, summed_rest, stats.astype(BF16)]
        for i, part in enumerate(parts):
            small[h, i * rows : (i + 1) * rows, :] = part
    for x in range(heads):
        out_refs[x][2 * chunk :, :] = small[chip ^ x]


def prefix_kernel(shape, message_refs, out_refs, q_all, tails, merged):
    heads, steps, group, dim, ranks, chunk = shape
    rows = steps * group
    local = group // ranks
    scale = 1.0 / math.sqrt(dim)
    me = lax.axis_index("seq")
    chip, rank = lax.div(me, ranks), lax.rem(me, ranks)
    all_rows = q_all.shape[0]
    tails[:, 0:dim] = jnp.zeros((all_rows, dim), F32)
    tails[:, dim:] = lanes_of(all_rows, dim, [NEGATIVE])
    kept = []
    for x in range(heads):
        base = (chip ^ x) * ranks
        start = 2 * chunk
        for y in range(ranks):
            place = pl.multiple_of((base + (rank ^ y)) * rows, rows)
            q_all[pl.ds(place, rows), :] = message_refs[x][start + y * rows : start + (y + 1) * rows, :]
        start += ranks * rows
        place = pl.multiple_of((base + rank) * rows, rows)
        high = message_refs[x][start : start + rows, :].astype(F32)
        rest = message_refs[x][start + rows : start + 2 * rows, :].astype(F32)
        stats = message_refs[x][start + 2 * rows : start + 3 * rows, :].astype(F32)
        tails[pl.ds(place, rows), 0:dim] = high + rest
        total = stats[:, SUM_LANE : SUM_LANE + 1] + stats[:, SUM_REST_LANE : SUM_REST_LANE + 1]
        tails[pl.ds(place, rows), dim:] = lanes_of(
            rows, dim, [stats[:, MAX_LANE : MAX_LANE + 1], total]
        )
        kept.append(stats[0:1, KEPT_LANE : KEPT_LANE + 1])
    block = lax.div(lax.broadcasted_iota(jnp.int32, (1, chunk), 1), BLOCK_TOKENS).astype(F32)
    q = q_all[...]
    tail_top = tails[:, dim + MAX_LANE : dim + MAX_LANE + 1]
    top = tail_top
    scores = []
    for x in range(heads):
        score = dot_rows(q, message_refs[x][0:chunk, :]) * scale
        score = jnp.where(block < kept[x], score, NEGATIVE)
        top = jnp.maximum(top, jnp.max(score, axis=1, keepdims=True))
        scores.append(score)
    factor = jnp.exp(tail_top - top)
    total = tails[:, dim + SUM_LANE : dim + SUM_LANE + 1] * factor
    summed = tails[:, 0:dim] * factor
    for x in range(heads):
        weights = jnp.exp(scores[x] - top)
        total = total + jnp.sum(weights, axis=1, keepdims=True)
        summed = summed + jnp.dot(
            weights.astype(BF16),
            message_refs[x][chunk : 2 * chunk, :],
            preferred_element_type=F32,
        )
    merged[0] = summed
    merged[1] = lanes_of(all_rows, dim, [top, total])
    count = all_rows // group
    for y in range(ranks):
        for i in range(local):
            head = (rank ^ y) * local + i
            for j in range(2):
                out_refs[y][i * count : (i + 1) * count, j * dim : (j + 1) * dim] = merged[
                    j, pl.ds(head, count, stride=group), :
                ]


def merge_kernel(local, part_refs, out_ref):
    dim = out_ref.shape[1] // local
    count = out_ref.shape[0]
    tops = [ref[:, dim + MAX_LANE : dim + MAX_LANE + 1] for ref in part_refs]
    top = functools.reduce(jnp.maximum, tops)
    total, summed = 0.0, 0.0
    for ref, part_top in zip(part_refs, tops):
        factor = jnp.exp(part_top - top)
        total = total + ref[:, dim + SUM_LANE : dim + SUM_LANE + 1] * factor
        summed = summed + ref[:, 0:dim] * factor
    head_out = summed / total
    for i in range(local):
        out_ref[:, i * dim : (i + 1) * dim] = head_out[i * count : (i + 1) * count].astype(BF16)


def project_kernel(heads, ranks, head_refs, weight_ref, out_refs, all_heads, product):
    me = lax.axis_index("seq")
    chip, rank = lax.div(me, ranks), lax.rem(me, ranks)
    prompt = lax.axis_index("prompt")
    count = head_refs[0].shape[0]
    for x, ref in enumerate(head_refs):
        all_heads[pl.ds(pl.multiple_of((prompt ^ x) * count, count), count), :] = ref[...]
    product[...] = jnp.dot(all_heads[...], weight_ref[...], preferred_element_type=F32)
    size = product.shape[0] // (heads * ranks)
    for y in range(ranks):
        pieces = [
            product[pl.ds(pl.multiple_of(((chip ^ x) * ranks + (rank ^ y)) * size, size), size), :]
            for x in range(heads)
        ]
        out_refs[y][...] = jnp.concatenate(pieces, axis=0).astype(out_refs[y].dtype)


def call(kernel, out_shape, in_specs, scratch_shapes=()):
    return pl.pallas_call(
        kernel,
        out_shape=out_shape,
        in_specs=in_specs,
        out_specs=jax.tree.map(lambda _: pl.BlockSpec(memory_space=pltpu.VMEM), out_shape),
        scratch_shapes=scratch_shapes,
        compiler_params=pltpu.CompilerParams(vmem_limit_bytes=VMEM_LIMIT),
    )


def swap(x, axis, distance):
    return lax.ppermute(x, axis, [(i, i ^ distance) for i in range(lax.axis_size(axis))])


def on_device(
    queries,
    prompt_key_cache,
    prompt_value_cache,
    kept,
    sample_keys,
    sample_values,
    suffix_len,
    decode_keys,
    decode_values,
    out_weight,
):
    seq_count, prompt_count = lax.axis_size("seq"), lax.axis_size("prompt")
    steps, head_count, dim = queries.shape[2:]
    heads, chunk = prompt_key_cache.shape[1:3]
    group = head_count // heads
    ranks = seq_count // heads
    local = group // ranks
    shape = (heads, steps, group, dim, ranks, chunk)
    rows = steps * group
    vmem, smem = pl.BlockSpec(memory_space=pltpu.VMEM), pl.BlockSpec(memory_space=pltpu.SMEM)

    own_queries = queries.reshape(steps * head_count, dim)
    rank_queries = [own_queries] + [swap(own_queries, "seq", y) for y in range(1, ranks)]

    small_rows = (ranks + 3) * rows
    message = jax.ShapeDtypeStruct((2 * chunk + small_rows, dim), BF16)

    def run_message(*refs):
        q_refs, refs = refs[:ranks], refs[ranks:]
        message_kernel(shape, q_refs, *refs[:8], refs[8 : 8 + heads], refs[8 + heads])

    messages = call(
        run_message,
        [message] * heads,
        [vmem] * ranks + [vmem, vmem, smem, vmem, vmem, smem, vmem, vmem],
        [pltpu.VMEM((heads, small_rows, dim), BF16)],
    )(
        *rank_queries,
        prompt_key_cache[0],
        prompt_value_cache[0],
        kept.reshape(heads),
        sample_keys[0, 0],
        sample_values[0, 0],
        suffix_len.reshape(1),
        decode_keys[0, 0],
        decode_values[0, 0],
    )
    messages = [messages[0]] + [swap(messages[x], "seq", x * ranks) for x in range(1, heads)]

    all_rows = seq_count * rows
    count = seq_count * steps
    part = jax.ShapeDtypeStruct((local * count, 2 * dim), F32)

    def run_prefix(*refs):
        prefix_kernel(shape, refs[:heads], refs[heads : heads + ranks], *refs[heads + ranks :])

    parts = call(
        run_prefix,
        [part] * ranks,
        [vmem] * heads,
        [
            pltpu.VMEM((all_rows, dim), BF16),
            pltpu.VMEM((all_rows, 2 * dim), F32),
            pltpu.VMEM((2, all_rows, dim), F32),
        ],
    )(*messages)
    parts = [parts[0]] + [swap(parts[y], "seq", y) for y in range(1, ranks)]

    def run_merge(*refs):
        merge_kernel(local, refs[:ranks], refs[ranks])

    head_out = call(
        run_merge, jax.ShapeDtypeStruct((count, local * dim), BF16), [vmem] * ranks
    )(*parts)
    head_outs = [head_out] + [swap(head_out, "prompt", x) for x in range(1, prompt_count)]

    columns = out_weight.shape[1]
    row_count = count * prompt_count
    size = row_count // seq_count

    def run_project(*refs):
        project_kernel(
            heads, ranks, refs[:prompt_count], refs[prompt_count],
            refs[prompt_count + 1 : prompt_count + 1 + ranks], *refs[prompt_count + 1 + ranks :]
        )

    terms = call(
        run_project,
        [jax.ShapeDtypeStruct((heads * size, columns), BF16 if y else F32) for y in range(ranks)],
        [vmem] * (prompt_count + 1),
        [
            pltpu.VMEM((row_count, local * dim), BF16),
            pltpu.VMEM((row_count, columns), F32),
        ],
    )(*head_outs, out_weight)
    total = terms[0]
    for y in range(1, ranks):
        total = total + swap(terms[y], "seq", y).astype(F32)
    total = total.reshape(heads, size, columns)
    result = total[0]
    for x in range(1, heads):
        result = result + swap(total[x].astype(BF16), "seq", x * ranks).astype(F32)
    return result.astype(BF16)


def solution(mesh):
    placed = (
        P("prompt", "seq", None, None, None),
        P("prompt", None, "seq", None),
        P("prompt", None, "seq", None),
        P("prompt", None, "seq"),
        P("prompt", "seq", None, None, None),
        P("prompt", "seq", None, None, None),
        P("prompt", "seq"),
        P("prompt", "seq", None, None, None),
        P("prompt", "seq", None, None, None),
        P("seq", "prompt"),
    )
    return jax.shard_map(
        on_device, mesh=mesh, in_specs=placed, out_specs=P("seq", "prompt"), check_vma=False
    )
```

time: 128 us -> 43.6 us (0.34)
  blocking collectives: 41.5 us -> 0 us
  waiting for transfers between devices: 44.9 us -> 17.7 us
  between operations: 14.4 us -> 0.73 us
  starting transfers between devices: 0.04 us -> 13 us
  other arithmetic: 12.2 us -> 0.67 us
  matrix products: 10.6 us -> 0 us
  local copies, waits for them, and re-layouts: 3.1 us -> 8.13 us
  Pallas kernels: 0 us -> 2.93 us
    all_gather x4 -> x0, blocking collectives: 41.5 us -> none  [the longest x2 17.4 us: joined(): everything = jax.tree.map(lambda part: lax.all_gather(part, axis), x)]
    reduce_scatter x1 -> x0, waiting for transfers between devices: 34.2 us -> none  [on_device(): lax.psum_scatter(jnp.dot(all_rows, out_weight, preferred_element_type=jnp...]
    ppermute x0 -> x12, waiting for transfers between devices: none -> 17.7 us  [swap(): lax.ppermute(x, axis, [(i, i ^ distance) for i in range(lax.axis_size(axi...]
    ppermute x0 -> x12, starting transfers between devices: none -> 13 us  [swap(): lax.ppermute(x, axis, [(i, i ^ distance) for i in range(lax.axis_size(axi...]
    dot_general x13 -> x0, matrix products: 10.6 us -> none  [the longest x4 4.32 us: one_head(): jnp.einsum('yaf,afi->yai', attention_weights.astype(jnp.bfloat16), value_...]
    all_gather x1 -> x0, waiting for transfers between devices: 10.6 us -> none  [joined(): everything = jax.tree.map(lambda part: lax.all_gather(part, axis), x)]
    add x14 -> x0, other arithmetic: 8.72 us -> none  [the longest x7 8.48 us: combine(): earlier[2] * early_factor[..., None] + later[2] * late_factor[..., None]]
    unnamed x13 -> x18, local copies, waits for them, and re-layouts: 0.04 us -> 8.12 us
  transfers between devices with their start and end apart: 2 -> 12, of which waited for: 2 -> 10; matrix products, arithmetic and copies ran while one was open for 0% -> 0% of each run, Pallas kernels for 0% -> 0%
where the time goes in v1:
time: 43.6 us; the launch traced here: 43.2 us
  waiting for transfers between devices  17.7 us (41%)
  starting transfers between devices  13 us (30%)
  local copies, waits for them, and re-layouts  8.13 us (19%)
  Pallas kernels  2.93 us (7%)
  between operations  0.73 us (2%)
  other arithmetic  0.67 us (2%)
    ppermute x12, waiting for transfers between devices, swap(): lax.ppermute(x, axis, [(i, i ^ distance) for i in range(lax.axis_size(axi...  17.7 us
    ppermute x12, starting transfers between devices, swap(): lax.ppermute(x, axis, [(i, i ^ distance) for i in range(lax.axis_size(axi...  13 us
    unnamed x18, local copies, waits for them, and re-layouts  8.12 us
    pallas_call x1, Pallas kernels, on_device(): call(run_message, [message] * heads, [vmem] * ranks + [vmem, vmem, smem,...  1.63 us
  transfers between devices with their start and end apart: 12, of which 10 were waited for; matrix products, arithmetic and copies ran while one was open for 0% of the time, Pallas kernels for 0%

profile of v1, /device:TPU:0, one launch (start us, length us, event | category | flops | bytes accessed | tf_op | source)
XLA Modules:
  0.0 43.2 jit_solution(3700481846680598251)
XLA Ops:
  0.0 0.5 %collective-permute-start = (bf16[64,128]{1,0:T(8,128)(2,1)}, bf16[64,128]{1,0:T(8,128)(2,1)S(1)}, u32[]{:S(2)}, u32[]{:S(2)}) collective-permute-start(bf16[64,128]{1,0:T(8,128)(2,1)} %bitcast.14), channel_id=1, source_target_pairs={{0,1},{1,0},{2,3},{3,2},{4,5},{5,4},{6,7},{7,6},{8,9},{9,8},{10,11... | collective-permute-start | bytes 49160 | tf_op jit(solution)/shard_map/ppermute | solution.py:195
  1.1 0.4 collective-permute-done.refs_1_
  1.5 0.0 copy-start.1
  1.5 0.9 %copy-done.1 = bf16[1,4,256,128]{3,2,1,0:T(8,128)(2,1)S(1)} copy-done((bf16[1,4,256,128]{3,2,1,0:T(8,128)(2,1)S(1)}, bf16[1,4,256,128]{3,2,1,0:T(8,128)(2,1)}, u32[]{:S(2)}) %copy-start.1) | copy-done | bytes 262168
  2.5 0.0 copy-start.2
  2.5 0.9 %copy-done.2 = bf16[1,4,256,128]{3,2,1,0:T(8,128)(2,1)S(1)} copy-done((bf16[1,4,256,128]{3,2,1,0:T(8,128)(2,1)S(1)}, bf16[1,4,256,128]{3,2,1,0:T(8,128)(2,1)}, u32[]{:S(2)}) %copy-start.2) | copy-done | bytes 262168
  3.4 0.0 copy-start.3
  3.4 0.9 %copy-done.3 = bf16[1,1,4,256,128]{4,3,2,1,0:T(8,128)(2,1)S(1)} copy-done((bf16[1,1,4,256,128]{4,3,2,1,0:T(8,128)(2,1)S(1)}, bf16[1,1,4,256,128]{4,3,2,1,0:T(8,128)(2,1)}, u32[]{:S(2)}) %copy-start.3) | copy-done | bytes 262168
  4.4 0.0 copy-start.4
  4.4 0.9 %copy-done.4 = bf16[1,1,4,256,128]{4,3,2,1,0:T(8,128)(2,1)S(1)} copy-done((bf16[1,1,4,256,128]{4,3,2,1,0:T(8,128)(2,1)S(1)}, bf16[1,1,4,256,128]{4,3,2,1,0:T(8,128)(2,1)}, u32[]{:S(2)}) %copy-start.4) | copy-done | bytes 262168
  5.3 0.0 copy-start.5
  5.3 0.7 %copy-done.5 = bf16[1,1,2,32,128]{4,3,2,1,0:T(8,128)(2,1)S(1)} copy-done((bf16[1,1,2,32,128]{4,3,2,1,0:T(8,128)(2,1)S(1)}, bf16[1,1,2,32,128]{4,3,2,1,0:T(8,128)(2,1)}, u32[]{:S(2)}) %copy-start.5) | copy-done | bytes 16408
  6.0 0.0 copy-start.6
  6.0 0.7 %copy-done.6 = bf16[1,1,2,4,128]{4,3,2,1,0:T(4,128)(2,1)S(1)} copy-done((bf16[1,1,2,4,128]{4,3,2,1,0:T(4,128)(2,1)S(1)}, bf16[1,1,2,4,128]{4,3,2,1,0:T(4,128)(2,1)}, u32[]{:S(2)}) %copy-start.6) | copy-done | bytes 2072
  6.7 0.0 copy-start.7
  6.7 0.7 %copy-done.7 = bf16[1,1,2,4,128]{4,3,2,1,0:T(4,128)(2,1)S(1)} copy-done((bf16[1,1,2,4,128]{4,3,2,1,0:T(4,128)(2,1)S(1)}, bf16[1,1,2,4,128]{4,3,2,1,0:T(4,128)(2,1)}, u32[]{:S(2)}) %copy-start.7) | copy-done | bytes 2072
  7.4 0.0 copy-start.8
  7.4 0.7 %copy-done.8 = s32[1,4,1]{1,2,0:T(1,128)S(1)} copy-done((s32[1,4,1]{1,2,0:T(1,128)S(1)}, s32[1,4,1]{1,2,0:T(1,128)}, u32[]{:S(2)}) %copy-start.8) | copy-done | bytes 40
  8.0 1.6 %shard_map.100 = (bf16[592,128]{1,0:T(8,128)(2,1)S(1)}, bf16[592,128]{1,0:T(8,128)(2,1)S(1)}, bf16[592,128]{1,0:T(8,128)(2,1)S(1)}, bf16[592,128]{1,0:T(8,128)(2,1)S(1)}) custom-call(bf16[64,128]{1,0:T(8,128)(2,1)S(1)} %bitcast.15, bf16[64,128]{1,0:T(8,128)(2,1)S(1)} %collective-permute-done.refs_1_, bf16[4,256,128]{2,1,0:T(8,128)(2,1)S(1)} %bitcast.10, ...), custom_call_target="tpu_custom_call" | custom-call | tf_op jit(solution)/shard_map/pallas_call | solution.py:230
  9.7 2.9 %collective-permute-start.1 = (bf16[592,128]{1,0:T(8,128)(2,1)S(1)}, bf16[592,128]{1,0:T(8,128)(2,1)S(1)}, u32[]{:S(2)}, u32[]{:S(2)}) collective-permute-start(bf16[592,128]{1,0:T(8,128)(2,1)S(1)} %get-tuple-element.14), channel_id=1, source_target_pairs={{0,2},{1,3},{2,0},{3,1},{4,6},{5,7},{6,4},{7,5},{8,10},{9,11},{10,... | collective-permute-start | bytes 454664 | tf_op jit(solution)/shard_map/ppermute | solution.py:195
  12.6 1.5 %collective-permute-start.2 = (bf16[592,128]{1,0:T(8,128)(2,1)S(1)}, bf16[592,128]{1,0:T(8,128)(2,1)S(1)}, u32[]{:S(2)}, u32[]{:S(2)}) collective-permute-start(bf16[592,128]{1,0:T(8,128)(2,1)S(1)} %get-tuple-element.15), channel_id=1, source_target_pairs={{0,4},{1,5},{2,6},{3,7},{4,0},{5,1},{6,2},{7,3},{8,12},{9,13},{10,... | collective-permute-start | bytes 454664 | tf_op jit(solution)/shard_map/ppermute | solution.py:195
  14.1 0.0 collective-permute-start.3
  14.1 3.2 %collective-permute-done.1.refs_1_ = bf16[592,128]{1,0:T(8,128)(2,1)S(1)} collective-permute-done((bf16[592,128]{1,0:T(8,128)(2,1)S(1)}, bf16[592,128]{1,0:T(8,128)(2,1)S(1)}, u32[]{:S(2)}, u32[]{:S(2)}) %collective-permute-start.1) | collective-permute-done | bytes 151584 | tf_op jit(solution)/shard_map/ppermute | solution.py:195
  17.3 4.3 %collective-permute-done.2.refs_2_ = bf16[592,128]{1,0:T(8,128)(2,1)S(1)} collective-permute-done((bf16[592,128]{1,0:T(8,128)(2,1)S(1)}, bf16[592,128]{1,0:T(8,128)(2,1)S(1)}, u32[]{:S(2)}, u32[]{:S(2)}) %collective-permute-start.2) | collective-permute-done | bytes 151584 | tf_op jit(solution)/shard_map/ppermute | solution.py:195
  21.6 0.0 collective-permute-done.3.refs_3_
  21.6 0.6 %shard_map.101 = (f32[64,256]{1,0:T(8,128)S(1)}, f32[64,256]{1,0:T(8,128)S(1)}) custom-call(bf16[592,128]{1,0:T(8,128)(2,1)S(1)} %get-tuple-element.13.refs_0_, bf16[592,128]{1,0:T(8,128)(2,1)S(1)} %collective-permute-done.1.refs_1_, bf16[592,128]{1,0:T(8,128)(2,1)S(1)} %collective-permute-done.2.refs_2_, bf16[592,128]{1,0:T(8,128)(2,1)S(1)} %collective-permute-done.3.refs_3_), custom_call_target="tpu_custom_call" | custom-call | tf_op jit(solution)/shard_map/pallas_call | solution.py:255
  22.2 0.1 collective-permute-start.4
  22.3 1.2 %collective-permute-done.4.refs_1_ = f32[64,256]{1,0:T(8,128)S(1)} collective-permute-done((f32[64,256]{1,0:T(8,128)S(1)}, f32[64,256]{1,0:T(8,128)S(1)}, u32[]{:S(2)}, u32[]{:S(2)}) %collective-permute-start.4) | collective-permute-done | bytes 65568 | tf_op jit(solution)/shard_map/ppermute | solution.py:195
  23.5 0.2 shard_map.102.refs_0_
  23.7 3.7 %collective-permute-start.7 = (bf16[16,512]{1,0:T(8,128)(2,1)S(1)}, bf16[16,512]{1,0:T(8,128)(2,1)S(1)}, u32[]{:S(2)}, u32[]{:S(2)}) collective-permute-start(bf16[16,512]{1,0:T(8,128)(2,1)S(1)} %shard_map.102.refs_0_), channel_id=1, source_target_pairs={{0,24},{8,16},{16,8},{24,0},{1,25},{9,17},{17,9},{25,1},{2,26},{10... | collective-permute-start | bytes 49160 | tf_op jit(solution)/shard_map/ppermute | solution.py:195
  27.4 0.0 collective-permute-start.6
  27.4 0.8 %collective-permute-start.5 = (bf16[16,512]{1,0:T(8,128)(2,1)S(1)}, bf16[16,512]{1,0:T(8,128)(2,1)S(1)}, u32[]{:S(2)}, u32[]{:S(2)}) collective-permute-start(bf16[16,512]{1,0:T(8,128)(2,1)S(1)} %shard_map.102.refs_0_), channel_id=1, source_target_pairs={{0,8},{8,0},{16,24},{24,16},{1,9},{9,1},{17,25},{25,17},{2,10},{10... | collective-permute-start | bytes 49160 | tf_op jit(solution)/shard_map/ppermute | solution.py:195
  28.1 1.1 %collective-permute-done.7.refs_3_ = bf16[16,512]{1,0:T(8,128)(2,1)S(1)} collective-permute-done((bf16[16,512]{1,0:T(8,128)(2,1)S(1)}, bf16[16,512]{1,0:T(8,128)(2,1)S(1)}, u32[]{:S(2)}, u32[]{:S(2)}) %collective-permute-start.7) | collective-permute-done | bytes 16416 | tf_op jit(solution)/shard_map/ppermute | solution.py:195
  29.3 2.7 %collective-permute-done.6.refs_2_ = bf16[16,512]{1,0:T(8,128)(2,1)S(1)} collective-permute-done((bf16[16,512]{1,0:T(8,128)(2,1)S(1)}, bf16[16,512]{1,0:T(8,128)(2,1)S(1)}, u32[]{:S(2)}, u32[]{:S(2)}) %collective-permute-start.6) | collective-permute-done | bytes 16416 | tf_op jit(solution)/shard_map/ppermute | solution.py:195
  32.0 0.0 collective-permute-done.5.refs_1_
  32.0 0.0 copy-start
  32.0 1.6 %copy-done = bf16[512,2048]{1,0:T(8,128)(2,1)S(1)} copy-done((bf16[512,2048]{1,0:T(8,128)(2,1)S(1)}, bf16[512,2048]{1,0:T(8,128)(2,1)}, u32[]{:S(2)}) %copy-start) | copy-done | bytes 2097176
  33.6 0.5 %shard_map.103 = (f32[32,2048]{1,0:T(8,128)S(1)}, bf16[32,2048]{1,0:T(8,128)(2,1)S(1)}) custom-call(bf16[16,512]{1,0:T(8,128)(2,1)S(1)} %shard_map.102.refs_0_, bf16[16,512]{1,0:T(8,128)(2,1)S(1)} %collective-permute-done.5.refs_1_, bf16[16,512]{1,0:T(8,128)(2,1)S(1)} %collective-permute-done.6.refs_2_, bf16[16,512]{1,0:T(8,128)(2,1)S(1)} %collective-permute-done.7.refs_3_, ...), custom_call_target="tpu_custom_call" | custom-call | tf_op jit(solution)/shard_map/pallas_call | solution.py:285
  34.1 0.1 collective-permute-start.8
  34.2 1.3 %collective-permute-done.8 = bf16[32,2048]{1,0:T(8,128)(2,1)S(1)} collective-permute-done((bf16[32,2048]{1,0:T(8,128)(2,1)S(1)}, bf16[32,2048]{1,0:T(8,128)(2,1)S(1)}, u32[]{:S(2)}, u32[]{:S(2)}) %collective-permute-start.8) | collective-permute-done | bytes 131104 | tf_op jit(solution)/shard_map/ppermute | solution.py:195
  35.6 1.3 %collective-permute-start.9 = (bf16[8,2048]{1,0:T(8,128)(2,1)S(1)}, bf16[8,2048]{1,0:T(8,128)(2,1)S(1)}, u32[]{:S(2)}, u32[]{:S(2)}) collective-permute-start(bf16[8,2048]{1,0:T(8,128)(2,1)S(1)} %get-tuple-element.23), channel_id=1, source_target_pairs={{0,2},{1,3},{2,0},{3,1},{4,6},{5,7},{6,4},{7,5},{8,10},{9,11},{10,... | collective-permute-start | bytes 98312 | tf_op jit(solution)/shard_map/ppermute | solution.py:195
  36.9 1.8 %collective-permute-start.11 = (bf16[8,2048]{1,0:T(8,128)(2,1)S(1)}, bf16[8,2048]{1,0:T(8,128)(2,1)S(1)}, u32[]{:S(2)}, u32[]{:S(2)}) collective-permute-start(bf16[8,2048]{1,0:T(8,128)(2,1)S(1)} %get-tuple-element.24), channel_id=1, source_target_pairs={{0,6},{1,7},{2,4},{3,5},{4,2},{5,3},{6,0},{7,1},{8,14},{9,15},{10,... | collective-permute-start | bytes 98312 | tf_op jit(solution)/shard_map/ppermute | solution.py:195
  38.6 0.5 %collective-permute-start.10 = (bf16[8,2048]{1,0:T(8,128)(2,1)S(1)}, bf16[8,2048]{1,0:T(8,128)(2,1)S(1)}, u32[]{:S(2)}, u32[]{:S(2)}) collective-permute-start(bf16[8,2048]{1,0:T(8,128)(2,1)S(1)} %get-tuple-element.25), channel_id=1, source_target_pairs={{0,4},{1,5},{2,6},{3,7},{4,0},{5,1},{6,2},{7,3},{8,12},{9,13},{10,... | collective-permute-start | bytes 98312 | tf_op jit(solution)/shard_map/ppermute | solution.py:195
  39.1 0.4 collective-permute-done.9
  39.6 2.1 %collective-permute-done.11 = bf16[8,2048]{1,0:T(8,128)(2,1)S(1)} collective-permute-done((bf16[8,2048]{1,0:T(8,128)(2,1)S(1)}, bf16[8,2048]{1,0:T(8,128)(2,1)S(1)}, u32[]{:S(2)}, u32[]{:S(2)}) %collective-permute-start.11) | collective-permute-done | bytes 32800 | tf_op jit(solution)/shard_map/ppermute | solution.py:195
  41.7 0.9 %collective-permute-done.10 = bf16[8,2048]{1,0:T(8,128)(2,1)S(1)} collective-permute-done((bf16[8,2048]{1,0:T(8,128)(2,1)S(1)}, bf16[8,2048]{1,0:T(8,128)(2,1)S(1)}, u32[]{:S(2)}, u32[]{:S(2)}) %collective-permute-start.10) | collective-permute-done | bytes 32800 | tf_op jit(solution)/shard_map/ppermute | solution.py:195
  42.5 0.6 %fusion.2 = bf16[8,2048]{1,0:T(8,128)(2,1)} fusion(f32[32,2048]{1,0:T(8,128)S(1)} %get-tuple-element.22, bf16[8,2048]{1,0:T(8,128)(2,1)S(1)} %collective-permute-done.11, bf16[8,2048]{1,0:T(8,128)(2,1)S(1)} %collective-permute-done.10, bf16[8,2048]{1,0:T(8,128)(2,1)S(1)} %collective-permute-done.9), kind=kLoop, calls=%fused_computation.4 | loop fusion | flops 114688 | bytes 196608 | tf_op jit(solution)/shard_map/convert_element_type | solution.py:301
  (2 shorter events, 0.0 us)
Async XLA Ops:
  0.0 1.5 %collective-permute-start = (bf16[64,128]{1,0:T(8,128)(2,1)}, bf16[64,128]{1,0:T(8,128)(2,1)S(1)}, u32[]{:S(2)}, u32[]{:S(2)}) collective-permute-start(bf16[64,128]{1,0:T(8,128)(2,1)} %bitcast.14), channel_id=1, source_target_pairs={{0,1},{1,0},{2,3},{3,2},{4,5},{5,4},{6,7},{7,6},{8,9},{9,8},{10,11... | collective-permute-start | bytes 49160 | tf_op jit(solution)/shard_map/ppermute | solution.py:195
  1.5 0.9 %copy-start.1 = (bf16[1,4,256,128]{3,2,1,0:T(8,128)(2,1)S(1)}, bf16[1,4,256,128]{3,2,1,0:T(8,128)(2,1)}, u32[]{:S(2)}) copy-start(bf16[1,4,256,128]{3,2,1,0:T(8,128)(2,1)} %param.11) | copy-start | bytes 786436
  2.5 0.9 %copy-start.2 = (bf16[1,4,256,128]{3,2,1,0:T(8,128)(2,1)S(1)}, bf16[1,4,256,128]{3,2,1,0:T(8,128)(2,1)}, u32[]{:S(2)}) copy-start(bf16[1,4,256,128]{3,2,1,0:T(8,128)(2,1)} %param.12) | copy-start | bytes 786436
  3.4 0.9 %copy-start.3 = (bf16[1,1,4,256,128]{4,3,2,1,0:T(8,128)(2,1)S(1)}, bf16[1,1,4,256,128]{4,3,2,1,0:T(8,128)(2,1)}, u32[]{:S(2)}) copy-start(bf16[1,1,4,256,128]{4,3,2,1,0:T(8,128)(2,1)} %param.14) | copy-start | bytes 786436
  4.4 0.9 %copy-start.4 = (bf16[1,1,4,256,128]{4,3,2,1,0:T(8,128)(2,1)S(1)}, bf16[1,1,4,256,128]{4,3,2,1,0:T(8,128)(2,1)}, u32[]{:S(2)}) copy-start(bf16[1,1,4,256,128]{4,3,2,1,0:T(8,128)(2,1)} %param.15) | copy-start | bytes 786436
  5.3 0.7 %copy-start.5 = (bf16[1,1,2,32,128]{4,3,2,1,0:T(8,128)(2,1)S(1)}, bf16[1,1,2,32,128]{4,3,2,1,0:T(8,128)(2,1)}, u32[]{:S(2)}) copy-start(bf16[1,1,2,32,128]{4,3,2,1,0:T(8,128)(2,1)} %param.10) | copy-start | bytes 49156
  6.0 0.7 %copy-start.6 = (bf16[1,1,2,4,128]{4,3,2,1,0:T(4,128)(2,1)S(1)}, bf16[1,1,2,4,128]{4,3,2,1,0:T(4,128)(2,1)}, u32[]{:S(2)}) copy-start(bf16[1,1,2,4,128]{4,3,2,1,0:T(4,128)(2,1)} %param.17) | copy-start | bytes 6148
  6.7 0.7 %copy-start.7 = (bf16[1,1,2,4,128]{4,3,2,1,0:T(4,128)(2,1)S(1)}, bf16[1,1,2,4,128]{4,3,2,1,0:T(4,128)(2,1)}, u32[]{:S(2)}) copy-start(bf16[1,1,2,4,128]{4,3,2,1,0:T(4,128)(2,1)} %param.18) | copy-start | bytes 6148
  7.4 0.7 %copy-start.8 = (s32[1,4,1]{1,2,0:T(1,128)S(1)}, s32[1,4,1]{1,2,0:T(1,128)}, u32[]{:S(2)}) copy-start(s32[1,4,1]{1,2,0:T(1,128)} %param.13) | copy-start | bytes 52
  9.7 7.6 %collective-permute-start.1 = (bf16[592,128]{1,0:T(8,128)(2,1)S(1)}, bf16[592,128]{1,0:T(8,128)(2,1)S(1)}, u32[]{:S(2)}, u32[]{:S(2)}) collective-permute-start(bf16[592,128]{1,0:T(8,128)(2,1)S(1)} %get-tuple-element.14), channel_id=1, source_target_pairs={{0,2},{1,3},{2,0},{3,1},{4,6},{5,7},{6,4},{7,5},{8,10},{9,11},{10,... | collective-permute-start | bytes 454664 | tf_op jit(solution)/shard_map/ppermute | solution.py:195
  12.6 9.0 %collective-permute-start.2 = (bf16[592,128]{1,0:T(8,128)(2,1)S(1)}, bf16[592,128]{1,0:T(8,128)(2,1)S(1)}, u32[]{:S(2)}, u32[]{:S(2)}) collective-permute-start(bf16[592,128]{1,0:T(8,128)(2,1)S(1)} %get-tuple-element.15), channel_id=1, source_target_pairs={{0,4},{1,5},{2,6},{3,7},{4,0},{5,1},{6,2},{7,3},{8,12},{9,13},{10,... | collective-permute-start | bytes 454664 | tf_op jit(solution)/shard_map/ppermute | solution.py:195
  14.1 7.5 %collective-permute-start.3 = (bf16[592,128]{1,0:T(8,128)(2,1)S(1)}, bf16[592,128]{1,0:T(8,128)(2,1)S(1)}, u32[]{:S(2)}, u32[]{:S(2)}) collective-permute-start(bf16[592,128]{1,0:T(8,128)(2,1)S(1)} %get-tuple-element.16), channel_id=1, source_target_pairs={{0,6},{1,7},{2,4},{3,5},{4,2},{5,3},{6,0},{7,1},{8,14},{9,15},{10,... | collective-permute-start | bytes 454664 | tf_op jit(solution)/shard_map/ppermute | solution.py:195
  22.2 1.3 %collective-permute-start.4 = (f32[64,256]{1,0:T(8,128)S(1)}, f32[64,256]{1,0:T(8,128)S(1)}, u32[]{:S(2)}, u32[]{:S(2)}) collective-permute-start(f32[64,256]{1,0:T(8,128)S(1)} %get-tuple-element.18), channel_id=1, source_target_pairs={{0,1},{1,0},{2,3},{3,2},{4,5},{5,4},{6,7},{7,6},{8,9},{9,8},{10,11... | collective-permute-start | bytes 196616 | tf_op jit(solution)/shard_map/ppermute | solution.py:195
  23.7 5.6 %collective-permute-start.7 = (bf16[16,512]{1,0:T(8,128)(2,1)S(1)}, bf16[16,512]{1,0:T(8,128)(2,1)S(1)}, u32[]{:S(2)}, u32[]{:S(2)}) collective-permute-start(bf16[16,512]{1,0:T(8,128)(2,1)S(1)} %shard_map.102.refs_0_), channel_id=1, source_target_pairs={{0,24},{8,16},{16,8},{24,0},{1,25},{9,17},{17,9},{25,1},{2,26},{10... | collective-permute-start | bytes 49160 | tf_op jit(solution)/shard_map/ppermute | solution.py:195
  27.4 4.6 %collective-permute-start.6 = (bf16[16,512]{1,0:T(8,128)(2,1)S(1)}, bf16[16,512]{1,0:T(8,128)(2,1)S(1)}, u32[]{:S(2)}, u32[]{:S(2)}) collective-permute-start(bf16[16,512]{1,0:T(8,128)(2,1)S(1)} %shard_map.102.refs_0_), channel_id=1, source_target_pairs={{0,16},{8,24},{16,0},{24,8},{1,17},{9,25},{17,1},{25,9},{2,18},{10... | collective-permute-start | bytes 49160 | tf_op jit(solution)/shard_map/ppermute | solution.py:195
  27.4 4.6 %collective-permute-start.5 = (bf16[16,512]{1,0:T(8,128)(2,1)S(1)}, bf16[16,512]{1,0:T(8,128)(2,1)S(1)}, u32[]{:S(2)}, u32[]{:S(2)}) collective-permute-start(bf16[16,512]{1,0:T(8,128)(2,1)S(1)} %shard_map.102.refs_0_), channel_id=1, source_target_pairs={{0,8},{8,0},{16,24},{24,16},{1,9},{9,1},{17,25},{25,17},{2,10},{10... | collective-permute-start | bytes 49160 | tf_op jit(solution)/shard_map/ppermute | solution.py:195
  32.0 1.6 %copy-start = (bf16[512,2048]{1,0:T(8,128)(2,1)S(1)}, bf16[512,2048]{1,0:T(8,128)(2,1)}, u32[]{:S(2)}) copy-start(bf16[512,2048]{1,0:T(8,128)(2,1)} %refs_4_.1) | copy-start | bytes 6291460
  34.1 1.4 %collective-permute-start.8 = (bf16[32,2048]{1,0:T(8,128)(2,1)S(1)}, bf16[32,2048]{1,0:T(8,128)(2,1)S(1)}, u32[]{:S(2)}, u32[]{:S(2)}) collective-permute-start(bf16[32,2048]{1,0:T(8,128)(2,1)S(1)} %get-tuple-element.20), channel_id=1, source_target_pairs={{0,1},{1,0},{2,3},{3,2},{4,5},{5,4},{6,7},{7,6},{8,9},{9,8},{10,11... | collective-permute-start | bytes 393224 | tf_op jit(solution)/shard_map/ppermute | solution.py:195
  35.6 4.0 %collective-permute-start.9 = (bf16[8,2048]{1,0:T(8,128)(2,1)S(1)}, bf16[8,2048]{1,0:T(8,128)(2,1)S(1)}, u32[]{:S(2)}, u32[]{:S(2)}) collective-permute-start(bf16[8,2048]{1,0:T(8,128)(2,1)S(1)} %get-tuple-element.23), channel_id=1, source_target_pairs={{0,2},{1,3},{2,0},{3,1},{4,6},{5,7},{6,4},{7,5},{8,10},{9,11},{10,... | collective-permute-start | bytes 98312 | tf_op jit(solution)/shard_map/ppermute | solution.py:195
  36.9 4.8 %collective-permute-start.11 = (bf16[8,2048]{1,0:T(8,128)(2,1)S(1)}, bf16[8,2048]{1,0:T(8,128)(2,1)S(1)}, u32[]{:S(2)}, u32[]{:S(2)}) collective-permute-start(bf16[8,2048]{1,0:T(8,128)(2,1)S(1)} %get-tuple-element.24), channel_id=1, source_target_pairs={{0,6},{1,7},{2,4},{3,5},{4,2},{5,3},{6,0},{7,1},{8,14},{9,15},{10,... | collective-permute-start | bytes 98312 | tf_op jit(solution)/shard_map/ppermute | solution.py:195
  38.6 3.9 %collective-permute-start.10 = (bf16[8,2048]{1,0:T(8,128)(2,1)S(1)}, bf16[8,2048]{1,0:T(8,128)(2,1)S(1)}, u32[]{:S(2)}, u32[]{:S(2)}) collective-permute-start(bf16[8,2048]{1,0:T(8,128)(2,1)S(1)} %get-tuple-element.25), channel_id=1, source_target_pairs={{0,4},{1,5},{2,6},{3,7},{4,0},{5,1},{6,2},{7,3},{8,12},{9,13},{10,... | collective-permute-start | bytes 98312 | tf_op jit(solution)/shard_map/ppermute | solution.py:195

commit v2 on v1

--- a/solution.py
+++ b/solution.py
@@ -28,35 +28,41 @@
     return lax.dot_general(a, b, (((1,), (1,)), ((), ())), preferred_element_type=F32)
 
 
-def message_kernel(
-    shape, q_refs, key_ref, value_ref, kept_ref, tail_key_ref, tail_value_ref, len_ref,
-    step_key_ref, step_value_ref, out_refs, small,
-):
+def copy_all(pairs, sems):
+    copies = [
+        pltpu.make_async_copy(source, target, sems.at[i]) for i, (source, target) in enumerate(pairs)
+    ]
+    for copy in copies:
+        copy.start()
+    return copies
+
+
+def message_kernel(shape, in_refs, out_refs, held, small, sems):
     heads, steps, group, dim, ranks, chunk = shape
     rows = steps * group
     scale = 1.0 / math.sqrt(dim)
     chip = lax.div(lax.axis_index("seq"), ranks)
-    for x in range(heads):
-        out_refs[x][0:chunk, :] = key_ref[chip ^ x]
-        out_refs[x][chunk : 2 * chunk, :] = value_ref[chip ^ x]
-    queries = [ref[...].astype(F32) for ref in q_refs]
+    key_ref, value_ref, *fetched = in_refs
+    pairs = list(zip(fetched, held))
+    for x in range(heads):
+        pairs.append((key_ref.at[chip ^ x], out_refs[x].at[0:chunk]))
+        pairs.append((value_ref.at[chip ^ x], out_refs[x].at[chunk : 2 * chunk]))
+    copies = [
+        pltpu.make_async_copy(source, target, sems.at[i]) for i, (source, target) in enumerate(pairs)
+    ]
+    for copy in copies:
+        copy.start()
+    for copy in copies[: len(held)]:
+        copy.wait()
+    q_ref, tail_key_ref, tail_value_ref, step_key_ref, step_value_ref, kept_ref, len_ref = held
+    queries = q_ref[...].astype(F32)
     step_keys = step_key_ref[...].astype(F32)
     step_values = step_value_ref[...].astype(F32)
     length = len_ref[0]
     position = lax.broadcasted_iota(jnp.int32, (rows, tail_key_ref.shape[1]), 1)
     step_of_row = lax.div(lax.broadcasted_iota(jnp.int32, (rows, 1), 0), group)
-
-    def of_head(whole, h):
-        return jnp.concatenate(
-            [
-                whole[t * heads * group + h * group : t * heads * group + (h + 1) * group]
-                for t in range(steps)
-            ],
-            axis=0,
-        )
-
     for h in range(heads):
-        q = of_head(queries[0], h)
+        q = rows_of_head(queries, shape, h)
         scores = dot_rows(q.astype(BF16), tail_key_ref[h]) * scale
         scores = jnp.where(position < length, scores, NEGATIVE)
         own = []
@@ -79,12 +85,43 @@
         total_high = total.astype(BF16).astype(F32)
         kept = kept_ref[h].astype(F32)
         stats = lanes_of(rows, dim, [top, total_high, total - total_high, kept])
-        parts = [q.astype(BF16)] + [of_head(other, h).astype(BF16) for other in queries[1:]]
-        parts += [summed_high, summed_rest, stats.astype(BF16)]
+        parts = [summed_high, summed_rest, stats.astype(BF16), q.astype(BF16)]
         for i, part in enumerate(parts):
             small[h, i * rows : (i + 1) * rows, :] = part
     for x in range(heads):
-        out_refs[x][2 * chunk :, :] = small[chip ^ x]
+        out_refs[x][2 * chunk : 2 * chunk + 4 * rows, :] = small[chip ^ x]
+    for copy in copies[len(held) :]:
+        copy.wait()
+
+
+def rows_of_head(whole, shape, h):
+    heads, steps, group, *_ = shape
+    return jnp.concatenate(
+        [
+            whole[(t * heads + h) * group : (t * heads + h + 1) * group]
+            for t in range(steps)
+        ],
+        axis=0,
+    )
+
+
+def query_kernel(shape, q_refs, out_refs, small):
+    heads, steps, group, dim, ranks, chunk = shape
+    rows = steps * group
+    chip = lax.div(lax.axis_index("seq"), ranks)
+    for y, ref in enumerate(q_refs):
+        queries = ref[...].astype(F32)
+        for h in range(heads):
+            small[h, y * rows : (y + 1) * rows, :] = rows_of_head(queries, shape, h).astype(BF16)
+    start = 2 * chunk + 4 * rows
+    for x in range(heads):
+        out_refs[x][start : start + len(q_refs) * rows, :] = small[chip ^ x]
+
+
+def fetch_kernel(after_ref, weight_ref, out_ref, sem):
+    copy = pltpu.make_async_copy(weight_ref, out_ref, sem)
+    copy.start()
+    copy.wait()
 
 
 def prefix_kernel(shape, message_refs, out_refs, q_all, tails, merged):
@@ -101,14 +138,14 @@
     for x in range(heads):
         base = (chip ^ x) * ranks
         start = 2 * chunk
-        for y in range(ranks):
-            place = pl.multiple_of((base + (rank ^ y)) * rows, rows)
-            q_all[pl.ds(place, rows), :] = message_refs[x][start + y * rows : start + (y + 1) * rows, :]
-        start += ranks * rows
         place = pl.multiple_of((base + rank) * rows, rows)
         high = message_refs[x][start : start + rows, :].astype(F32)
         rest = message_refs[x][start + rows : start + 2 * rows, :].astype(F32)
         stats = message_refs[x][start + 2 * rows : start + 3 * rows, :].astype(F32)
+        start += 3 * rows
+        for y in range(ranks):
+            row = pl.multiple_of((base + (rank ^ y)) * rows, rows)
+            q_all[pl.ds(row, rows), :] = message_refs[x][start + y * rows : start + (y + 1) * rows, :]
         tails[pl.ds(place, rows), 0:dim] = high + rest
         total = stats[:, SUM_LANE : SUM_LANE + 1] + stats[:, SUM_REST_LANE : SUM_REST_LANE + 1]
         tails[pl.ds(place, rows), dim:] = lanes_of(
@@ -180,15 +217,20 @@
         out_refs[y][...] = jnp.concatenate(pieces, axis=0).astype(out_refs[y].dtype)
 
 
-def call(kernel, out_shape, in_specs, scratch_shapes=()):
+def call(kernel, out_shape, in_specs, scratch_shapes=(), aliases=None):
     return pl.pallas_call(
         kernel,
         out_shape=out_shape,
         in_specs=in_specs,
         out_specs=jax.tree.map(lambda _: pl.BlockSpec(memory_space=pltpu.VMEM), out_shape),
         scratch_shapes=scratch_shapes,
+        input_output_aliases=aliases or {},
         compiler_params=pltpu.CompilerParams(vmem_limit_bytes=VMEM_LIMIT),
     )
+
+
+def in_hbm(x):
+    return pltpu.with_memory_space_constraint(x, pltpu.HBM)
 
 
 def swap(x, axis, distance):
@@ -215,34 +257,59 @@
     local = group // ranks
     shape = (heads, steps, group, dim, ranks, chunk)
     rows = steps * group
-    vmem, smem = pl.BlockSpec(memory_space=pltpu.VMEM), pl.BlockSpec(memory_space=pltpu.SMEM)
-
+    vmem = pl.BlockSpec(memory_space=pltpu.VMEM)
+    hbm = pl.BlockSpec(memory_space=pltpu.HBM)
     own_queries = queries.reshape(steps * head_count, dim)
-    rank_queries = [own_queries] + [swap(own_queries, "seq", y) for y in range(1, ranks)]
-
-    small_rows = (ranks + 3) * rows
-    message = jax.ShapeDtypeStruct((2 * chunk + small_rows, dim), BF16)
+    other_queries = [swap(own_queries, "seq", y) for y in range(1, ranks)]
+
+    fetched = [
+        own_queries,
+        sample_keys[0, 0],
+        sample_values[0, 0],
+        decode_keys[0, 0],
+        decode_values[0, 0],
+        kept.reshape(heads),
+        suffix_len.reshape(1),
+    ]
+    sources = [prompt_key_cache[0], prompt_value_cache[0], *fetched]
+    message = jax.ShapeDtypeStruct((2 * chunk + (ranks + 3) * rows, dim), BF16)
 
     def run_message(*refs):
-        q_refs, refs = refs[:ranks], refs[ranks:]
-        message_kernel(shape, q_refs, *refs[:8], refs[8 : 8 + heads], refs[8 + heads])
+        n, m = len(sources), len(sources) + heads
+        message_kernel(shape, refs[:n], refs[n:m], refs[m : m + len(fetched)], *refs[m + len(fetched) :])
 
     messages = call(
         run_message,
         [message] * heads,
-        [vmem] * ranks + [vmem, vmem, smem, vmem, vmem, smem, vmem, vmem],
-        [pltpu.VMEM((heads, small_rows, dim), BF16)],
-    )(
-        *rank_queries,
-        prompt_key_cache[0],
-        prompt_value_cache[0],
-        kept.reshape(heads),
-        sample_keys[0, 0],
-        sample_values[0, 0],
-        suffix_len.reshape(1),
-        decode_keys[0, 0],
-        decode_values[0, 0],
-    )
+        [hbm] * len(sources),
+        [
+            (pltpu.SMEM if x.dtype == jnp.int32 else pltpu.VMEM)(x.shape, x.dtype)
+            for x in fetched
+        ]
+        + [
+            pltpu.VMEM((heads, 4 * rows, dim), BF16),
+            pltpu.SemaphoreType.DMA((len(fetched) + 2 * heads,)),
+        ],
+    )(*[x if x.dtype == jnp.int32 else in_hbm(x) for x in sources])
+
+    def run_query(*refs):
+        n = ranks - 1
+        query_kernel(shape, refs[:n], refs[n + heads : n + 2 * heads], refs[-1])
+
+    if ranks > 1:
+        messages = call(
+            run_query,
+            [message] * heads,
+            [vmem] * (ranks - 1 + heads),
+            [pltpu.VMEM((heads, (ranks - 1) * rows, dim), BF16)],
+            {ranks - 1 + x: x for x in range(heads)},
+        )(*other_queries, *messages)
+    weight = call(
+        fetch_kernel,
+        jax.ShapeDtypeStruct(out_weight.shape, BF16),
+        [pl.BlockSpec(memory_space=pl.ANY), hbm],
+        [pltpu.SemaphoreType.DMA(())],
+    )(messages[0], in_hbm(out_weight))
     messages = [messages[0]] + [swap(messages[x], "seq", x * ranks) for x in range(1, heads)]
 
     all_rows = seq_count * rows
@@ -290,7 +357,7 @@
             pltpu.VMEM((row_count, local * dim), BF16),
             pltpu.VMEM((row_count, columns), F32),
         ],
-    )(*head_outs, out_weight)
+    )(*head_outs, weight)
     total = terms[0]
     for y in range(1, ranks):
         total = total + swap(terms[y], "seq", y).astype(F32)

time: 43.6 us -> 36.3 us (0.83)
  local copies, waits for them, and re-layouts: 8.13 us -> 0.66 us
  Pallas kernels: 2.93 us -> 5.23 us
  waiting for transfers between devices: 17.7 us -> 16 us
    unnamed x18 -> x2, local copies, waits for them, and re-layouts: 8.12 us -> 0.65 us
    pallas_call x1 -> x3, Pallas kernels: 1.63 us -> 3.92 us  [the longest x1 2.3 us: on_device(): call(run_message, [message] * heads, [hbm] * len(sources), [(pltpu.SMEM i...]
    ppermute x12, waiting for transfers between devices: 17.7 us -> 16 us  [swap(): lax.ppermute(x, axis, [(i, i ^ distance) for i in range(lax.axis_size(axi...]
  transfers between devices with their start and end apart: 12 -> 12, of which waited for: 10 -> 8; matrix products, arithmetic and copies ran while one was open for 0% -> 0% of each run, Pallas kernels for 0% -> 11%
where the time goes in v2:
time: 36.3 us; the launch traced here: 36 us
  waiting for transfers between devices  16 us (44%)
  starting transfers between devices  12.7 us (35%)
  Pallas kernels  5.23 us (14%)
  between operations  0.76 us (2%)
  other arithmetic  0.67 us (2%)
  local copies, waits for them, and re-layouts  0.66 us (2%)
    ppermute x12, waiting for transfers between devices, swap(): lax.ppermute(x, axis, [(i, i ^ distance) for i in range(lax.axis_size(axi...  16 us
    ppermute x12, starting transfers between devices, swap(): lax.ppermute(x, axis, [(i, i ^ distance) for i in range(lax.axis_size(axi...  12.7 us
    pallas_call x1, Pallas kernels, on_device(): call(run_message, [message] * heads, [hbm] * len(sources), [(pltpu.SMEM i...  2.3 us
    pallas_call x1, Pallas kernels, on_device(): call(fetch_kernel, jax.ShapeDtypeStruct(out_weight.shape, BF16), [pl.Bloc...  1.6 us
  transfers between devices with their start and end apart: 12, of which 8 were waited for; matrix products, arithmetic and copies ran while one was open for 0% of the time, Pallas kernels for 11%

profile of v2, /device:TPU:0, one launch (start us, length us, event | category | flops | bytes accessed | tf_op | source)
XLA Modules:
  0.0 36.0 jit_solution(8821781445547478295)
XLA Ops:
  0.0 0.5 %collective-permute-start = (bf16[64,128]{1,0:T(8,128)(2,1)}, bf16[64,128]{1,0:T(8,128)(2,1)S(1)}, u32[]{:S(2)}, u32[]{:S(2)}) collective-permute-start(bf16[64,128]{1,0:T(8,128)(2,1)} %bitcast.15), channel_id=1, source_target_pairs={{0,1},{1,0},{2,3},{3,2},{4,5},{5,4},{6,7},{7,6},{8,9},{9,8},{10,11... | collective-permute-start | bytes 49160 | tf_op jit(solution)/shard_map/ppermute | solution.py:237
  1.1 0.0 copy-start
  1.1 0.6 %copy-done = s32[1,4,1]{1,2,0:T(1,128)S(1)} copy-done((s32[1,4,1]{1,2,0:T(1,128)S(1)}, s32[1,4,1]{1,2,0:T(1,128)}, u32[]{:S(2)}) %copy-start) | copy-done | bytes 40
  1.8 2.3 %shard_map.100 = (bf16[592,128]{1,0:T(8,128)(2,1)S(1)}, bf16[592,128]{1,0:T(8,128)(2,1)S(1)}, bf16[592,128]{1,0:T(8,128)(2,1)S(1)}, bf16[592,128]{1,0:T(8,128)(2,1)S(1)}) custom-call(bf16[4,256,128]{2,1,0:T(8,128)(2,1)} %bitcast.11, bf16[4,256,128]{2,1,0:T(8,128)(2,1)} %bitcast.12, bf16[64,128]{1,0:T(8,128)(2,1)} %bitcast.16, bf16[4,256,128]{2,1,0:T(8,128)(2,1)} %bitcast.13, ...), custom_call_target="tpu_custom_call" | custom-call | tf_op jit(solution)/shard_map/pallas_call | solution.py:281
  4.1 0.0 collective-permute-done.refs_0_
  4.1 2.6 %collective-permute-start.1 = (bf16[592,128]{1,0:T(8,128)(2,1)S(1)}, bf16[592,128]{1,0:T(8,128)(2,1)S(1)}, u32[]{:S(2)}, u32[]{:S(2)}) collective-permute-start(bf16[592,128]{1,0:T(8,128)(2,1)S(1)} %get-tuple-element.22), channel_id=1, source_target_pairs={{0,2},{1,3},{2,0},{3,1},{4,6},{5,7},{6,4},{7,5},{8,10},{9,11},{10,... | collective-permute-start | bytes 454664 | tf_op jit(solution)/shard_map/ppermute | solution.py:237
  6.7 1.5 %collective-permute-start.2 = (bf16[592,128]{1,0:T(8,128)(2,1)S(1)}, bf16[592,128]{1,0:T(8,128)(2,1)S(1)}, u32[]{:S(2)}, u32[]{:S(2)}) collective-permute-start(bf16[592,128]{1,0:T(8,128)(2,1)S(1)} %get-tuple-element.23), channel_id=1, source_target_pairs={{0,4},{1,5},{2,6},{3,7},{4,0},{5,1},{6,2},{7,3},{8,12},{9,13},{10,... | collective-permute-start | bytes 454664 | tf_op jit(solution)/shard_map/ppermute | solution.py:237
  8.2 0.0 collective-permute-start.3
  8.2 3.2 %collective-permute-done.1.refs_1_ = bf16[592,128]{1,0:T(8,128)(2,1)S(1)} collective-permute-done((bf16[592,128]{1,0:T(8,128)(2,1)S(1)}, bf16[592,128]{1,0:T(8,128)(2,1)S(1)}, u32[]{:S(2)}, u32[]{:S(2)}) %collective-permute-start.1) | collective-permute-done | bytes 151584 | tf_op jit(solution)/shard_map/ppermute | solution.py:237
  11.5 4.5 %collective-permute-done.2.refs_2_ = bf16[592,128]{1,0:T(8,128)(2,1)S(1)} collective-permute-done((bf16[592,128]{1,0:T(8,128)(2,1)S(1)}, bf16[592,128]{1,0:T(8,128)(2,1)S(1)}, u32[]{:S(2)}, u32[]{:S(2)}) %collective-permute-start.2) | collective-permute-done | bytes 151584 | tf_op jit(solution)/shard_map/ppermute | solution.py:237
  16.0 0.0 collective-permute-done.3.refs_3_
  16.0 0.6 %shard_map.102 = (f32[64,256]{1,0:T(8,128)S(1)}, f32[64,256]{1,0:T(8,128)S(1)}) custom-call(bf16[592,128]{1,0:T(8,128)(2,1)S(1)} %get-tuple-element.21.refs_0_.after_ref, bf16[592,128]{1,0:T(8,128)(2,1)S(1)} %collective-permute-done.1.refs_1_, bf16[592,128]{1,0:T(8,128)(2,1)S(1)} %collective-permute-done.2.refs_2_, ...), custom_call_target="tpu_custom_call" | custom-call | tf_op jit(solution)/shard_map/pallas_call | solution.py:322
  16.6 0.1 collective-permute-start.4
  16.7 1.2 %collective-permute-done.4.refs_1_ = f32[64,256]{1,0:T(8,128)S(1)} collective-permute-done((f32[64,256]{1,0:T(8,128)S(1)}, f32[64,256]{1,0:T(8,128)S(1)}, u32[]{:S(2)}, u32[]{:S(2)}) %collective-permute-start.4) | collective-permute-done | bytes 65568 | tf_op jit(solution)/shard_map/ppermute | solution.py:237
  17.9 0.2 shard_map.103.refs_0_
  18.1 3.7 %collective-permute-start.7 = (bf16[16,512]{1,0:T(8,128)(2,1)S(1)}, bf16[16,512]{1,0:T(8,128)(2,1)S(1)}, u32[]{:S(2)}, u32[]{:S(2)}) collective-permute-start(bf16[16,512]{1,0:T(8,128)(2,1)S(1)} %shard_map.103.refs_0_), channel_id=1, source_target_pairs={{0,24},{8,16},{16,8},{24,0},{1,25},{9,17},{17,9},{25,1},{2,26},{10... | collective-permute-start | bytes 49160 | tf_op jit(solution)/shard_map/ppermute | solution.py:237
  21.8 0.0 collective-permute-start.6
  21.8 0.8 %collective-permute-start.5 = (bf16[16,512]{1,0:T(8,128)(2,1)S(1)}, bf16[16,512]{1,0:T(8,128)(2,1)S(1)}, u32[]{:S(2)}, u32[]{:S(2)}) collective-permute-start(bf16[16,512]{1,0:T(8,128)(2,1)S(1)} %shard_map.103.refs_0_), channel_id=1, source_target_pairs={{0,8},{8,0},{16,24},{24,16},{1,9},{9,1},{17,25},{25,17},{2,10},{10... | collective-permute-start | bytes 49160 | tf_op jit(solution)/shard_map/ppermute | solution.py:237
  22.6 1.6 %shard_map.104.refs_4_ = bf16[512,2048]{1,0:T(8,128)(2,1)S(1)} custom-call(bf16[592,128]{1,0:T(8,128)(2,1)S(1)} %get-tuple-element.21.refs_0_.after_ref, bf16[512,2048]{1,0:T(8,128)(2,1)} %weight_ref.1), custom_call_target="tpu_custom_call" | custom-call | tf_op jit(solution)/shard_map/pallas_call | solution.py:307
  24.2 0.0 collective-permute-done.7.refs_3_
  24.2 2.2 %collective-permute-done.6.refs_2_ = bf16[16,512]{1,0:T(8,128)(2,1)S(1)} collective-permute-done((bf16[16,512]{1,0:T(8,128)(2,1)S(1)}, bf16[16,512]{1,0:T(8,128)(2,1)S(1)}, u32[]{:S(2)}, u32[]{:S(2)}) %collective-permute-start.6) | collective-permute-done | bytes 16416 | tf_op jit(solution)/shard_map/ppermute | solution.py:237
  26.4 0.0 collective-permute-done.5.refs_1_
  26.4 0.5 %shard_map.105 = (f32[32,2048]{1,0:T(8,128)S(1)}, bf16[32,2048]{1,0:T(8,128)(2,1)S(1)}) custom-call(bf16[16,512]{1,0:T(8,128)(2,1)S(1)} %shard_map.103.refs_0_, bf16[16,512]{1,0:T(8,128)(2,1)S(1)} %collective-permute-done.5.refs_1_, bf16[16,512]{1,0:T(8,128)(2,1)S(1)} %collective-permute-done.6.refs_2_, bf16[16,512]{1,0:T(8,128)(2,1)S(1)} %collective-permute-done.7.refs_3_, ...), custom_call_target="tpu_custom_call" | custom-call | tf_op jit(solution)/shard_map/pallas_call | solution.py:352
  26.9 0.1 collective-permute-start.8
  27.0 1.3 %collective-permute-done.8 = bf16[32,2048]{1,0:T(8,128)(2,1)S(1)} collective-permute-done((bf16[32,2048]{1,0:T(8,128)(2,1)S(1)}, bf16[32,2048]{1,0:T(8,128)(2,1)S(1)}, u32[]{:S(2)}, u32[]{:S(2)}) %collective-permute-start.8) | collective-permute-done | bytes 131104 | tf_op jit(solution)/shard_map/ppermute | solution.py:237
  28.4 1.3 %collective-permute-start.9 = (bf16[8,2048]{1,0:T(8,128)(2,1)S(1)}, bf16[8,2048]{1,0:T(8,128)(2,1)S(1)}, u32[]{:S(2)}, u32[]{:S(2)}) collective-permute-start(bf16[8,2048]{1,0:T(8,128)(2,1)S(1)} %get-tuple-element.31), channel_id=1, source_target_pairs={{0,2},{1,3},{2,0},{3,1},{4,6},{5,7},{6,4},{7,5},{8,10},{9,11},{10,... | collective-permute-start | bytes 98312 | tf_op jit(solution)/shard_map/ppermute | solution.py:237
  29.7 1.7 %collective-permute-start.11 = (bf16[8,2048]{1,0:T(8,128)(2,1)S(1)}, bf16[8,2048]{1,0:T(8,128)(2,1)S(1)}, u32[]{:S(2)}, u32[]{:S(2)}) collective-permute-start(bf16[8,2048]{1,0:T(8,128)(2,1)S(1)} %get-tuple-element.32), channel_id=1, source_target_pairs={{0,6},{1,7},{2,4},{3,5},{4,2},{5,3},{6,0},{7,1},{8,14},{9,15},{10,... | collective-permute-start | bytes 98312 | tf_op jit(solution)/shard_map/ppermute | solution.py:237
  31.5 0.5 %collective-permute-start.10 = (bf16[8,2048]{1,0:T(8,128)(2,1)S(1)}, bf16[8,2048]{1,0:T(8,128)(2,1)S(1)}, u32[]{:S(2)}, u32[]{:S(2)}) collective-permute-start(bf16[8,2048]{1,0:T(8,128)(2,1)S(1)} %get-tuple-element.33), channel_id=1, source_target_pairs={{0,4},{1,5},{2,6},{3,7},{4,0},{5,1},{6,2},{7,3},{8,12},{9,13},{10,... | collective-permute-start | bytes 98312 | tf_op jit(solution)/shard_map/ppermute | solution.py:237
  32.0 0.4 %collective-permute-done.9 = bf16[8,2048]{1,0:T(8,128)(2,1)S(1)} collective-permute-done((bf16[8,2048]{1,0:T(8,128)(2,1)S(1)}, bf16[8,2048]{1,0:T(8,128)(2,1)S(1)}, u32[]{:S(2)}, u32[]{:S(2)}) %collective-permute-start.9) | collective-permute-done | bytes 32800 | tf_op jit(solution)/shard_map/ppermute | solution.py:237
  32.4 2.1 %collective-permute-done.11 = bf16[8,2048]{1,0:T(8,128)(2,1)S(1)} collective-permute-done((bf16[8,2048]{1,0:T(8,128)(2,1)S(1)}, bf16[8,2048]{1,0:T(8,128)(2,1)S(1)}, u32[]{:S(2)}, u32[]{:S(2)}) %collective-permute-start.11) | collective-permute-done | bytes 32800 | tf_op jit(solution)/shard_map/ppermute | solution.py:237
  34.5 0.8 %collective-permute-done.10 = bf16[8,2048]{1,0:T(8,128)(2,1)S(1)} collective-permute-done((bf16[8,2048]{1,0:T(8,128)(2,1)S(1)}, bf16[8,2048]{1,0:T(8,128)(2,1)S(1)}, u32[]{:S(2)}, u32[]{:S(2)}) %collective-permute-start.10) | collective-permute-done | bytes 32800 | tf_op jit(solution)/shard_map/ppermute | solution.py:237
  35.4 0.6 %fusion.2 = bf16[8,2048]{1,0:T(8,128)(2,1)} fusion(f32[32,2048]{1,0:T(8,128)S(1)} %get-tuple-element.30, bf16[8,2048]{1,0:T(8,128)(2,1)S(1)} %collective-permute-done.11, bf16[8,2048]{1,0:T(8,128)(2,1)S(1)} %collective-permute-done.10, bf16[8,2048]{1,0:T(8,128)(2,1)S(1)} %collective-permute-done.9), kind=kLoop, calls=%fused_computation.4 | loop fusion | flops 114688 | bytes 196608 | tf_op jit(solution)/shard_map/convert_element_type | solution.py:368
  (3 shorter events, 0.1 us)
Async XLA Ops:
  0.0 4.1 %collective-permute-start = (bf16[64,128]{1,0:T(8,128)(2,1)}, bf16[64,128]{1,0:T(8,128)(2,1)S(1)}, u32[]{:S(2)}, u32[]{:S(2)}) collective-permute-start(bf16[64,128]{1,0:T(8,128)(2,1)} %bitcast.15), channel_id=1, source_target_pairs={{0,1},{1,0},{2,3},{3,2},{4,5},{5,4},{6,7},{7,6},{8,9},{9,8},{10,11... | collective-permute-start | bytes 49160 | tf_op jit(solution)/shard_map/ppermute | solution.py:237
  1.1 0.7 %copy-start = (s32[1,4,1]{1,2,0:T(1,128)S(1)}, s32[1,4,1]{1,2,0:T(1,128)}, u32[]{:S(2)}) copy-start(s32[1,4,1]{1,2,0:T(1,128)} %param.13) | copy-start | bytes 52
  4.1 7.3 %collective-permute-start.1 = (bf16[592,128]{1,0:T(8,128)(2,1)S(1)}, bf16[592,128]{1,0:T(8,128)(2,1)S(1)}, u32[]{:S(2)}, u32[]{:S(2)}) collective-permute-start(bf16[592,128]{1,0:T(8,128)(2,1)S(1)} %get-tuple-element.22), channel_id=1, source_target_pairs={{0,2},{1,3},{2,0},{3,1},{4,6},{5,7},{6,4},{7,5},{8,10},{9,11},{10,... | collective-permute-start | bytes 454664 | tf_op jit(solution)/shard_map/ppermute | solution.py:237
  6.7 9.3 %collective-permute-start.2 = (bf16[592,128]{1,0:T(8,128)(2,1)S(1)}, bf16[592,128]{1,0:T(8,128)(2,1)S(1)}, u32[]{:S(2)}, u32[]{:S(2)}) collective-permute-start(bf16[592,128]{1,0:T(8,128)(2,1)S(1)} %get-tuple-element.23), channel_id=1, source_target_pairs={{0,4},{1,5},{2,6},{3,7},{4,0},{5,1},{6,2},{7,3},{8,12},{9,13},{10,... | collective-permute-start | bytes 454664 | tf_op jit(solution)/shard_map/ppermute | solution.py:237
  8.2 7.8 %collective-permute-start.3 = (bf16[592,128]{1,0:T(8,128)(2,1)S(1)}, bf16[592,128]{1,0:T(8,128)(2,1)S(1)}, u32[]{:S(2)}, u32[]{:S(2)}) collective-permute-start(bf16[592,128]{1,0:T(8,128)(2,1)S(1)} %get-tuple-element.24), channel_id=1, source_target_pairs={{0,6},{1,7},{2,4},{3,5},{4,2},{5,3},{6,0},{7,1},{8,14},{9,15},{10,... | collective-permute-start | bytes 454664 | tf_op jit(solution)/shard_map/ppermute | solution.py:237
  16.6 1.3 %collective-permute-start.4 = (f32[64,256]{1,0:T(8,128)S(1)}, f32[64,256]{1,0:T(8,128)S(1)}, u32[]{:S(2)}, u32[]{:S(2)}) collective-permute-start(f32[64,256]{1,0:T(8,128)S(1)} %get-tuple-element.26), channel_id=1, source_target_pairs={{0,1},{1,0},{2,3},{3,2},{4,5},{5,4},{6,7},{7,6},{8,9},{9,8},{10,11... | collective-permute-start | bytes 196616 | tf_op jit(solution)/shard_map/ppermute | solution.py:237
  18.1 6.1 %collective-permute-start.7 = (bf16[16,512]{1,0:T(8,128)(2,1)S(1)}, bf16[16,512]{1,0:T(8,128)(2,1)S(1)}, u32[]{:S(2)}, u32[]{:S(2)}) collective-permute-start(bf16[16,512]{1,0:T(8,128)(2,1)S(1)} %shard_map.103.refs_0_), channel_id=1, source_target_pairs={{0,24},{8,16},{16,8},{24,0},{1,25},{9,17},{17,9},{25,1},{2,26},{10... | collective-permute-start | bytes 49160 | tf_op jit(solution)/shard_map/ppermute | solution.py:237
  21.8 4.6 %collective-permute-start.6 = (bf16[16,512]{1,0:T(8,128)(2,1)S(1)}, bf16[16,512]{1,0:T(8,128)(2,1)S(1)}, u32[]{:S(2)}, u32[]{:S(2)}) collective-permute-start(bf16[16,512]{1,0:T(8,128)(2,1)S(1)} %shard_map.103.refs_0_), channel_id=1, source_target_pairs={{0,16},{8,24},{16,0},{24,8},{1,17},{9,25},{17,1},{25,9},{2,18},{10... | collective-permute-start | bytes 49160 | tf_op jit(solution)/shard_map/ppermute | solution.py:237
  21.8 4.6 %collective-permute-start.5 = (bf16[16,512]{1,0:T(8,128)(2,1)S(1)}, bf16[16,512]{1,0:T(8,128)(2,1)S(1)}, u32[]{:S(2)}, u32[]{:S(2)}) collective-permute-start(bf16[16,512]{1,0:T(8,128)(2,1)S(1)} %shard_map.103.refs_0_), channel_id=1, source_target_pairs={{0,8},{8,0},{16,24},{24,16},{1,9},{9,1},{17,25},{25,17},{2,10},{10... | collective-permute-start | bytes 49160 | tf_op jit(solution)/shard_map/ppermute | solution.py:237
  26.9 1.4 %collective-permute-start.8 = (bf16[32,2048]{1,0:T(8,128)(2,1)S(1)}, bf16[32,2048]{1,0:T(8,128)(2,1)S(1)}, u32[]{:S(2)}, u32[]{:S(2)}) collective-permute-start(bf16[32,2048]{1,0:T(8,128)(2,1)S(1)} %get-tuple-element.28), channel_id=1, source_target_pairs={{0,1},{1,0},{2,3},{3,2},{4,5},{5,4},{6,7},{7,6},{8,9},{9,8},{10,11... | collective-permute-start | bytes 393224 | tf_op jit(solution)/shard_map/ppermute | solution.py:237
  28.4 4.0 %collective-permute-start.9 = (bf16[8,2048]{1,0:T(8,128)(2,1)S(1)}, bf16[8,2048]{1,0:T(8,128)(2,1)S(1)}, u32[]{:S(2)}, u32[]{:S(2)}) collective-permute-start(bf16[8,2048]{1,0:T(8,128)(2,1)S(1)} %get-tuple-element.31), channel_id=1, source_target_pairs={{0,2},{1,3},{2,0},{3,1},{4,6},{5,7},{6,4},{7,5},{8,10},{9,11},{10,... | collective-permute-start | bytes 98312 | tf_op jit(solution)/shard_map/ppermute | solution.py:237
  29.7 4.8 %collective-permute-start.11 = (bf16[8,2048]{1,0:T(8,128)(2,1)S(1)}, bf16[8,2048]{1,0:T(8,128)(2,1)S(1)}, u32[]{:S(2)}, u32[]{:S(2)}) collective-permute-start(bf16[8,2048]{1,0:T(8,128)(2,1)S(1)} %get-tuple-element.32), channel_id=1, source_target_pairs={{0,6},{1,7},{2,4},{3,5},{4,2},{5,3},{6,0},{7,1},{8,14},{9,15},{10,... | collective-permute-start | bytes 98312 | tf_op jit(solution)/shard_map/ppermute | solution.py:237
  31.5 3.9 %collective-permute-start.10 = (bf16[8,2048]{1,0:T(8,128)(2,1)S(1)}, bf16[8,2048]{1,0:T(8,128)(2,1)S(1)}, u32[]{:S(2)}, u32[]{:S(2)}) collective-permute-start(bf16[8,2048]{1,0:T(8,128)(2,1)S(1)} %get-tuple-element.33), channel_id=1, source_target_pairs={{0,4},{1,5},{2,6},{3,7},{4,0},{5,1},{6,2},{7,3},{8,12},{9,13},{10,... | collective-permute-start | bytes 98312 | tf_op jit(solution)/shard_map/ppermute | solution.py:237

commit v3 on v2

--- a/solution.py
+++ b/solution.py
@@ -9,6 +9,7 @@
 from jax.sharding import PartitionSpec as P
 
 BLOCK_TOKENS = 128
+KEPT_SLOTS = 2
 NEGATIVE = -1e30
 F32 = jnp.float32
 BF16 = jnp.bfloat16
@@ -58,36 +59,50 @@
     queries = q_ref[...].astype(F32)
     step_keys = step_key_ref[...].astype(F32)
     step_values = step_value_ref[...].astype(F32)
-    length = len_ref[0]
-    position = lax.broadcasted_iota(jnp.int32, (rows, tail_key_ref.shape[1]), 1)
-    step_of_row = lax.div(lax.broadcasted_iota(jnp.int32, (rows, 1), 0), group)
-    for h in range(heads):
-        q = rows_of_head(queries, shape, h)
-        scores = dot_rows(q.astype(BF16), tail_key_ref[h]) * scale
-        scores = jnp.where(position < length, scores, NEGATIVE)
-        own = []
-        for u in range(steps):
-            score = jnp.sum(q * step_keys[u, h : h + 1], axis=1, keepdims=True) * scale
-            own.append(jnp.where(step_of_row >= u, score, NEGATIVE))
-        top = jnp.max(scores, axis=1, keepdims=True)
-        for score in own:
-            top = jnp.maximum(top, score)
-        top = top.astype(BF16).astype(F32)
-        weights = jnp.exp(scores - top)
-        total = jnp.sum(weights, axis=1, keepdims=True)
-        summed = jnp.dot(weights.astype(BF16), tail_value_ref[h], preferred_element_type=F32)
-        for u, score in enumerate(own):
-            weight = jnp.exp(score - top)
-            total = total + weight
-            summed = summed + weight.astype(BF16).astype(F32) * step_values[u, h : h + 1]
-        summed_high = summed.astype(BF16)
-        summed_rest = (summed - summed_high.astype(F32)).astype(BF16)
-        total_high = total.astype(BF16).astype(F32)
-        kept = kept_ref[h].astype(F32)
-        stats = lanes_of(rows, dim, [top, total_high, total - total_high, kept])
-        parts = [summed_high, summed_rest, stats.astype(BF16), q.astype(BF16)]
-        for i, part in enumerate(parts):
-            small[h, i * rows : (i + 1) * rows, :] = part
+    all_rows = heads * rows
+    q = jnp.concatenate([rows_of_head(queries, shape, h) for h in range(heads)], axis=0)
+    q_narrow = q.astype(BF16)
+
+    def by_head(x):
+        return [x[h * rows : (h + 1) * rows] for h in range(heads)]
+
+    def spread(x):
+        return jnp.concatenate([jnp.broadcast_to(x[h : h + 1], (rows, dim)) for h in range(heads)], axis=0)
+
+    scores = jnp.concatenate(
+        [dot_rows(part, tail_key_ref[h]) for h, part in enumerate(by_head(q_narrow))], axis=0
+    )
+    position = lax.broadcasted_iota(jnp.int32, scores.shape, 1)
+    scores = jnp.where(position < len_ref[0], scores * scale, NEGATIVE)
+    row = lax.broadcasted_iota(jnp.int32, (all_rows, 1), 0)
+    step_of_row = lax.rem(lax.div(row, group), steps)
+    own = []
+    for u in range(steps):
+        score = jnp.sum(q * spread(step_keys[u]), axis=1, keepdims=True) * scale
+        own.append(jnp.where(step_of_row >= u, score, NEGATIVE))
+    top = functools.reduce(jnp.maximum, own, jnp.max(scores, axis=1, keepdims=True))
+    top = top.astype(BF16).astype(F32)
+    weights = jnp.exp(scores - top)
+    total = jnp.sum(weights, axis=1, keepdims=True)
+    summed = jnp.concatenate(
+        [
+            jnp.dot(part, tail_value_ref[h], preferred_element_type=F32)
+            for h, part in enumerate(by_head(weights.astype(BF16)))
+        ],
+        axis=0,
+    )
+    for u, score in enumerate(own):
+        weight = jnp.exp(score - top)
+        total = total + weight
+        summed = summed + weight.astype(BF16).astype(F32) * spread(step_values[u])
+    summed_high = summed.astype(BF16)
+    summed_rest = (summed - summed_high.astype(F32)).astype(BF16)
+    total_high = total.astype(BF16).astype(F32)
+    kept = jnp.concatenate([jnp.full((rows, 1), kept_ref[h].astype(F32)) for h in range(heads)], axis=0)
+    stats = lanes_of(all_rows, dim, [top, total_high, total - total_high, kept]).astype(BF16)
+    for i, part in enumerate([summed_high, summed_rest, stats, q_narrow]):
+        for h, piece in enumerate(by_head(part)):
+            small[h, i * rows : (i + 1) * rows, :] = piece
     for x in range(heads):
         out_refs[x][2 * chunk : 2 * chunk + 4 * rows, :] = small[chip ^ x]
     for copy in copies[len(held) :]:
@@ -127,7 +142,6 @@
 def prefix_kernel(shape, message_refs, out_refs, q_all, tails, merged):
     heads, steps, group, dim, ranks, chunk = shape
     rows = steps * group
-    local = group // ranks
     scale = 1.0 / math.sqrt(dim)
     me = lax.axis_index("seq")
     chip, rank = lax.div(me, ranks), lax.rem(me, ranks)
@@ -173,21 +187,15 @@
             message_refs[x][chunk : 2 * chunk, :],
             preferred_element_type=F32,
         )
-    merged[0] = summed
-    merged[1] = lanes_of(all_rows, dim, [top, total])
-    count = all_rows // group
+    merged[:, 0:dim] = summed
+    merged[:, dim:] = lanes_of(all_rows, dim, [top, total])
+    block = all_rows // ranks
     for y in range(ranks):
-        for i in range(local):
-            head = (rank ^ y) * local + i
-            for j in range(2):
-                out_refs[y][i * count : (i + 1) * count, j * dim : (j + 1) * dim] = merged[
-                    j, pl.ds(head, count, stride=group), :
-                ]
-
-
-def merge_kernel(local, part_refs, out_ref):
-    dim = out_ref.shape[1] // local
-    count = out_ref.shape[0]
+        out_refs[y][...] = merged[pl.ds(pl.multiple_of((rank ^ y) * block, block), block), :]
+
+
+def merge_kernel(group, part_refs, out_ref, merged):
+    dim = out_ref.shape[1] // group
     tops = [ref[:, dim + MAX_LANE : dim + MAX_LANE + 1] for ref in part_refs]
     top = functools.reduce(jnp.maximum, tops)
     total, summed = 0.0, 0.0
@@ -195,26 +203,29 @@
         factor = jnp.exp(part_top - top)
         total = total + ref[:, dim + SUM_LANE : dim + SUM_LANE + 1] * factor
         summed = summed + ref[:, 0:dim] * factor
-    head_out = summed / total
-    for i in range(local):
-        out_ref[:, i * dim : (i + 1) * dim] = head_out[i * count : (i + 1) * count].astype(BF16)
-
-
-def project_kernel(heads, ranks, head_refs, weight_ref, out_refs, all_heads, product):
+    merged[...] = summed / total
+    count = out_ref.shape[0]
+    for g in range(group):
+        out_ref[:, g * dim : (g + 1) * dim] = merged[pl.ds(g, count, stride=group), :].astype(BF16)
+
+
+def project_kernel(ranks, head_refs, weight_refs, out_refs, all_heads):
     me = lax.axis_index("seq")
     chip, rank = lax.div(me, ranks), lax.rem(me, ranks)
     prompt = lax.axis_index("prompt")
     count = head_refs[0].shape[0]
     for x, ref in enumerate(head_refs):
-        all_heads[pl.ds(pl.multiple_of((prompt ^ x) * count, count), count), :] = ref[...]
-    product[...] = jnp.dot(all_heads[...], weight_ref[...], preferred_element_type=F32)
-    size = product.shape[0] // (heads * ranks)
-    for y in range(ranks):
-        pieces = [
-            product[pl.ds(pl.multiple_of(((chip ^ x) * ranks + (rank ^ y)) * size, size), size), :]
-            for x in range(heads)
-        ]
-        out_refs[y][...] = jnp.concatenate(pieces, axis=0).astype(out_refs[y].dtype)
+        place = pl.multiple_of((chip ^ prompt ^ x) * count, count)
+        all_heads[pl.ds(place, count), :] = ref[...].astype(F32)
+    depth = weight_refs[0].shape[0]
+    product = 0.0
+    for y, ref in enumerate(weight_refs):
+        columns = pl.ds(pl.multiple_of((rank ^ y) * depth, depth), depth)
+        product = product + jnp.dot(
+            all_heads[:, columns].astype(BF16), ref[...], preferred_element_type=F32
+        )
+    for x, ref in enumerate(out_refs):
+        ref[...] = product[x * count : (x + 1) * count].astype(ref.dtype)
 
 
 def call(kernel, out_shape, in_specs, scratch_shapes=(), aliases=None):
@@ -235,6 +246,169 @@
 
 def swap(x, axis, distance):
     return lax.ppermute(x, axis, [(i, i ^ distance) for i in range(lax.axis_size(axis))])
+
+
+def joined(x, axis, combine):
+    everything = jax.tree.map(lambda part: lax.all_gather(part, axis), x)
+    initial = jax.tree.map(lambda part: part[0], everything)
+
+    def lap(k, so_far):
+        return combine(so_far, jax.tree.map(lambda part: part[k], everything))
+
+    return lax.fori_loop(1, lax.axis_size(axis), lap, initial)
+
+
+def combine(earlier, later):
+    highest = jnp.maximum(earlier[0], later[0])
+    early_factor = jnp.exp(earlier[0] - highest)
+    late_factor = jnp.exp(later[0] - highest)
+    softmax_total = earlier[1] * early_factor + later[1] * late_factor
+    summed = earlier[2] * early_factor[..., None] + later[2] * late_factor[..., None]
+    return (highest, softmax_total, summed)
+
+
+def general_path(
+    queries,
+    prompt_key_cache,
+    prompt_value_cache,
+    kept,
+    sample_keys,
+    sample_values,
+    suffix_len,
+    decode_keys,
+    decode_values,
+    out_weight,
+):
+    seq_count = lax.axis_size("seq")
+    seq_index = lax.axis_index("seq")
+    own_count = queries.shape[1]
+    step_count = queries.shape[2]
+    head_count = queries.shape[3]
+    head_dim = queries.shape[4]
+    kv_count = prompt_key_cache.shape[1]
+    group_size = head_count // kv_count
+    logit_scale = 1.0 / math.sqrt(head_dim)
+    gathered = lax.all_gather(queries, "seq", axis=1, tiled=True)
+    sample_count = gathered.shape[1]
+    grouped_queries = gathered[0].reshape(sample_count, step_count, kv_count, group_size, head_dim)
+    query_rows = jnp.transpose(grouped_queries, (2, 0, 1, 3, 4)).reshape(
+        kv_count, sample_count * step_count * group_size, head_dim
+    )
+    key_cache_store = prompt_key_cache[0].reshape(kv_count, KEPT_SLOTS, BLOCK_TOKENS, head_dim)
+    value_cache_store = prompt_value_cache[0].reshape(kv_count, KEPT_SLOTS, BLOCK_TOKENS, head_dim)
+    kept_block_counts = kept[0, :, 0]
+    active_mask = jnp.arange(KEPT_SLOTS, dtype=jnp.int32)[None, :] < kept_block_counts[:, None]
+
+    def one_head(pieces):
+        head_row_block, key_block_list, value_block_list, live_blocks = pieces
+        logit_scores = (
+            jnp.einsum(
+                "eg,mxg->emx", head_row_block, key_block_list, preferred_element_type=jnp.float32
+            )
+            * logit_scale
+        )
+        block_max = jnp.where(live_blocks[None, :], jnp.max(logit_scores, axis=2), NEGATIVE)
+        attention_weights = jnp.where(
+            live_blocks[None, :, None], jnp.exp(logit_scores - block_max[:, :, None]), 0.0
+        )
+        block_sum = jnp.sum(attention_weights, axis=2)
+        block_output = jnp.einsum(
+            "yaf,afi->yai",
+            attention_weights.astype(jnp.bfloat16),
+            value_block_list,
+            preferred_element_type=jnp.float32,
+        )
+        highest = jnp.max(block_max, axis=1)
+        factor = jnp.exp(block_max - highest[:, None])
+        return (
+            highest,
+            jnp.sum(factor * block_sum, axis=1),
+            jnp.sum(factor[:, :, None] * block_output, axis=1),
+        )
+
+    prompt_maximum, prompt_sum, prompt_output = lax.map(
+        one_head, (query_rows, key_cache_store, value_cache_store, active_mask)
+    )
+    own_queries = queries[0].reshape(own_count, step_count, kv_count, group_size, head_dim)
+    suffix_scores = (
+        jnp.einsum(
+            "nthgd,nhid->nhtgi", own_queries, sample_keys[0], preferred_element_type=jnp.float32
+        )
+        * logit_scale
+    )
+    fresh_scores = (
+        jnp.einsum(
+            "nthgd,nuhd->nhtgu", own_queries, decode_keys[0], preferred_element_type=jnp.float32
+        )
+        * logit_scale
+    )
+    position = jnp.arange(sample_keys.shape[3], dtype=jnp.int32)
+    sample_token_mask = (position[None, :] < suffix_len[0][:, None])[:, None, None, None, :]
+    step_index = jnp.arange(step_count, dtype=jnp.int32)
+    newest_token_mask = (step_index[None, :] <= step_index[:, None])[None, None, :, None, :]
+    tail_max = jnp.maximum(
+        jnp.max(jnp.where(sample_token_mask, suffix_scores, NEGATIVE), axis=4),
+        jnp.max(jnp.where(newest_token_mask, fresh_scores, NEGATIVE), axis=4),
+    )
+    suffix_weights = jnp.where(sample_token_mask, jnp.exp(suffix_scores - tail_max[..., None]), 0.0)
+    fresh_weights = jnp.where(newest_token_mask, jnp.exp(fresh_scores - tail_max[..., None]), 0.0)
+    tail_sum = jnp.sum(suffix_weights, axis=4) + jnp.sum(fresh_weights, axis=4)
+    tail_out = jnp.einsum(
+        "nhtgi,nhid->nhtgd",
+        suffix_weights.astype(jnp.bfloat16),
+        sample_values[0],
+        preferred_element_type=jnp.float32,
+    )
+    tail_out = tail_out + jnp.einsum(
+        "nhtgu,nuhd->nhtgd",
+        fresh_weights.astype(jnp.bfloat16),
+        decode_values[0],
+        preferred_element_type=jnp.float32,
+    )
+    tail_part = (
+        jnp.transpose(tail_max, (1, 0, 2, 3)),
+        jnp.transpose(tail_sum, (1, 0, 2, 3)),
+        jnp.transpose(tail_out, (1, 0, 2, 3, 4)),
+    )
+    prefix = (
+        prompt_maximum.reshape(kv_count, sample_count, step_count, group_size),
+        prompt_sum.reshape(kv_count, sample_count, step_count, group_size),
+        prompt_output.reshape(kv_count, sample_count, step_count, group_size, head_dim),
+    )
+    offset = seq_index * own_count
+    own_part = tuple((lax.dynamic_slice_in_dim(member, offset, own_count, 1) for member in prefix))
+    merged = combine(own_part, tail_part)
+    prefix = tuple(
+        (
+            lax.dynamic_update_slice_in_dim(member, update, offset, 1)
+            for member, update in zip(prefix, merged)
+        )
+    )
+    part_max = jnp.transpose(prefix[0], (1, 2, 0, 3)).reshape(sample_count, step_count, head_count)
+    part_total = jnp.transpose(prefix[1], (1, 2, 0, 3)).reshape(
+        sample_count, step_count, head_count
+    )
+    part_out = jnp.transpose(prefix[2], (1, 2, 0, 3, 4)).reshape(
+        sample_count, step_count, head_count, head_dim
+    )
+    local_heads = head_count // seq_count
+    highest, softmax_total, summed = joined((part_max, part_total, part_out), "seq", combine)
+    highest = lax.dynamic_slice_in_dim(highest, seq_index * local_heads, local_heads, 2)
+    softmax_total = lax.dynamic_slice_in_dim(softmax_total, seq_index * local_heads, local_heads, 2)
+    summed = lax.dynamic_slice_in_dim(summed, seq_index * local_heads, local_heads, 2)
+    head_out = (
+        (summed / softmax_total[..., None])
+        .astype(jnp.bfloat16)
+        .reshape(sample_count * step_count, local_heads * head_dim)
+    )
+    all_rows = lax.all_gather(head_out, "prompt", axis=0, tiled=True)
+    result = lax.psum_scatter(
+        jnp.dot(all_rows, out_weight, preferred_element_type=jnp.float32),
+        "seq",
+        scatter_dimension=0,
+        tiled=True,
+    )
+    return result.astype(jnp.bfloat16)
 
 
 def on_device(
@@ -250,11 +424,15 @@
     out_weight,
 ):
     seq_count, prompt_count = lax.axis_size("seq"), lax.axis_size("prompt")
+    if prompt_count != prompt_key_cache.shape[1]:
+        return general_path(
+            queries, prompt_key_cache, prompt_value_cache, kept, sample_keys, sample_values,
+            suffix_len, decode_keys, decode_values, out_weight,
+        )
     steps, head_count, dim = queries.shape[2:]
     heads, chunk = prompt_key_cache.shape[1:3]
     group = head_count // heads
     ranks = seq_count // heads
-    local = group // ranks
     shape = (heads, steps, group, dim, ranks, chunk)
     rows = steps * group
     vmem = pl.BlockSpec(memory_space=pltpu.VMEM)
@@ -290,7 +468,7 @@
             pltpu.VMEM((heads, 4 * rows, dim), BF16),
             pltpu.SemaphoreType.DMA((len(fetched) + 2 * heads,)),
         ],
-    )(*[x if x.dtype == jnp.int32 else in_hbm(x) for x in sources])
+    )(*[x if x.size == 1 else in_hbm(x) for x in sources])
 
     def run_query(*refs):
         n = ranks - 1
@@ -304,6 +482,8 @@
             [pltpu.VMEM((heads, (ranks - 1) * rows, dim), BF16)],
             {ranks - 1 + x: x for x in range(heads)},
         )(*other_queries, *messages)
+    late_weight, messages = lax.optimization_barrier((out_weight, messages))
+    other_weights = [swap(late_weight, "seq", y) for y in range(1, ranks)]
     weight = call(
         fetch_kernel,
         jax.ShapeDtypeStruct(out_weight.shape, BF16),
@@ -313,8 +493,8 @@
     messages = [messages[0]] + [swap(messages[x], "seq", x * ranks) for x in range(1, heads)]
 
     all_rows = seq_count * rows
-    count = seq_count * steps
-    part = jax.ShapeDtypeStruct((local * count, 2 * dim), F32)
+    block = all_rows // ranks
+    part = jax.ShapeDtypeStruct((block, 2 * dim), F32)
 
     def run_prefix(*refs):
         prefix_kernel(shape, refs[:heads], refs[heads : heads + ranks], *refs[heads + ranks :])
@@ -326,45 +506,39 @@
         [
             pltpu.VMEM((all_rows, dim), BF16),
             pltpu.VMEM((all_rows, 2 * dim), F32),
-            pltpu.VMEM((2, all_rows, dim), F32),
+            pltpu.VMEM((all_rows, 2 * dim), F32),
         ],
     )(*messages)
     parts = [parts[0]] + [swap(parts[y], "seq", y) for y in range(1, ranks)]
 
     def run_merge(*refs):
-        merge_kernel(local, refs[:ranks], refs[ranks])
-
+        merge_kernel(group, refs[:ranks], *refs[ranks:])
+
+    count = block // group
     head_out = call(
-        run_merge, jax.ShapeDtypeStruct((count, local * dim), BF16), [vmem] * ranks
+        run_merge,
+        jax.ShapeDtypeStruct((count, group * dim), BF16),
+        [vmem] * ranks,
+        [pltpu.VMEM((block, dim), F32)],
     )(*parts)
     head_outs = [head_out] + [swap(head_out, "prompt", x) for x in range(1, prompt_count)]
 
-    columns = out_weight.shape[1]
-    row_count = count * prompt_count
-    size = row_count // seq_count
-
     def run_project(*refs):
-        project_kernel(
-            heads, ranks, refs[:prompt_count], refs[prompt_count],
-            refs[prompt_count + 1 : prompt_count + 1 + ranks], *refs[prompt_count + 1 + ranks :]
-        )
+        n, m = prompt_count, prompt_count + ranks
+        project_kernel(ranks, refs[:n], refs[n:m], refs[m : m + heads], refs[m + heads])
 
     terms = call(
         run_project,
-        [jax.ShapeDtypeStruct((heads * size, columns), BF16 if y else F32) for y in range(ranks)],
-        [vmem] * (prompt_count + 1),
         [
-            pltpu.VMEM((row_count, local * dim), BF16),
-            pltpu.VMEM((row_count, columns), F32),
+            jax.ShapeDtypeStruct((count, out_weight.shape[1]), BF16 if x else F32)
+            for x in range(heads)
         ],
-    )(*head_outs, weight)
-    total = terms[0]
-    for y in range(1, ranks):
-        total = total + swap(terms[y], "seq", y).astype(F32)
-    total = total.reshape(heads, size, columns)
-    result = total[0]
-    for x in range(1, heads):
-        result = result + swap(total[x].astype(BF16), "seq", x * ranks).astype(F32)
+        [vmem] * (prompt_count + ranks),
+        [pltpu.VMEM((prompt_count * count, group * dim), F32)],
+    )(*head_outs, weight, *other_weights)
+    result = terms[0]
+    for x in reversed(range(1, heads)):
+        result = result + swap(terms[x], "seq", x * ranks).astype(F32)
     return result.astype(BF16)
 
 

time: 36.3 us -> 33.5 us (0.923)
  waiting for transfers between devices: 16 us -> 14 us
  local copies, waits for them, and re-layouts: 0.66 us -> 0 us
  starting transfers between devices: 12.7 us -> 13.1 us
  Pallas kernels: 5.23 us -> 4.85 us
    ppermute x12, waiting for transfers between devices: 16 us -> 14 us  [swap(): lax.ppermute(x, axis, [(i, i ^ distance) for i in range(lax.axis_size(axi...]
    pallas_call x1, Pallas kernels: 2.3 us -> 1.62 us  [on_device(): call(run_message, [message] * heads, [hbm] * len(sources), [(pltpu.SMEM i...]
    unnamed x2 -> x0, local copies, waits for them, and re-layouts: 0.65 us -> none
    ppermute x12, starting transfers between devices: 12.7 us -> 13.1 us  [swap(): lax.ppermute(x, axis, [(i, i ^ distance) for i in range(lax.axis_size(axi...]
  transfers between devices with their start and end apart: 12 -> 12, of which waited for: 8 -> 7; matrix products, arithmetic and copies ran while one was open for 0% -> 0% of each run, Pallas kernels for 11% -> 12%
where the time goes in v3:
time: 33.5 us; the launch traced here: 33.2 us
  waiting for transfers between devices  14 us (42%)
  starting transfers between devices  13.1 us (39%)
  Pallas kernels  4.85 us (14%)
  between operations  0.72 us (2%)
  other arithmetic  0.64 us (2%)
    ppermute x12, waiting for transfers between devices, swap(): lax.ppermute(x, axis, [(i, i ^ distance) for i in range(lax.axis_size(axi...  14 us
    ppermute x12, starting transfers between devices, swap(): lax.ppermute(x, axis, [(i, i ^ distance) for i in range(lax.axis_size(axi...  13.1 us
    pallas_call x1, Pallas kernels, on_device(): call(run_message, [message] * heads, [hbm] * len(sources), [(pltpu.SMEM i...  1.62 us
    pallas_call x1, Pallas kernels, on_device(): call(fetch_kernel, jax.ShapeDtypeStruct(out_weight.shape, BF16), [pl.Bloc...  1.6 us
    pallas_call x1, Pallas kernels, on_device(): call(run_project, [jax.ShapeDtypeStruct((count, out_weight.shape[1]), BF1...  0.82 us
  transfers between devices with their start and end apart: 12, of which 7 were waited for; matrix products, arithmetic and copies ran while one was open for 0% of the time, Pallas kernels for 12%

profile of v3, /device:TPU:0, one launch (start us, length us, event | category | flops | bytes accessed | tf_op | source)
XLA Modules:
  0.0 33.2 jit_solution(15801597673335022703)
XLA Ops:
  0.0 0.5 %collective-permute-start = (bf16[64,128]{1,0:T(8,128)(2,1)}, bf16[64,128]{1,0:T(8,128)(2,1)S(1)}, u32[]{:S(2)}, u32[]{:S(2)}) collective-permute-start(bf16[64,128]{1,0:T(8,128)(2,1)} %bitcast.14), channel_id=1, source_target_pairs={{0,1},{1,0},{2,3},{3,2},{4,5},{5,4},{6,7},{7,6},{8,9},{9,8},{10,11... | collective-permute-start | bytes 49160 | tf_op jit(solution)/shard_map/ppermute | solution.py:248
  1.1 1.6 %shard_map.100 = (bf16[592,128]{1,0:T(8,128)(2,1)S(1)}, bf16[592,128]{1,0:T(8,128)(2,1)S(1)}, bf16[592,128]{1,0:T(8,128)(2,1)S(1)}, bf16[592,128]{1,0:T(8,128)(2,1)S(1)}) custom-call(bf16[4,256,128]{2,1,0:T(8,128)(2,1)} %bitcast.10, bf16[4,256,128]{2,1,0:T(8,128)(2,1)} %bitcast.11, bf16[64,128]{1,0:T(8,128)(2,1)} %bitcast.15, bf16[4,256,128]{2,1,0:T(8,128)(2,1)} %bitcast.12, ...), custom_call_target="tpu_custom_call" | custom-call | tf_op jit(solution)/shard_map/pallas_call | solution.py:459
  2.7 0.0 collective-permute-done.refs_0_
  2.8 0.1 collective-permute-start.8
  2.9 2.9 %collective-permute-start.1 = (bf16[592,128]{1,0:T(8,128)(2,1)S(1)}, bf16[592,128]{1,0:T(8,128)(2,1)S(1)}, u32[]{:S(2)}, u32[]{:S(2)}) collective-permute-start(bf16[592,128]{1,0:T(8,128)(2,1)S(1)} %get-tuple-element.33), channel_id=1, source_target_pairs={{0,2},{1,3},{2,0},{3,1},{4,6},{5,7},{6,4},{7,5},{8,10},{9,11},{10,... | collective-permute-start | bytes 454664 | tf_op jit(solution)/shard_map/ppermute | solution.py:248
  5.8 1.5 %collective-permute-start.2 = (bf16[592,128]{1,0:T(8,128)(2,1)S(1)}, bf16[592,128]{1,0:T(8,128)(2,1)S(1)}, u32[]{:S(2)}, u32[]{:S(2)}) collective-permute-start(bf16[592,128]{1,0:T(8,128)(2,1)S(1)} %get-tuple-element.34), channel_id=1, source_target_pairs={{0,4},{1,5},{2,6},{3,7},{4,0},{5,1},{6,2},{7,3},{8,12},{9,13},{10,... | collective-permute-start | bytes 454664 | tf_op jit(solution)/shard_map/ppermute | solution.py:248
  7.4 0.0 collective-permute-start.3
  7.4 3.2 %collective-permute-done.1.refs_1_ = bf16[592,128]{1,0:T(8,128)(2,1)S(1)} collective-permute-done((bf16[592,128]{1,0:T(8,128)(2,1)S(1)}, bf16[592,128]{1,0:T(8,128)(2,1)S(1)}, u32[]{:S(2)}, u32[]{:S(2)}) %collective-permute-start.1) | collective-permute-done | bytes 151584 | tf_op jit(solution)/shard_map/ppermute | solution.py:248
  10.6 4.2 %collective-permute-done.2.refs_2_ = bf16[592,128]{1,0:T(8,128)(2,1)S(1)} collective-permute-done((bf16[592,128]{1,0:T(8,128)(2,1)S(1)}, bf16[592,128]{1,0:T(8,128)(2,1)S(1)}, u32[]{:S(2)}, u32[]{:S(2)}) %collective-permute-start.2) | collective-permute-done | bytes 151584 | tf_op jit(solution)/shard_map/ppermute | solution.py:248
  14.7 0.0 collective-permute-done.3.refs_3_
  14.7 0.6 %shard_map.102 = (f32[64,256]{1,0:T(8,128)S(1)}, f32[64,256]{1,0:T(8,128)S(1)}) custom-call(bf16[592,128]{1,0:T(8,128)(2,1)S(1)} %get-tuple-element.32.refs_0_.after_ref, bf16[592,128]{1,0:T(8,128)(2,1)S(1)} %collective-permute-done.1.refs_1_, bf16[592,128]{1,0:T(8,128)(2,1)S(1)} %collective-permute-done.2.refs_2_, ...), custom_call_target="tpu_custom_call" | custom-call | tf_op jit(solution)/shard_map/pallas_call | solution.py:502
  15.3 0.1 collective-permute-start.4
  15.4 1.2 %collective-permute-done.4.refs_1_ = f32[64,256]{1,0:T(8,128)S(1)} collective-permute-done((f32[64,256]{1,0:T(8,128)S(1)}, f32[64,256]{1,0:T(8,128)S(1)}, u32[]{:S(2)}, u32[]{:S(2)}) %collective-permute-start.4) | collective-permute-done | bytes 65568 | tf_op jit(solution)/shard_map/ppermute | solution.py:248
  16.7 0.2 shard_map.103.refs_0_
  16.8 3.7 %collective-permute-start.7 = (bf16[8,1024]{1,0:T(8,128)(2,1)S(1)}, bf16[8,1024]{1,0:T(8,128)(2,1)S(1)}, u32[]{:S(2)}, u32[]{:S(2)}) collective-permute-start(bf16[8,1024]{1,0:T(8,128)(2,1)S(1)} %shard_map.103.refs_0_), channel_id=1, source_target_pairs={{0,24},{8,16},{16,8},{24,0},{1,25},{9,17},{17,9},{25,1},{2,26},{10... | collective-permute-start | bytes 49160 | tf_op jit(solution)/shard_map/ppermute | solution.py:248
  20.5 0.0 collective-permute-start.6
  20.5 0.8 %collective-permute-start.5 = (bf16[8,1024]{1,0:T(8,128)(2,1)S(1)}, bf16[8,1024]{1,0:T(8,128)(2,1)S(1)}, u32[]{:S(2)}, u32[]{:S(2)}) collective-permute-start(bf16[8,1024]{1,0:T(8,128)(2,1)S(1)} %shard_map.103.refs_0_), channel_id=1, source_target_pairs={{0,8},{8,0},{16,24},{24,16},{1,9},{9,1},{17,25},{25,17},{2,10},{10... | collective-permute-start | bytes 49160 | tf_op jit(solution)/shard_map/ppermute | solution.py:248
  21.3 1.6 %shard_map.104.refs_4_ = bf16[512,2048]{1,0:T(8,128)(2,1)S(1)} custom-call(bf16[592,128]{1,0:T(8,128)(2,1)S(1)} %get-tuple-element.32.refs_0_.after_ref, bf16[512,2048]{1,0:T(8,128)(2,1)} %weight_ref.1), custom_call_target="tpu_custom_call" | custom-call | tf_op jit(solution)/shard_map/pallas_call | solution.py:487
  22.9 0.0 collective-permute-done.7.refs_3_
  22.9 2.2 %collective-permute-done.6.refs_2_ = bf16[8,1024]{1,0:T(8,128)(2,1)S(1)} collective-permute-done((bf16[8,1024]{1,0:T(8,128)(2,1)S(1)}, bf16[8,1024]{1,0:T(8,128)(2,1)S(1)}, u32[]{:S(2)}, u32[]{:S(2)}) %collective-permute-start.6) | collective-permute-done | bytes 16416 | tf_op jit(solution)/shard_map/ppermute | solution.py:248
  25.2 0.0 collective-permute-done.5.refs_1_
  25.2 0.0 collective-permute-done.8.refs_5_
  25.2 0.8 %shard_map.105 = (f32[8,2048]{1,0:T(8,128)S(1)}, bf16[8,2048]{1,0:T(8,128)(2,1)S(1)}, bf16[8,2048]{1,0:T(8,128)(2,1)S(1)}, bf16[8,2048]{1,0:T(8,128)(2,1)S(1)}) custom-call(bf16[8,1024]{1,0:T(8,128)(2,1)S(1)} %shard_map.103.refs_0_, bf16[8,1024]{1,0:T(8,128)(2,1)S(1)} %collective-permute-done.5.refs_1_, bf16[8,1024]{1,0:T(8,128)(2,1)S(1)} %collective-permute-done.6.refs_2_, ...), custom_call_target="tpu_custom_call" | custom-call | tf_op jit(solution)/shard_map/pallas_call | solution.py:530
  26.0 1.5 %collective-permute-start.9 = (bf16[8,2048]{1,0:T(8,128)(2,1)S(1)}, bf16[8,2048]{1,0:T(8,128)(2,1)S(1)}, u32[]{:S(2)}, u32[]{:S(2)}) collective-permute-start(bf16[8,2048]{1,0:T(8,128)(2,1)S(1)} %get-tuple-element.40), channel_id=1, source_target_pairs={{0,6},{1,7},{2,4},{3,5},{4,2},{5,3},{6,0},{7,1},{8,14},{9,15},{10,... | collective-permute-start | bytes 98312 | tf_op jit(solution)/shard_map/ppermute | solution.py:248
  27.5 1.2 %collective-permute-start.10 = (bf16[8,2048]{1,0:T(8,128)(2,1)S(1)}, bf16[8,2048]{1,0:T(8,128)(2,1)S(1)}, u32[]{:S(2)}, u32[]{:S(2)}) collective-permute-start(bf16[8,2048]{1,0:T(8,128)(2,1)S(1)} %get-tuple-element.41), channel_id=1, source_target_pairs={{0,4},{1,5},{2,6},{3,7},{4,0},{5,1},{6,2},{7,3},{8,12},{9,13},{10,... | collective-permute-start | bytes 98312 | tf_op jit(solution)/shard_map/ppermute | solution.py:248
  28.7 0.8 %collective-permute-start.11 = (bf16[8,2048]{1,0:T(8,128)(2,1)S(1)}, bf16[8,2048]{1,0:T(8,128)(2,1)S(1)}, u32[]{:S(2)}, u32[]{:S(2)}) collective-permute-start(bf16[8,2048]{1,0:T(8,128)(2,1)S(1)} %get-tuple-element.42), channel_id=1, source_target_pairs={{0,2},{1,3},{2,0},{3,1},{4,6},{5,7},{6,4},{7,5},{8,10},{9,11},{10,... | collective-permute-start | bytes 98312 | tf_op jit(solution)/shard_map/ppermute | solution.py:248
  29.5 1.3 %collective-permute-done.9 = bf16[8,2048]{1,0:T(8,128)(2,1)S(1)} collective-permute-done((bf16[8,2048]{1,0:T(8,128)(2,1)S(1)}, bf16[8,2048]{1,0:T(8,128)(2,1)S(1)}, u32[]{:S(2)}, u32[]{:S(2)}) %collective-permute-start.9) | collective-permute-done | bytes 32800 | tf_op jit(solution)/shard_map/ppermute | solution.py:248
  30.8 0.6 %collective-permute-done.10 = bf16[8,2048]{1,0:T(8,128)(2,1)S(1)} collective-permute-done((bf16[8,2048]{1,0:T(8,128)(2,1)S(1)}, bf16[8,2048]{1,0:T(8,128)(2,1)S(1)}, u32[]{:S(2)}, u32[]{:S(2)}) %collective-permute-start.10) | collective-permute-done | bytes 32800 | tf_op jit(solution)/shard_map/ppermute | solution.py:248
  31.4 1.2 %collective-permute-done.11 = bf16[8,2048]{1,0:T(8,128)(2,1)S(1)} collective-permute-done((bf16[8,2048]{1,0:T(8,128)(2,1)S(1)}, bf16[8,2048]{1,0:T(8,128)(2,1)S(1)}, u32[]{:S(2)}, u32[]{:S(2)}) %collective-permute-start.11) | collective-permute-done | bytes 32800 | tf_op jit(solution)/shard_map/ppermute | solution.py:248
  32.6 0.6 %add_convert_fusion = bf16[8,2048]{1,0:T(8,128)(2,1)} fusion(bf16[8,2048]{1,0:T(8,128)(2,1)S(1)} %collective-permute-done.11, bf16[8,2048]{1,0:T(8,128)(2,1)S(1)} %collective-permute-done.10, f32[8,2048]{1,0:T(8,128)S(1)} %get-tuple-element.39, bf16[8,2048]{1,0:T(8,128)(2,1)S(1)} %collective-permute-done.9), kind=kLoop, calls=%fused_computation | loop fusion | flops 114688 | bytes 196608 | tf_op jit(solution)/shard_map/convert_element_type | solution.py:542
  (1 shorter events, 0.0 us)
Async XLA Ops:
  0.0 2.7 %collective-permute-start = (bf16[64,128]{1,0:T(8,128)(2,1)}, bf16[64,128]{1,0:T(8,128)(2,1)S(1)}, u32[]{:S(2)}, u32[]{:S(2)}) collective-permute-start(bf16[64,128]{1,0:T(8,128)(2,1)} %bitcast.14), channel_id=1, source_target_pairs={{0,1},{1,0},{2,3},{3,2},{4,5},{5,4},{6,7},{7,6},{8,9},{9,8},{10,11... | collective-permute-start | bytes 49160 | tf_op jit(solution)/shard_map/ppermute | solution.py:248
  2.8 22.4 %collective-permute-start.8 = (bf16[512,2048]{1,0:T(8,128)(2,1)}, bf16[512,2048]{1,0:T(8,128)(2,1)S(1)}, u32[]{:S(2)}, u32[]{:S(2)}) collective-permute-start(bf16[512,2048]{1,0:T(8,128)(2,1)} %weight_ref.1), channel_id=1, source_target_pairs={{0,1},{1,0},{2,3},{3,2},{4,5},{5,4},{6,7},{7,6},{8,9},{9,8},{10,11... | collective-permute-start | bytes 6291464 | tf_op jit(solution)/shard_map/ppermute | solution.py:248
  2.9 7.7 %collective-permute-start.1 = (bf16[592,128]{1,0:T(8,128)(2,1)S(1)}, bf16[592,128]{1,0:T(8,128)(2,1)S(1)}, u32[]{:S(2)}, u32[]{:S(2)}) collective-permute-start(bf16[592,128]{1,0:T(8,128)(2,1)S(1)} %get-tuple-element.33), channel_id=1, source_target_pairs={{0,2},{1,3},{2,0},{3,1},{4,6},{5,7},{6,4},{7,5},{8,10},{9,11},{10,... | collective-permute-start | bytes 454664 | tf_op jit(solution)/shard_map/ppermute | solution.py:248
  5.8 8.9 %collective-permute-start.2 = (bf16[592,128]{1,0:T(8,128)(2,1)S(1)}, bf16[592,128]{1,0:T(8,128)(2,1)S(1)}, u32[]{:S(2)}, u32[]{:S(2)}) collective-permute-start(bf16[592,128]{1,0:T(8,128)(2,1)S(1)} %get-tuple-element.34), channel_id=1, source_target_pairs={{0,4},{1,5},{2,6},{3,7},{4,0},{5,1},{6,2},{7,3},{8,12},{9,13},{10,... | collective-permute-start | bytes 454664 | tf_op jit(solution)/shard_map/ppermute | solution.py:248
  7.4 7.4 %collective-permute-start.3 = (bf16[592,128]{1,0:T(8,128)(2,1)S(1)}, bf16[592,128]{1,0:T(8,128)(2,1)S(1)}, u32[]{:S(2)}, u32[]{:S(2)}) collective-permute-start(bf16[592,128]{1,0:T(8,128)(2,1)S(1)} %get-tuple-element.35), channel_id=1, source_target_pairs={{0,6},{1,7},{2,4},{3,5},{4,2},{5,3},{6,0},{7,1},{8,14},{9,15},{10,... | collective-permute-start | bytes 454664 | tf_op jit(solution)/shard_map/ppermute | solution.py:248
  15.3 1.3 %collective-permute-start.4 = (f32[64,256]{1,0:T(8,128)S(1)}, f32[64,256]{1,0:T(8,128)S(1)}, u32[]{:S(2)}, u32[]{:S(2)}) collective-permute-start(f32[64,256]{1,0:T(8,128)S(1)} %get-tuple-element.37), channel_id=1, source_target_pairs={{0,1},{1,0},{2,3},{3,2},{4,5},{5,4},{6,7},{7,6},{8,9},{9,8},{10,11... | collective-permute-start | bytes 196616 | tf_op jit(solution)/shard_map/ppermute | solution.py:248
  16.8 6.1 %collective-permute-start.7 = (bf16[8,1024]{1,0:T(8,128)(2,1)S(1)}, bf16[8,1024]{1,0:T(8,128)(2,1)S(1)}, u32[]{:S(2)}, u32[]{:S(2)}) collective-permute-start(bf16[8,1024]{1,0:T(8,128)(2,1)S(1)} %shard_map.103.refs_0_), channel_id=1, source_target_pairs={{0,24},{8,16},{16,8},{24,0},{1,25},{9,17},{17,9},{25,1},{2,26},{10... | collective-permute-start | bytes 49160 | tf_op jit(solution)/shard_map/ppermute | solution.py:248
  20.5 4.6 %collective-permute-start.6 = (bf16[8,1024]{1,0:T(8,128)(2,1)S(1)}, bf16[8,1024]{1,0:T(8,128)(2,1)S(1)}, u32[]{:S(2)}, u32[]{:S(2)}) collective-permute-start(bf16[8,1024]{1,0:T(8,128)(2,1)S(1)} %shard_map.103.refs_0_), channel_id=1, source_target_pairs={{0,16},{8,24},{16,0},{24,8},{1,17},{9,25},{17,1},{25,9},{2,18},{10... | collective-permute-start | bytes 49160 | tf_op jit(solution)/shard_map/ppermute | solution.py:248
  20.5 4.6 %collective-permute-start.5 = (bf16[8,1024]{1,0:T(8,128)(2,1)S(1)}, bf16[8,1024]{1,0:T(8,128)(2,1)S(1)}, u32[]{:S(2)}, u32[]{:S(2)}) collective-permute-start(bf16[8,1024]{1,0:T(8,128)(2,1)S(1)} %shard_map.103.refs_0_), channel_id=1, source_target_pairs={{0,8},{8,0},{16,24},{24,16},{1,9},{9,1},{17,25},{25,17},{2,10},{10... | collective-permute-start | bytes 49160 | tf_op jit(solution)/shard_map/ppermute | solution.py:248
  26.0 4.8 %collective-permute-start.9 = (bf16[8,2048]{1,0:T(8,128)(2,1)S(1)}, bf16[8,2048]{1,0:T(8,128)(2,1)S(1)}, u32[]{:S(2)}, u32[]{:S(2)}) collective-permute-start(bf16[8,2048]{1,0:T(8,128)(2,1)S(1)} %get-tuple-element.40), channel_id=1, source_target_pairs={{0,6},{1,7},{2,4},{3,5},{4,2},{5,3},{6,0},{7,1},{8,14},{9,15},{10,... | collective-permute-start | bytes 98312 | tf_op jit(solution)/shard_map/ppermute | solution.py:248
  27.5 3.9 %collective-permute-start.10 = (bf16[8,2048]{1,0:T(8,128)(2,1)S(1)}, bf16[8,2048]{1,0:T(8,128)(2,1)S(1)}, u32[]{:S(2)}, u32[]{:S(2)}) collective-permute-start(bf16[8,2048]{1,0:T(8,128)(2,1)S(1)} %get-tuple-element.41), channel_id=1, source_target_pairs={{0,4},{1,5},{2,6},{3,7},{4,0},{5,1},{6,2},{7,3},{8,12},{9,13},{10,... | collective-permute-start | bytes 98312 | tf_op jit(solution)/shard_map/ppermute | solution.py:248
  28.7 3.9 %collective-permute-start.11 = (bf16[8,2048]{1,0:T(8,128)(2,1)S(1)}, bf16[8,2048]{1,0:T(8,128)(2,1)S(1)}, u32[]{:S(2)}, u32[]{:S(2)}) collective-permute-start(bf16[8,2048]{1,0:T(8,128)(2,1)S(1)} %get-tuple-element.42), channel_id=1, source_target_pairs={{0,2},{1,3},{2,0},{3,1},{4,6},{5,7},{6,4},{7,5},{8,10},{9,11},{10,... | collective-permute-start | bytes 98312 | tf_op jit(solution)/shard_map/ppermute | solution.py:248

commit v4 on v3

--- a/solution.py
+++ b/solution.py
@@ -139,7 +139,7 @@
     copy.wait()
 
 
-def prefix_kernel(shape, message_refs, out_refs, q_all, tails, merged):
+def prefix_kernel(shape, message_refs, out_ref, q_all, tails):
     heads, steps, group, dim, ranks, chunk = shape
     rows = steps * group
     scale = 1.0 / math.sqrt(dim)
@@ -187,15 +187,17 @@
             message_refs[x][chunk : 2 * chunk, :],
             preferred_element_type=F32,
         )
-    merged[:, 0:dim] = summed
-    merged[:, dim:] = lanes_of(all_rows, dim, [top, total])
-    block = all_rows // ranks
-    for y in range(ranks):
-        out_refs[y][...] = merged[pl.ds(pl.multiple_of((rank ^ y) * block, block), block), :]
-
-
-def merge_kernel(group, part_refs, out_ref, merged):
-    dim = out_ref.shape[1] // group
+    out_ref[:, 0:dim] = summed
+    out_ref[:, dim:] = lanes_of(all_rows, dim, [top, total])
+
+
+def block_of(rank, chip, prompt, ranks):
+    return rank ^ jnp.where(chip == prompt, 0, 1) if ranks > 1 else rank
+
+
+def merge_kernel(group, ranks, part_refs, out_refs, merged):
+    count = out_refs[0].shape[0]
+    dim = out_refs[0].shape[1] // group
     tops = [ref[:, dim + MAX_LANE : dim + MAX_LANE + 1] for ref in part_refs]
     top = functools.reduce(jnp.maximum, tops)
     total, summed = 0.0, 0.0
@@ -204,9 +206,14 @@
         total = total + ref[:, dim + SUM_LANE : dim + SUM_LANE + 1] * factor
         summed = summed + ref[:, 0:dim] * factor
     merged[...] = summed / total
-    count = out_ref.shape[0]
-    for g in range(group):
-        out_ref[:, g * dim : (g + 1) * dim] = merged[pl.ds(g, count, stride=group), :].astype(BF16)
+    me = lax.axis_index("seq")
+    chip, rank = lax.div(me, ranks), lax.rem(me, ranks)
+    prompt = lax.axis_index("prompt")
+    for out_ref, side in zip(out_refs, (0, 1 if ranks > 1 else 0)):
+        block = block_of(rank ^ side, chip, prompt, ranks)
+        for g in range(group):
+            place = pl.ds(block * (count * group) + g, count, stride=group)
+            out_ref[:, g * dim : (g + 1) * dim] = merged[place, :].astype(BF16)
 
 
 def project_kernel(ranks, head_refs, weight_refs, out_refs, all_heads):
@@ -411,6 +418,16 @@
     return result.astype(jnp.bfloat16)
 
 
+def cross(x, target):
+    prompts, seqs = lax.axis_size("prompt"), lax.axis_size("seq")
+    pairs = []
+    for p in range(prompts):
+        for s in range(seqs):
+            to_p, to_s = target(p, s)
+            pairs.append((p * seqs + s, to_p * seqs + to_s))
+    return lax.ppermute(x, ("prompt", "seq"), pairs)
+
+
 def on_device(
     queries,
     prompt_key_cache,
@@ -493,35 +510,32 @@
     messages = [messages[0]] + [swap(messages[x], "seq", x * ranks) for x in range(1, heads)]
 
     all_rows = seq_count * rows
-    block = all_rows // ranks
-    part = jax.ShapeDtypeStruct((block, 2 * dim), F32)
 
     def run_prefix(*refs):
-        prefix_kernel(shape, refs[:heads], refs[heads : heads + ranks], *refs[heads + ranks :])
-
-    parts = call(
+        prefix_kernel(shape, refs[:heads], *refs[heads:])
+
+    part = call(
         run_prefix,
-        [part] * ranks,
+        jax.ShapeDtypeStruct((all_rows, 2 * dim), F32),
         [vmem] * heads,
-        [
-            pltpu.VMEM((all_rows, dim), BF16),
-            pltpu.VMEM((all_rows, 2 * dim), F32),
-            pltpu.VMEM((all_rows, 2 * dim), F32),
-        ],
+        [pltpu.VMEM((all_rows, dim), BF16), pltpu.VMEM((all_rows, 2 * dim), F32)],
     )(*messages)
-    parts = [parts[0]] + [swap(parts[y], "seq", y) for y in range(1, ranks)]
+    parts = [part] + [swap(part, "seq", y) for y in range(1, ranks)]
 
     def run_merge(*refs):
-        merge_kernel(group, refs[:ranks], *refs[ranks:])
-
-    count = block // group
-    head_out = call(
+        merge_kernel(group, ranks, refs[:ranks], refs[ranks : ranks + 2], refs[ranks + 2])
+
+    count = all_rows // (ranks * group)
+    staying, leaving = call(
         run_merge,
-        jax.ShapeDtypeStruct((count, group * dim), BF16),
+        [jax.ShapeDtypeStruct((count, group * dim), BF16)] * 2,
         [vmem] * ranks,
-        [pltpu.VMEM((block, dim), F32)],
+        [pltpu.VMEM((all_rows, dim), F32)],
     )(*parts)
-    head_outs = [head_out] + [swap(head_out, "prompt", x) for x in range(1, prompt_count)]
+    flip = 1 if ranks > 1 else 0
+    head_outs = [staying] + [
+        cross(leaving, lambda p, s, x=x: (p ^ x, s ^ flip)) for x in range(1, prompt_count)
+    ]
 
     def run_project(*refs):
         n, m = prompt_count, prompt_count + ranks
@@ -538,7 +552,7 @@
     )(*head_outs, weight, *other_weights)
     result = terms[0]
     for x in reversed(range(1, heads)):
-        result = result + swap(terms[x], "seq", x * ranks).astype(F32)
+        result = result + swap(terms[x], "seq", x * ranks + flip).astype(F32)
     return result.astype(BF16)
 
 

time: 33.5 us -> 31.9 us (0.952)
  waiting for transfers between devices: 14 us -> 13.1 us
  starting transfers between devices: 13.1 us -> 12.3 us
    ppermute x12 -> x9, starting transfers between devices: 13.1 us -> 8.28 us  [swap(): lax.ppermute(x, axis, [(i, i ^ distance) for i in range(lax.axis_size(axi...]
    ppermute x0 -> x3, starting transfers between devices: none -> 4.03 us  [cross(): return lax.ppermute(x, ('prompt', 'seq'), pairs)]
    ppermute x12 -> x9, waiting for transfers between devices: 14 us -> 11.3 us  [swap(): lax.ppermute(x, axis, [(i, i ^ distance) for i in range(lax.axis_size(axi...]
    ppermute x0 -> x3, waiting for transfers between devices: none -> 1.85 us  [cross(): return lax.ppermute(x, ('prompt', 'seq'), pairs)]
  transfers between devices with their start and end apart: 12 -> 12, of which waited for: 7 -> 7; matrix products, arithmetic and copies ran while one was open for 0% -> 0% of each run, Pallas kernels for 12% -> 13%
where the time goes in v4:
time: 31.9 us; the launch traced here: 31.7 us
  waiting for transfers between devices  13.1 us (41%)
  starting transfers between devices  12.3 us (39%)
  Pallas kernels  4.88 us (15%)
  between operations  0.72 us (2%)
  other arithmetic  0.64 us (2%)
    ppermute x9, waiting for transfers between devices, swap(): lax.ppermute(x, axis, [(i, i ^ distance) for i in range(lax.axis_size(axi...  11.3 us
    ppermute x9, starting transfers between devices, swap(): lax.ppermute(x, axis, [(i, i ^ distance) for i in range(lax.axis_size(axi...  8.28 us
    ppermute x3, starting transfers between devices, cross(): return lax.ppermute(x, ('prompt', 'seq'), pairs)  4.03 us
    ppermute x3, waiting for transfers between devices, cross(): return lax.ppermute(x, ('prompt', 'seq'), pairs)  1.85 us
    pallas_call x1, Pallas kernels, on_device(): call(run_message, [message] * heads, [hbm] * len(sources), [(pltpu.SMEM i...  1.62 us
    pallas_call x1, Pallas kernels, on_device(): call(fetch_kernel, jax.ShapeDtypeStruct(out_weight.shape, BF16), [pl.Bloc...  1.6 us
    pallas_call x1, Pallas kernels, on_device(): call(run_project, [jax.ShapeDtypeStruct((count, out_weight.shape[1]), BF1...  0.82 us
  transfers between devices with their start and end apart: 12, of which 7 were waited for; matrix products, arithmetic and copies ran while one was open for 0% of the time, Pallas kernels for 13%

profile of v4, /device:TPU:0, one launch (start us, length us, event | category | flops | bytes accessed | tf_op | source)
XLA Modules:
  0.0 31.7 jit_solution(387925186097304003)
XLA Ops:
  0.0 0.5 %collective-permute-start = (bf16[64,128]{1,0:T(8,128)(2,1)}, bf16[64,128]{1,0:T(8,128)(2,1)S(1)}, u32[]{:S(2)}, u32[]{:S(2)}) collective-permute-start(bf16[64,128]{1,0:T(8,128)(2,1)} %bitcast.14), channel_id=1, source_target_pairs={{0,1},{1,0},{2,3},{3,2},{4,5},{5,4},{6,7},{7,6},{8,9},{9,8},{10,11... | collective-permute-start | bytes 49160 | tf_op jit(solution)/shard_map/ppermute | solution.py:255
  1.1 1.6 %shard_map.100 = (bf16[592,128]{1,0:T(8,128)(2,1)S(1)}, bf16[592,128]{1,0:T(8,128)(2,1)S(1)}, bf16[592,128]{1,0:T(8,128)(2,1)S(1)}, bf16[592,128]{1,0:T(8,128)(2,1)S(1)}) custom-call(bf16[4,256,128]{2,1,0:T(8,128)(2,1)} %bitcast.10, bf16[4,256,128]{2,1,0:T(8,128)(2,1)} %bitcast.11, bf16[64,128]{1,0:T(8,128)(2,1)} %bitcast.15, bf16[4,256,128]{2,1,0:T(8,128)(2,1)} %bitcast.12, ...), custom_call_target="tpu_custom_call" | custom-call | tf_op jit(solution)/shard_map/pallas_call | solution.py:476
  2.7 0.0 collective-permute-done.refs_0_
  2.8 0.1 collective-permute-start.8
  2.9 2.9 %collective-permute-start.1 = (bf16[592,128]{1,0:T(8,128)(2,1)S(1)}, bf16[592,128]{1,0:T(8,128)(2,1)S(1)}, u32[]{:S(2)}, u32[]{:S(2)}) collective-permute-start(bf16[592,128]{1,0:T(8,128)(2,1)S(1)} %get-tuple-element.33), channel_id=1, source_target_pairs={{0,2},{1,3},{2,0},{3,1},{4,6},{5,7},{6,4},{7,5},{8,10},{9,11},{10,... | collective-permute-start | bytes 454664 | tf_op jit(solution)/shard_map/ppermute | solution.py:255
  5.8 1.5 %collective-permute-start.2 = (bf16[592,128]{1,0:T(8,128)(2,1)S(1)}, bf16[592,128]{1,0:T(8,128)(2,1)S(1)}, u32[]{:S(2)}, u32[]{:S(2)}) collective-permute-start(bf16[592,128]{1,0:T(8,128)(2,1)S(1)} %get-tuple-element.34), channel_id=1, source_target_pairs={{0,4},{1,5},{2,6},{3,7},{4,0},{5,1},{6,2},{7,3},{8,12},{9,13},{10,... | collective-permute-start | bytes 454664 | tf_op jit(solution)/shard_map/ppermute | solution.py:255
  7.4 0.0 collective-permute-start.3
  7.4 3.2 %collective-permute-done.1.refs_1_ = bf16[592,128]{1,0:T(8,128)(2,1)S(1)} collective-permute-done((bf16[592,128]{1,0:T(8,128)(2,1)S(1)}, bf16[592,128]{1,0:T(8,128)(2,1)S(1)}, u32[]{:S(2)}, u32[]{:S(2)}) %collective-permute-start.1) | collective-permute-done | bytes 151584 | tf_op jit(solution)/shard_map/ppermute | solution.py:255
  10.6 4.2 %collective-permute-done.2.refs_2_ = bf16[592,128]{1,0:T(8,128)(2,1)S(1)} collective-permute-done((bf16[592,128]{1,0:T(8,128)(2,1)S(1)}, bf16[592,128]{1,0:T(8,128)(2,1)S(1)}, u32[]{:S(2)}, u32[]{:S(2)}) %collective-permute-start.2) | collective-permute-done | bytes 151584 | tf_op jit(solution)/shard_map/ppermute | solution.py:255
  14.7 0.0 collective-permute-done.3.refs_3_
  14.7 0.6 %shard_map.102.refs_0_ = f32[128,256]{1,0:T(8,128)S(1)} custom-call(bf16[592,128]{1,0:T(8,128)(2,1)S(1)} %get-tuple-element.32.refs_0_.after_ref, bf16[592,128]{1,0:T(8,128)(2,1)S(1)} %collective-permute-done.1.refs_1_, bf16[592,128]{1,0:T(8,128)(2,1)S(1)} %collective-permute-done.2.refs_2_, bf16[592,128]{1,0:T(8,128)(2,1)S(1)} %collective-permute-done.3.refs_3_), custom_call_target="tpu_custom_call" | custom-call | tf_op jit(solution)/shard_map/pallas_call | solution.py:517
  15.3 0.1 collective-permute-start.4
  15.4 1.3 %collective-permute-done.4.refs_1_ = f32[128,256]{1,0:T(8,128)S(1)} collective-permute-done((f32[128,256]{1,0:T(8,128)S(1)}, f32[128,256]{1,0:T(8,128)S(1)}, u32[]{:S(2)}, u32[]{:S(2)}) %collective-permute-start.4) | collective-permute-done | bytes 131104 | tf_op jit(solution)/shard_map/ppermute | solution.py:255
  16.7 0.2 shard_map.103
  17.0 3.4 %collective-permute-start.7 = (bf16[8,1024]{1,0:T(8,128)(2,1)S(1)}, bf16[8,1024]{1,0:T(8,128)(2,1)S(1)}, u32[]{:S(2)}, u32[]{:S(2)}) collective-permute-start(bf16[8,1024]{1,0:T(8,128)(2,1)S(1)} %get-tuple-element.37), channel_id=1, source_target_pairs={{0,25},{1,24},{2,27},{3,26},{4,29},{5,28},{6,31},{7,30},{8,17},{9,... | collective-permute-start | bytes 49160 | tf_op jit(solution)/shard_map/ppermute | solution.py:428
  20.4 0.0 collective-permute-start.6
  20.4 0.6 %collective-permute-start.5 = (bf16[8,1024]{1,0:T(8,128)(2,1)S(1)}, bf16[8,1024]{1,0:T(8,128)(2,1)S(1)}, u32[]{:S(2)}, u32[]{:S(2)}) collective-permute-start(bf16[8,1024]{1,0:T(8,128)(2,1)S(1)} %get-tuple-element.37), channel_id=1, source_target_pairs={{0,9},{1,8},{2,11},{3,10},{4,13},{5,12},{6,15},{7,14},{8,1},{9,0},... | collective-permute-start | bytes 49160 | tf_op jit(solution)/shard_map/ppermute | solution.py:428
  21.0 1.6 %shard_map.104.refs_4_ = bf16[512,2048]{1,0:T(8,128)(2,1)S(1)} custom-call(bf16[592,128]{1,0:T(8,128)(2,1)S(1)} %get-tuple-element.32.refs_0_.after_ref, bf16[512,2048]{1,0:T(8,128)(2,1)} %weight_ref.1), custom_call_target="tpu_custom_call" | custom-call | tf_op jit(solution)/shard_map/pallas_call | solution.py:504
  22.6 0.0 collective-permute-done.7.refs_3_
  22.6 1.8 %collective-permute-done.6.refs_2_ = bf16[8,1024]{1,0:T(8,128)(2,1)S(1)} collective-permute-done((bf16[8,1024]{1,0:T(8,128)(2,1)S(1)}, bf16[8,1024]{1,0:T(8,128)(2,1)S(1)}, u32[]{:S(2)}, u32[]{:S(2)}) %collective-permute-start.6) | collective-permute-done | bytes 16416 | tf_op jit(solution)/shard_map/ppermute | solution.py:428
  24.5 0.0 collective-permute-done.5.refs_1_
  24.5 0.0 collective-permute-done.8.refs_5_
  24.5 0.8 %shard_map.105 = (f32[8,2048]{1,0:T(8,128)S(1)}, bf16[8,2048]{1,0:T(8,128)(2,1)S(1)}, bf16[8,2048]{1,0:T(8,128)(2,1)S(1)}, bf16[8,2048]{1,0:T(8,128)(2,1)S(1)}) custom-call(bf16[8,1024]{1,0:T(8,128)(2,1)S(1)} %get-tuple-element.36.refs_0_, bf16[8,1024]{1,0:T(8,128)(2,1)S(1)} %collective-permute-done.5.refs_1_, ...), custom_call_target="tpu_custom_call" | custom-call | tf_op jit(solution)/shard_map/pallas_call | solution.py:544
  25.3 1.5 %collective-permute-start.9 = (bf16[8,2048]{1,0:T(8,128)(2,1)S(1)}, bf16[8,2048]{1,0:T(8,128)(2,1)S(1)}, u32[]{:S(2)}, u32[]{:S(2)}) collective-permute-start(bf16[8,2048]{1,0:T(8,128)(2,1)S(1)} %get-tuple-element.40), channel_id=1, source_target_pairs={{0,7},{1,6},{2,5},{3,4},{4,3},{5,2},{6,1},{7,0},{8,15},{9,14},{10,... | collective-permute-start | bytes 98312 | tf_op jit(solution)/shard_map/ppermute | solution.py:255
  26.7 1.0 %collective-permute-start.10 = (bf16[8,2048]{1,0:T(8,128)(2,1)S(1)}, bf16[8,2048]{1,0:T(8,128)(2,1)S(1)}, u32[]{:S(2)}, u32[]{:S(2)}) collective-permute-start(bf16[8,2048]{1,0:T(8,128)(2,1)S(1)} %get-tuple-element.41), channel_id=1, source_target_pairs={{0,5},{1,4},{2,7},{3,6},{4,1},{5,0},{6,3},{7,2},{8,13},{9,12},{10,... | collective-permute-start | bytes 98312 | tf_op jit(solution)/shard_map/ppermute | solution.py:255
  27.7 0.7 %collective-permute-start.11 = (bf16[8,2048]{1,0:T(8,128)(2,1)S(1)}, bf16[8,2048]{1,0:T(8,128)(2,1)S(1)}, u32[]{:S(2)}, u32[]{:S(2)}) collective-permute-start(bf16[8,2048]{1,0:T(8,128)(2,1)S(1)} %get-tuple-element.42), channel_id=1, source_target_pairs={{0,3},{1,2},{2,1},{3,0},{4,7},{5,6},{6,5},{7,4},{8,11},{9,10},{10,... | collective-permute-start | bytes 98312 | tf_op jit(solution)/shard_map/ppermute | solution.py:255
  28.5 1.1 %collective-permute-done.9 = bf16[8,2048]{1,0:T(8,128)(2,1)S(1)} collective-permute-done((bf16[8,2048]{1,0:T(8,128)(2,1)S(1)}, bf16[8,2048]{1,0:T(8,128)(2,1)S(1)}, u32[]{:S(2)}, u32[]{:S(2)}) %collective-permute-start.9) | collective-permute-done | bytes 32800 | tf_op jit(solution)/shard_map/ppermute | solution.py:255
  29.5 1.2 %collective-permute-done.10 = bf16[8,2048]{1,0:T(8,128)(2,1)S(1)} collective-permute-done((bf16[8,2048]{1,0:T(8,128)(2,1)S(1)}, bf16[8,2048]{1,0:T(8,128)(2,1)S(1)}, u32[]{:S(2)}, u32[]{:S(2)}) %collective-permute-start.10) | collective-permute-done | bytes 32800 | tf_op jit(solution)/shard_map/ppermute | solution.py:255
  30.7 0.3 %collective-permute-done.11 = bf16[8,2048]{1,0:T(8,128)(2,1)S(1)} collective-permute-done((bf16[8,2048]{1,0:T(8,128)(2,1)S(1)}, bf16[8,2048]{1,0:T(8,128)(2,1)S(1)}, u32[]{:S(2)}, u32[]{:S(2)}) %collective-permute-start.11) | collective-permute-done | bytes 32800 | tf_op jit(solution)/shard_map/ppermute | solution.py:255
  31.1 0.6 %add_convert_fusion = bf16[8,2048]{1,0:T(8,128)(2,1)} fusion(bf16[8,2048]{1,0:T(8,128)(2,1)S(1)} %collective-permute-done.11, bf16[8,2048]{1,0:T(8,128)(2,1)S(1)} %collective-permute-done.10, f32[8,2048]{1,0:T(8,128)S(1)} %get-tuple-element.39, bf16[8,2048]{1,0:T(8,128)(2,1)S(1)} %collective-permute-done.9), kind=kLoop, calls=%fused_computation | loop fusion | flops 114688 | bytes 196608 | tf_op jit(solution)/shard_map/convert_element_type | solution.py:556
  (1 shorter events, 0.0 us)
Async XLA Ops:
  0.0 2.7 %collective-permute-start = (bf16[64,128]{1,0:T(8,128)(2,1)}, bf16[64,128]{1,0:T(8,128)(2,1)S(1)}, u32[]{:S(2)}, u32[]{:S(2)}) collective-permute-start(bf16[64,128]{1,0:T(8,128)(2,1)} %bitcast.14), channel_id=1, source_target_pairs={{0,1},{1,0},{2,3},{3,2},{4,5},{5,4},{6,7},{7,6},{8,9},{9,8},{10,11... | collective-permute-start | bytes 49160 | tf_op jit(solution)/shard_map/ppermute | solution.py:255
  2.8 21.7 %collective-permute-start.8 = (bf16[512,2048]{1,0:T(8,128)(2,1)}, bf16[512,2048]{1,0:T(8,128)(2,1)S(1)}, u32[]{:S(2)}, u32[]{:S(2)}) collective-permute-start(bf16[512,2048]{1,0:T(8,128)(2,1)} %weight_ref.1), channel_id=1, source_target_pairs={{0,1},{1,0},{2,3},{3,2},{4,5},{5,4},{6,7},{7,6},{8,9},{9,8},{10,11... | collective-permute-start | bytes 6291464 | tf_op jit(solution)/shard_map/ppermute | solution.py:255
  2.9 7.7 %collective-permute-start.1 = (bf16[592,128]{1,0:T(8,128)(2,1)S(1)}, bf16[592,128]{1,0:T(8,128)(2,1)S(1)}, u32[]{:S(2)}, u32[]{:S(2)}) collective-permute-start(bf16[592,128]{1,0:T(8,128)(2,1)S(1)} %get-tuple-element.33), channel_id=1, source_target_pairs={{0,2},{1,3},{2,0},{3,1},{4,6},{5,7},{6,4},{7,5},{8,10},{9,11},{10,... | collective-permute-start | bytes 454664 | tf_op jit(solution)/shard_map/ppermute | solution.py:255
  5.8 8.9 %collective-permute-start.2 = (bf16[592,128]{1,0:T(8,128)(2,1)S(1)}, bf16[592,128]{1,0:T(8,128)(2,1)S(1)}, u32[]{:S(2)}, u32[]{:S(2)}) collective-permute-start(bf16[592,128]{1,0:T(8,128)(2,1)S(1)} %get-tuple-element.34), channel_id=1, source_target_pairs={{0,4},{1,5},{2,6},{3,7},{4,0},{5,1},{6,2},{7,3},{8,12},{9,13},{10,... | collective-permute-start | bytes 454664 | tf_op jit(solution)/shard_map/ppermute | solution.py:255
  7.4 7.4 %collective-permute-start.3 = (bf16[592,128]{1,0:T(8,128)(2,1)S(1)}, bf16[592,128]{1,0:T(8,128)(2,1)S(1)}, u32[]{:S(2)}, u32[]{:S(2)}) collective-permute-start(bf16[592,128]{1,0:T(8,128)(2,1)S(1)} %get-tuple-element.35), channel_id=1, source_target_pairs={{0,6},{1,7},{2,4},{3,5},{4,2},{5,3},{6,0},{7,1},{8,14},{9,15},{10,... | collective-permute-start | bytes 454664 | tf_op jit(solution)/shard_map/ppermute | solution.py:255
  15.3 1.4 %collective-permute-start.4 = (f32[128,256]{1,0:T(8,128)S(1)}, f32[128,256]{1,0:T(8,128)S(1)}, u32[]{:S(2)}, u32[]{:S(2)}) collective-permute-start(f32[128,256]{1,0:T(8,128)S(1)} %shard_map.102.refs_0_), channel_id=1, source_target_pairs={{0,1},{1,0},{2,3},{3,2},{4,5},{5,4},{6,7},{7,6},{8,9},{9,8},{10,11... | collective-permute-start | bytes 393224 | tf_op jit(solution)/shard_map/ppermute | solution.py:255
  17.0 5.6 %collective-permute-start.7 = (bf16[8,1024]{1,0:T(8,128)(2,1)S(1)}, bf16[8,1024]{1,0:T(8,128)(2,1)S(1)}, u32[]{:S(2)}, u32[]{:S(2)}) collective-permute-start(bf16[8,1024]{1,0:T(8,128)(2,1)S(1)} %get-tuple-element.37), channel_id=1, source_target_pairs={{0,25},{1,24},{2,27},{3,26},{4,29},{5,28},{6,31},{7,30},{8,17},{9,... | collective-permute-start | bytes 49160 | tf_op jit(solution)/shard_map/ppermute | solution.py:428
  20.4 4.1 %collective-permute-start.6 = (bf16[8,1024]{1,0:T(8,128)(2,1)S(1)}, bf16[8,1024]{1,0:T(8,128)(2,1)S(1)}, u32[]{:S(2)}, u32[]{:S(2)}) collective-permute-start(bf16[8,1024]{1,0:T(8,128)(2,1)S(1)} %get-tuple-element.37), channel_id=1, source_target_pairs={{0,17},{1,16},{2,19},{3,18},{4,21},{5,20},{6,23},{7,22},{8,25},{9,... | collective-permute-start | bytes 49160 | tf_op jit(solution)/shard_map/ppermute | solution.py:428
  20.4 4.1 %collective-permute-start.5 = (bf16[8,1024]{1,0:T(8,128)(2,1)S(1)}, bf16[8,1024]{1,0:T(8,128)(2,1)S(1)}, u32[]{:S(2)}, u32[]{:S(2)}) collective-permute-start(bf16[8,1024]{1,0:T(8,128)(2,1)S(1)} %get-tuple-element.37), channel_id=1, source_target_pairs={{0,9},{1,8},{2,11},{3,10},{4,13},{5,12},{6,15},{7,14},{8,1},{9,0},... | collective-permute-start | bytes 49160 | tf_op jit(solution)/shard_map/ppermute | solution.py:428
  25.3 4.3 %collective-permute-start.9 = (bf16[8,2048]{1,0:T(8,128)(2,1)S(1)}, bf16[8,2048]{1,0:T(8,128)(2,1)S(1)}, u32[]{:S(2)}, u32[]{:S(2)}) collective-permute-start(bf16[8,2048]{1,0:T(8,128)(2,1)S(1)} %get-tuple-element.40), channel_id=1, source_target_pairs={{0,7},{1,6},{2,5},{3,4},{4,3},{5,2},{6,1},{7,0},{8,15},{9,14},{10,... | collective-permute-start | bytes 98312 | tf_op jit(solution)/shard_map/ppermute | solution.py:255
  26.7 4.0 %collective-permute-start.10 = (bf16[8,2048]{1,0:T(8,128)(2,1)S(1)}, bf16[8,2048]{1,0:T(8,128)(2,1)S(1)}, u32[]{:S(2)}, u32[]{:S(2)}) collective-permute-start(bf16[8,2048]{1,0:T(8,128)(2,1)S(1)} %get-tuple-element.41), channel_id=1, source_target_pairs={{0,5},{1,4},{2,7},{3,6},{4,1},{5,0},{6,3},{7,2},{8,13},{9,12},{10,... | collective-permute-start | bytes 98312 | tf_op jit(solution)/shard_map/ppermute | solution.py:255
  27.7 3.3 %collective-permute-start.11 = (bf16[8,2048]{1,0:T(8,128)(2,1)S(1)}, bf16[8,2048]{1,0:T(8,128)(2,1)S(1)}, u32[]{:S(2)}, u32[]{:S(2)}) collective-permute-start(bf16[8,2048]{1,0:T(8,128)(2,1)S(1)} %get-tuple-element.42), channel_id=1, source_target_pairs={{0,3},{1,2},{2,1},{3,0},{4,7},{5,6},{6,5},{7,4},{8,11},{9,10},{10,... | collective-permute-start | bytes 98312 | tf_op jit(solution)/shard_map/ppermute | solution.py:255

commit v5 on v4

--- a/solution.py
+++ b/solution.py
@@ -14,15 +14,23 @@
 F32 = jnp.float32
 BF16 = jnp.bfloat16
 VMEM_LIMIT = 16 * 1024 * 1024
-MAX_LANE, SUM_LANE, SUM_REST_LANE, KEPT_LANE = 0, 1, 2, 3
+MAX_LANE, SUM_LANE = 0, 1
 
 
 def lanes_of(rows, width, values):
     lane = lax.broadcasted_iota(jnp.int32, (rows, width), 1)
     filled = jnp.zeros((rows, width), F32)
     for i, value in enumerate(values):
-        filled = jnp.where(lane == i, value, filled)
+        filled = jnp.where(lane == i, jnp.asarray(value, F32), filled)
     return filled
+
+
+def in_pieces(x, count):
+    pieces = []
+    for _ in range(count):
+        pieces.append(x.astype(BF16))
+        x = x - pieces[-1].astype(F32)
+    return pieces
 
 
 def dot_rows(a, b):
@@ -81,7 +89,6 @@
         score = jnp.sum(q * spread(step_keys[u]), axis=1, keepdims=True) * scale
         own.append(jnp.where(step_of_row >= u, score, NEGATIVE))
     top = functools.reduce(jnp.maximum, own, jnp.max(scores, axis=1, keepdims=True))
-    top = top.astype(BF16).astype(F32)
     weights = jnp.exp(scores - top)
     total = jnp.sum(weights, axis=1, keepdims=True)
     summed = jnp.concatenate(
@@ -95,11 +102,9 @@
         weight = jnp.exp(score - top)
         total = total + weight
         summed = summed + weight.astype(BF16).astype(F32) * spread(step_values[u])
-    summed_high = summed.astype(BF16)
-    summed_rest = (summed - summed_high.astype(F32)).astype(BF16)
-    total_high = total.astype(BF16).astype(F32)
+    summed_high, summed_rest = in_pieces(summed, 2)
     kept = jnp.concatenate([jnp.full((rows, 1), kept_ref[h].astype(F32)) for h in range(heads)], axis=0)
-    stats = lanes_of(all_rows, dim, [top, total_high, total - total_high, kept]).astype(BF16)
+    stats = lanes_of(all_rows, dim, [*in_pieces(top, 3), *in_pieces(total, 3), kept]).astype(BF16)
     for i, part in enumerate([summed_high, summed_rest, stats, q_narrow]):
         for h, piece in enumerate(by_head(part)):
             small[h, i * rows : (i + 1) * rows, :] = piece
@@ -161,11 +166,10 @@
             row = pl.multiple_of((base + (rank ^ y)) * rows, rows)
             q_all[pl.ds(row, rows), :] = message_refs[x][start + y * rows : start + (y + 1) * rows, :]
         tails[pl.ds(place, rows), 0:dim] = high + rest
-        total = stats[:, SUM_LANE : SUM_LANE + 1] + stats[:, SUM_REST_LANE : SUM_REST_LANE + 1]
-        tails[pl.ds(place, rows), dim:] = lanes_of(
-            rows, dim, [stats[:, MAX_LANE : MAX_LANE + 1], total]
-        )
-        kept.append(stats[0:1, KEPT_LANE : KEPT_LANE + 1])
+        tail_top = stats[:, 0:1] + stats[:, 1:2] + stats[:, 2:3]
+        total = stats[:, 3:4] + stats[:, 4:5] + stats[:, 5:6]
+        tails[pl.ds(place, rows), dim:] = lanes_of(rows, dim, [tail_top, total])
+        kept.append(stats[0:1, 6:7])
     block = lax.div(lax.broadcasted_iota(jnp.int32, (1, chunk), 1), BLOCK_TOKENS).astype(F32)
     q = q_all[...]
     tail_top = tails[:, dim + MAX_LANE : dim + MAX_LANE + 1]
@@ -512,14 +516,14 @@
     all_rows = seq_count * rows
 
     def run_prefix(*refs):
-        prefix_kernel(shape, refs[:heads], *refs[heads:])
+        prefix_kernel(shape, refs[:heads], *refs[heads + 1 :])
 
     part = call(
         run_prefix,
         jax.ShapeDtypeStruct((all_rows, 2 * dim), F32),
-        [vmem] * heads,
+        [vmem] * heads + [pl.BlockSpec(memory_space=pl.ANY)],
         [pltpu.VMEM((all_rows, dim), BF16), pltpu.VMEM((all_rows, 2 * dim), F32)],
-    )(*messages)
+    )(*messages, weight)
     parts = [part] + [swap(part, "seq", y) for y in range(1, ranks)]
 
     def run_merge(*refs):

time: 31.9 us -> 32 us (level)
    ppermute x3, waiting for transfers between devices: 1.85 us -> 3.46 us  [cross(): return lax.ppermute(x, ('prompt', 'seq'), pairs)]
    ppermute x9, waiting for transfers between devices: 11.3 us -> 9.69 us  [swap(): lax.ppermute(x, axis, [(i, i ^ distance) for i in range(lax.axis_size(axi...]
  transfers between devices with their start and end apart: 12 -> 12, of which waited for: 7 -> 8; matrix products, arithmetic and copies ran while one was open for 0% -> 0% of each run, Pallas kernels for 13% -> 13%
where the time goes in v5:
time: 32 us; the launch traced here: 31.7 us
  waiting for transfers between devices  13.2 us (41%)
  starting transfers between devices  12.3 us (38%)
  Pallas kernels  4.92 us (15%)
  between operations  0.71 us (2%)
  other arithmetic  0.64 us (2%)
    ppermute x9, waiting for transfers between devices, swap(): lax.ppermute(x, axis, [(i, i ^ distance) for i in range(lax.axis_size(axi...  9.69 us
    ppermute x9, starting transfers between devices, swap(): lax.ppermute(x, axis, [(i, i ^ distance) for i in range(lax.axis_size(axi...  8.29 us
    ppermute x3, starting transfers between devices, cross(): return lax.ppermute(x, ('prompt', 'seq'), pairs)  4.04 us
    ppermute x3, waiting for transfers between devices, cross(): return lax.ppermute(x, ('prompt', 'seq'), pairs)  3.46 us
    pallas_call x1, Pallas kernels, on_device(): call(run_message, [message] * heads, [hbm] * len(sources), [(pltpu.SMEM i...  1.62 us
    pallas_call x1, Pallas kernels, on_device(): call(fetch_kernel, jax.ShapeDtypeStruct(out_weight.shape, BF16), [pl.Bloc...  1.6 us
    pallas_call x1, Pallas kernels, on_device(): call(run_project, [jax.ShapeDtypeStruct((count, out_weight.shape[1]), BF1...  0.82 us
    pallas_call x1, Pallas kernels, on_device(): call(run_prefix, jax.ShapeDtypeStruct((all_rows, 2 * dim), F32), [vmem] *...  0.65 us
  transfers between devices with their start and end apart: 12, of which 8 were waited for; matrix products, arithmetic and copies ran while one was open for 0% of the time, Pallas kernels for 13%

profile of v5, /device:TPU:0, one launch (start us, length us, event | category | flops | bytes accessed | tf_op | source)
XLA Modules:
  0.0 31.7 jit_solution(6833334237938418771)
XLA Ops:
  0.0 0.5 %collective-permute-start = (bf16[64,128]{1,0:T(8,128)(2,1)}, bf16[64,128]{1,0:T(8,128)(2,1)S(1)}, u32[]{:S(2)}, u32[]{:S(2)}) collective-permute-start(bf16[64,128]{1,0:T(8,128)(2,1)} %bitcast.14), channel_id=1, source_target_pairs={{0,1},{1,0},{2,3},{3,2},{4,5},{5,4},{6,7},{7,6},{8,9},{9,8},{10,11... | collective-permute-start | bytes 49160 | tf_op jit(solution)/shard_map/ppermute | solution.py:259
  1.1 1.6 %shard_map.100 = (bf16[592,128]{1,0:T(8,128)(2,1)S(1)}, bf16[592,128]{1,0:T(8,128)(2,1)S(1)}, bf16[592,128]{1,0:T(8,128)(2,1)S(1)}, bf16[592,128]{1,0:T(8,128)(2,1)S(1)}) custom-call(bf16[4,256,128]{2,1,0:T(8,128)(2,1)} %bitcast.10, bf16[4,256,128]{2,1,0:T(8,128)(2,1)} %bitcast.11, bf16[64,128]{1,0:T(8,128)(2,1)} %bitcast.15, bf16[4,256,128]{2,1,0:T(8,128)(2,1)} %bitcast.12, ...), custom_call_target="tpu_custom_call" | custom-call | tf_op jit(solution)/shard_map/pallas_call | solution.py:480
  2.7 0.0 collective-permute-done.refs_0_
  2.8 0.1 collective-permute-start.8
  2.9 2.9 %collective-permute-start.1 = (bf16[592,128]{1,0:T(8,128)(2,1)S(1)}, bf16[592,128]{1,0:T(8,128)(2,1)S(1)}, u32[]{:S(2)}, u32[]{:S(2)}) collective-permute-start(bf16[592,128]{1,0:T(8,128)(2,1)S(1)} %get-tuple-element.33), channel_id=1, source_target_pairs={{0,2},{1,3},{2,0},{3,1},{4,6},{5,7},{6,4},{7,5},{8,10},{9,11},{10,... | collective-permute-start | bytes 454664 | tf_op jit(solution)/shard_map/ppermute | solution.py:259
  5.8 1.5 %collective-permute-start.2 = (bf16[592,128]{1,0:T(8,128)(2,1)S(1)}, bf16[592,128]{1,0:T(8,128)(2,1)S(1)}, u32[]{:S(2)}, u32[]{:S(2)}) collective-permute-start(bf16[592,128]{1,0:T(8,128)(2,1)S(1)} %get-tuple-element.34), channel_id=1, source_target_pairs={{0,4},{1,5},{2,6},{3,7},{4,0},{5,1},{6,2},{7,3},{8,12},{9,13},{10,... | collective-permute-start | bytes 454664 | tf_op jit(solution)/shard_map/ppermute | solution.py:259
  7.4 0.0 collective-permute-start.3
  7.4 1.6 %shard_map.102.refs_4_ = bf16[512,2048]{1,0:T(8,128)(2,1)S(1)} custom-call(bf16[592,128]{1,0:T(8,128)(2,1)S(1)} %get-tuple-element.32.after_ref.refs_0_, bf16[512,2048]{1,0:T(8,128)(2,1)} %weight_ref.1), custom_call_target="tpu_custom_call" | custom-call | tf_op jit(solution)/shard_map/pallas_call | solution.py:508
  9.0 1.6 %collective-permute-done.1.refs_1_ = bf16[592,128]{1,0:T(8,128)(2,1)S(1)} collective-permute-done((bf16[592,128]{1,0:T(8,128)(2,1)S(1)}, bf16[592,128]{1,0:T(8,128)(2,1)S(1)}, u32[]{:S(2)}, u32[]{:S(2)}) %collective-permute-start.1) | collective-permute-done | bytes 151584 | tf_op jit(solution)/shard_map/ppermute | solution.py:259
  10.6 4.2 %collective-permute-done.2.refs_2_ = bf16[592,128]{1,0:T(8,128)(2,1)S(1)} collective-permute-done((bf16[592,128]{1,0:T(8,128)(2,1)S(1)}, bf16[592,128]{1,0:T(8,128)(2,1)S(1)}, u32[]{:S(2)}, u32[]{:S(2)}) %collective-permute-start.2) | collective-permute-done | bytes 151584 | tf_op jit(solution)/shard_map/ppermute | solution.py:259
  14.7 0.0 collective-permute-done.3.refs_3_
  14.7 0.6 %shard_map.103.refs_0_ = f32[128,256]{1,0:T(8,128)S(1)} custom-call(bf16[592,128]{1,0:T(8,128)(2,1)S(1)} %get-tuple-element.32.after_ref.refs_0_, bf16[592,128]{1,0:T(8,128)(2,1)S(1)} %collective-permute-done.1.refs_1_, bf16[592,128]{1,0:T(8,128)(2,1)S(1)} %collective-permute-done.2.refs_2_, bf16[592,128]{1,0:T(8,128)(2,1)S(1)} %collective-permute-done.3.refs_3_, ...), custom_call_target="tpu_custom_call" | custom-call | tf_op jit(solution)/shard_map/pallas_call | solution.py:521
  15.4 0.1 collective-permute-start.4
  15.4 1.3 %collective-permute-done.4.refs_1_ = f32[128,256]{1,0:T(8,128)S(1)} collective-permute-done((f32[128,256]{1,0:T(8,128)S(1)}, f32[128,256]{1,0:T(8,128)S(1)}, u32[]{:S(2)}, u32[]{:S(2)}) %collective-permute-start.4) | collective-permute-done | bytes 131104 | tf_op jit(solution)/shard_map/ppermute | solution.py:259
  16.8 0.2 shard_map.104
  17.0 3.4 %collective-permute-start.7 = (bf16[8,1024]{1,0:T(8,128)(2,1)S(1)}, bf16[8,1024]{1,0:T(8,128)(2,1)S(1)}, u32[]{:S(2)}, u32[]{:S(2)}) collective-permute-start(bf16[8,1024]{1,0:T(8,128)(2,1)S(1)} %get-tuple-element.37), channel_id=1, source_target_pairs={{0,25},{1,24},{2,27},{3,26},{4,29},{5,28},{6,31},{7,30},{8,17},{9,... | collective-permute-start | bytes 49160 | tf_op jit(solution)/shard_map/ppermute | solution.py:432
  20.4 0.0 collective-permute-start.6
  20.4 0.6 %collective-permute-start.5 = (bf16[8,1024]{1,0:T(8,128)(2,1)S(1)}, bf16[8,1024]{1,0:T(8,128)(2,1)S(1)}, u32[]{:S(2)}, u32[]{:S(2)}) collective-permute-start(bf16[8,1024]{1,0:T(8,128)(2,1)S(1)} %get-tuple-element.37), channel_id=1, source_target_pairs={{0,9},{1,8},{2,11},{3,10},{4,13},{5,12},{6,15},{7,14},{8,1},{9,0},... | collective-permute-start | bytes 49160 | tf_op jit(solution)/shard_map/ppermute | solution.py:432
  21.0 1.0 %collective-permute-done.7.refs_3_ = bf16[8,1024]{1,0:T(8,128)(2,1)S(1)} collective-permute-done((bf16[8,1024]{1,0:T(8,128)(2,1)S(1)}, bf16[8,1024]{1,0:T(8,128)(2,1)S(1)}, u32[]{:S(2)}, u32[]{:S(2)}) %collective-permute-start.7) | collective-permute-done | bytes 16416 | tf_op jit(solution)/shard_map/ppermute | solution.py:432
  22.0 2.5 %collective-permute-done.6.refs_2_ = bf16[8,1024]{1,0:T(8,128)(2,1)S(1)} collective-permute-done((bf16[8,1024]{1,0:T(8,128)(2,1)S(1)}, bf16[8,1024]{1,0:T(8,128)(2,1)S(1)}, u32[]{:S(2)}, u32[]{:S(2)}) %collective-permute-start.6) | collective-permute-done | bytes 16416 | tf_op jit(solution)/shard_map/ppermute | solution.py:432
  24.5 0.0 collective-permute-done.5.refs_1_
  24.5 0.0 collective-permute-done.8.refs_5_
  24.5 0.8 %shard_map.105 = (f32[8,2048]{1,0:T(8,128)S(1)}, bf16[8,2048]{1,0:T(8,128)(2,1)S(1)}, bf16[8,2048]{1,0:T(8,128)(2,1)S(1)}, bf16[8,2048]{1,0:T(8,128)(2,1)S(1)}) custom-call(bf16[8,1024]{1,0:T(8,128)(2,1)S(1)} %get-tuple-element.36.refs_0_, bf16[8,1024]{1,0:T(8,128)(2,1)S(1)} %collective-permute-done.5.refs_1_, ...), custom_call_target="tpu_custom_call" | custom-call | tf_op jit(solution)/shard_map/pallas_call | solution.py:548
  25.3 1.5 %collective-permute-start.9 = (bf16[8,2048]{1,0:T(8,128)(2,1)S(1)}, bf16[8,2048]{1,0:T(8,128)(2,1)S(1)}, u32[]{:S(2)}, u32[]{:S(2)}) collective-permute-start(bf16[8,2048]{1,0:T(8,128)(2,1)S(1)} %get-tuple-element.40), channel_id=1, source_target_pairs={{0,7},{1,6},{2,5},{3,4},{4,3},{5,2},{6,1},{7,0},{8,15},{9,14},{10,... | collective-permute-start | bytes 98312 | tf_op jit(solution)/shard_map/ppermute | solution.py:259
  26.8 1.0 %collective-permute-start.10 = (bf16[8,2048]{1,0:T(8,128)(2,1)S(1)}, bf16[8,2048]{1,0:T(8,128)(2,1)S(1)}, u32[]{:S(2)}, u32[]{:S(2)}) collective-permute-start(bf16[8,2048]{1,0:T(8,128)(2,1)S(1)} %get-tuple-element.41), channel_id=1, source_target_pairs={{0,5},{1,4},{2,7},{3,6},{4,1},{5,0},{6,3},{7,2},{8,13},{9,12},{10,... | collective-permute-start | bytes 98312 | tf_op jit(solution)/shard_map/ppermute | solution.py:259
  27.8 0.8 %collective-permute-start.11 = (bf16[8,2048]{1,0:T(8,128)(2,1)S(1)}, bf16[8,2048]{1,0:T(8,128)(2,1)S(1)}, u32[]{:S(2)}, u32[]{:S(2)}) collective-permute-start(bf16[8,2048]{1,0:T(8,128)(2,1)S(1)} %get-tuple-element.42), channel_id=1, source_target_pairs={{0,3},{1,2},{2,1},{3,0},{4,7},{5,6},{6,5},{7,4},{8,11},{9,10},{10,... | collective-permute-start | bytes 98312 | tf_op jit(solution)/shard_map/ppermute | solution.py:259
  28.5 1.1 %collective-permute-done.9 = bf16[8,2048]{1,0:T(8,128)(2,1)S(1)} collective-permute-done((bf16[8,2048]{1,0:T(8,128)(2,1)S(1)}, bf16[8,2048]{1,0:T(8,128)(2,1)S(1)}, u32[]{:S(2)}, u32[]{:S(2)}) %collective-permute-start.9) | collective-permute-done | bytes 32800 | tf_op jit(solution)/shard_map/ppermute | solution.py:259
  29.6 1.2 %collective-permute-done.10 = bf16[8,2048]{1,0:T(8,128)(2,1)S(1)} collective-permute-done((bf16[8,2048]{1,0:T(8,128)(2,1)S(1)}, bf16[8,2048]{1,0:T(8,128)(2,1)S(1)}, u32[]{:S(2)}, u32[]{:S(2)}) %collective-permute-start.10) | collective-permute-done | bytes 32800 | tf_op jit(solution)/shard_map/ppermute | solution.py:259
  30.8 0.3 collective-permute-done.11
  31.1 0.6 %add_convert_fusion = bf16[8,2048]{1,0:T(8,128)(2,1)} fusion(bf16[8,2048]{1,0:T(8,128)(2,1)S(1)} %collective-permute-done.11, bf16[8,2048]{1,0:T(8,128)(2,1)S(1)} %collective-permute-done.10, f32[8,2048]{1,0:T(8,128)S(1)} %get-tuple-element.39, bf16[8,2048]{1,0:T(8,128)(2,1)S(1)} %collective-permute-done.9), kind=kLoop, calls=%fused_computation | loop fusion | flops 114688 | bytes 196608 | tf_op jit(solution)/shard_map/convert_element_type | solution.py:560
  (1 shorter events, 0.0 us)
Async XLA Ops:
  0.0 2.7 %collective-permute-start = (bf16[64,128]{1,0:T(8,128)(2,1)}, bf16[64,128]{1,0:T(8,128)(2,1)S(1)}, u32[]{:S(2)}, u32[]{:S(2)}) collective-permute-start(bf16[64,128]{1,0:T(8,128)(2,1)} %bitcast.14), channel_id=1, source_target_pairs={{0,1},{1,0},{2,3},{3,2},{4,5},{5,4},{6,7},{7,6},{8,9},{9,8},{10,11... | collective-permute-start | bytes 49160 | tf_op jit(solution)/shard_map/ppermute | solution.py:259
  2.8 21.7 %collective-permute-start.8 = (bf16[512,2048]{1,0:T(8,128)(2,1)}, bf16[512,2048]{1,0:T(8,128)(2,1)S(1)}, u32[]{:S(2)}, u32[]{:S(2)}) collective-permute-start(bf16[512,2048]{1,0:T(8,128)(2,1)} %weight_ref.1), channel_id=1, source_target_pairs={{0,1},{1,0},{2,3},{3,2},{4,5},{5,4},{6,7},{7,6},{8,9},{9,8},{10,11... | collective-permute-start | bytes 6291464 | tf_op jit(solution)/shard_map/ppermute | solution.py:259
  2.9 7.7 %collective-permute-start.1 = (bf16[592,128]{1,0:T(8,128)(2,1)S(1)}, bf16[592,128]{1,0:T(8,128)(2,1)S(1)}, u32[]{:S(2)}, u32[]{:S(2)}) collective-permute-start(bf16[592,128]{1,0:T(8,128)(2,1)S(1)} %get-tuple-element.33), channel_id=1, source_target_pairs={{0,2},{1,3},{2,0},{3,1},{4,6},{5,7},{6,4},{7,5},{8,10},{9,11},{10,... | collective-permute-start | bytes 454664 | tf_op jit(solution)/shard_map/ppermute | solution.py:259
  5.8 8.9 %collective-permute-start.2 = (bf16[592,128]{1,0:T(8,128)(2,1)S(1)}, bf16[592,128]{1,0:T(8,128)(2,1)S(1)}, u32[]{:S(2)}, u32[]{:S(2)}) collective-permute-start(bf16[592,128]{1,0:T(8,128)(2,1)S(1)} %get-tuple-element.34), channel_id=1, source_target_pairs={{0,4},{1,5},{2,6},{3,7},{4,0},{5,1},{6,2},{7,3},{8,12},{9,13},{10,... | collective-permute-start | bytes 454664 | tf_op jit(solution)/shard_map/ppermute | solution.py:259
  7.4 7.4 %collective-permute-start.3 = (bf16[592,128]{1,0:T(8,128)(2,1)S(1)}, bf16[592,128]{1,0:T(8,128)(2,1)S(1)}, u32[]{:S(2)}, u32[]{:S(2)}) collective-permute-start(bf16[592,128]{1,0:T(8,128)(2,1)S(1)} %get-tuple-element.35), channel_id=1, source_target_pairs={{0,6},{1,7},{2,4},{3,5},{4,2},{5,3},{6,0},{7,1},{8,14},{9,15},{10,... | collective-permute-start | bytes 454664 | tf_op jit(solution)/shard_map/ppermute | solution.py:259
  15.4 1.4 %collective-permute-start.4 = (f32[128,256]{1,0:T(8,128)S(1)}, f32[128,256]{1,0:T(8,128)S(1)}, u32[]{:S(2)}, u32[]{:S(2)}) collective-permute-start(f32[128,256]{1,0:T(8,128)S(1)} %shard_map.103.refs_0_), channel_id=1, source_target_pairs={{0,1},{1,0},{2,3},{3,2},{4,5},{5,4},{6,7},{7,6},{8,9},{9,8},{10,11... | collective-permute-start | bytes 393224 | tf_op jit(solution)/shard_map/ppermute | solution.py:259
  17.0 5.0 %collective-permute-start.7 = (bf16[8,1024]{1,0:T(8,128)(2,1)S(1)}, bf16[8,1024]{1,0:T(8,128)(2,1)S(1)}, u32[]{:S(2)}, u32[]{:S(2)}) collective-permute-start(bf16[8,1024]{1,0:T(8,128)(2,1)S(1)} %get-tuple-element.37), channel_id=1, source_target_pairs={{0,25},{1,24},{2,27},{3,26},{4,29},{5,28},{6,31},{7,30},{8,17},{9,... | collective-permute-start | bytes 49160 | tf_op jit(solution)/shard_map/ppermute | solution.py:432
  20.4 4.1 %collective-permute-start.6 = (bf16[8,1024]{1,0:T(8,128)(2,1)S(1)}, bf16[8,1024]{1,0:T(8,128)(2,1)S(1)}, u32[]{:S(2)}, u32[]{:S(2)}) collective-permute-start(bf16[8,1024]{1,0:T(8,128)(2,1)S(1)} %get-tuple-element.37), channel_id=1, source_target_pairs={{0,17},{1,16},{2,19},{3,18},{4,21},{5,20},{6,23},{7,22},{8,25},{9,... | collective-permute-start | bytes 49160 | tf_op jit(solution)/shard_map/ppermute | solution.py:432
  20.4 4.1 %collective-permute-start.5 = (bf16[8,1024]{1,0:T(8,128)(2,1)S(1)}, bf16[8,1024]{1,0:T(8,128)(2,1)S(1)}, u32[]{:S(2)}, u32[]{:S(2)}) collective-permute-start(bf16[8,1024]{1,0:T(8,128)(2,1)S(1)} %get-tuple-element.37), channel_id=1, source_target_pairs={{0,9},{1,8},{2,11},{3,10},{4,13},{5,12},{6,15},{7,14},{8,1},{9,0},... | collective-permute-start | bytes 49160 | tf_op jit(solution)/shard_map/ppermute | solution.py:432
  25.3 4.3 %collective-permute-start.9 = (bf16[8,2048]{1,0:T(8,128)(2,1)S(1)}, bf16[8,2048]{1,0:T(8,128)(2,1)S(1)}, u32[]{:S(2)}, u32[]{:S(2)}) collective-permute-start(bf16[8,2048]{1,0:T(8,128)(2,1)S(1)} %get-tuple-element.40), channel_id=1, source_target_pairs={{0,7},{1,6},{2,5},{3,4},{4,3},{5,2},{6,1},{7,0},{8,15},{9,14},{10,... | collective-permute-start | bytes 98312 | tf_op jit(solution)/shard_map/ppermute | solution.py:259
  26.8 4.0 %collective-permute-start.10 = (bf16[8,2048]{1,0:T(8,128)(2,1)S(1)}, bf16[8,2048]{1,0:T(8,128)(2,1)S(1)}, u32[]{:S(2)}, u32[]{:S(2)}) collective-permute-start(bf16[8,2048]{1,0:T(8,128)(2,1)S(1)} %get-tuple-element.41), channel_id=1, source_target_pairs={{0,5},{1,4},{2,7},{3,6},{4,1},{5,0},{6,3},{7,2},{8,13},{9,12},{10,... | collective-permute-start | bytes 98312 | tf_op jit(solution)/shard_map/ppermute | solution.py:259
  27.8 3.3 %collective-permute-start.11 = (bf16[8,2048]{1,0:T(8,128)(2,1)S(1)}, bf16[8,2048]{1,0:T(8,128)(2,1)S(1)}, u32[]{:S(2)}, u32[]{:S(2)}) collective-permute-start(bf16[8,2048]{1,0:T(8,128)(2,1)S(1)} %get-tuple-element.42), channel_id=1, source_target_pairs={{0,3},{1,2},{2,1},{3,0},{4,7},{5,6},{6,5},{7,4},{8,11},{9,10},{10,... | collective-permute-start | bytes 98312 | tf_op jit(solution)/shard_map/ppermute | solution.py:259

commit v6 on v5

--- a/solution.py
+++ b/solution.py
@@ -220,13 +220,23 @@
             out_ref[:, g * dim : (g + 1) * dim] = merged[place, :].astype(BF16)
 
 
+def prompt_targets(count):
+    if count == 4:
+        return ((1, 0, 3, 2), (3, 2, 0, 1), (2, 3, 1, 0))
+    return tuple(tuple(p ^ x for p in range(count)) for x in range(1, count))
+
+
 def project_kernel(ranks, head_refs, weight_refs, out_refs, all_heads):
     me = lax.axis_index("seq")
     chip, rank = lax.div(me, ranks), lax.rem(me, ranks)
     prompt = lax.axis_index("prompt")
     count = head_refs[0].shape[0]
     for x, ref in enumerate(head_refs):
-        place = pl.multiple_of((chip ^ prompt ^ x) * count, count)
+        sender = prompt
+        if x:
+            for p, target in enumerate(prompt_targets(len(head_refs))[x - 1]):
+                sender = jnp.where(prompt == target, p, sender)
+        place = pl.multiple_of((chip ^ sender) * count, count)
         all_heads[pl.ds(place, count), :] = ref[...].astype(F32)
     depth = weight_refs[0].shape[0]
     product = 0.0
@@ -538,7 +548,8 @@
     )(*parts)
     flip = 1 if ranks > 1 else 0
     head_outs = [staying] + [
-        cross(leaving, lambda p, s, x=x: (p ^ x, s ^ flip)) for x in range(1, prompt_count)
+        cross(leaving, lambda p, s, targets=targets: (targets[p], s ^ flip))
+        for targets in prompt_targets(prompt_count)
     ]
 
     def run_project(*refs):

time: 32 us -> 31.2 us (0.975)
  waiting for transfers between devices: 13.2 us -> 12.6 us
    ppermute x3, waiting for transfers between devices: 3.46 us -> 2.81 us  [cross(): return lax.ppermute(x, ('prompt', 'seq'), pairs)]
  transfers between devices with their start and end apart: 12 -> 12, of which waited for: 8 -> 9; matrix products, arithmetic and copies ran while one was open for 0% -> 0% of each run, Pallas kernels for 13% -> 13%
where the time goes in v6:
time: 31.2 us; the launch traced here: 31 us
  waiting for transfers between devices  12.6 us (40%)
  starting transfers between devices  12.1 us (39%)
  Pallas kernels  4.92 us (16%)
  between operations  0.71 us (2%)
  other arithmetic  0.64 us (2%)
    ppermute x9, waiting for transfers between devices, swap(): lax.ppermute(x, axis, [(i, i ^ distance) for i in range(lax.axis_size(axi...  9.8 us
    ppermute x9, starting transfers between devices, swap(): lax.ppermute(x, axis, [(i, i ^ distance) for i in range(lax.axis_size(axi...  8.18 us
    ppermute x3, starting transfers between devices, cross(): return lax.ppermute(x, ('prompt', 'seq'), pairs)  3.95 us
    ppermute x3, waiting for transfers between devices, cross(): return lax.ppermute(x, ('prompt', 'seq'), pairs)  2.81 us
    pallas_call x1, Pallas kernels, on_device(): call(run_message, [message] * heads, [hbm] * len(sources), [(pltpu.SMEM i...  1.62 us
    pallas_call x1, Pallas kernels, on_device(): call(fetch_kernel, jax.ShapeDtypeStruct(out_weight.shape, BF16), [pl.Bloc...  1.6 us
    pallas_call x1, Pallas kernels, on_device(): call(run_project, [jax.ShapeDtypeStruct((count, out_weight.shape[1]), BF1...  0.82 us
    pallas_call x1, Pallas kernels, on_device(): call(run_prefix, jax.ShapeDtypeStruct((all_rows, 2 * dim), F32), [vmem] *...  0.65 us
  transfers between devices with their start and end apart: 12, of which 9 were waited for; matrix products, arithmetic and copies ran while one was open for 0% of the time, Pallas kernels for 13%

profile of v6, /device:TPU:0, one launch (start us, length us, event | category | flops | bytes accessed | tf_op | source)
XLA Modules:
  0.0 31.0 jit_solution(5893516525264112726)
XLA Ops:
  0.0 0.5 %collective-permute-start = (bf16[64,128]{1,0:T(8,128)(2,1)}, bf16[64,128]{1,0:T(8,128)(2,1)S(1)}, u32[]{:S(2)}, u32[]{:S(2)}) collective-permute-start(bf16[64,128]{1,0:T(8,128)(2,1)} %bitcast.14), channel_id=1, source_target_pairs={{0,1},{1,0},{2,3},{3,2},{4,5},{5,4},{6,7},{7,6},{8,9},{9,8},{10,11... | collective-permute-start | bytes 49160 | tf_op jit(solution)/shard_map/ppermute | solution.py:269
  1.1 1.6 %shard_map.100 = (bf16[592,128]{1,0:T(8,128)(2,1)S(1)}, bf16[592,128]{1,0:T(8,128)(2,1)S(1)}, bf16[592,128]{1,0:T(8,128)(2,1)S(1)}, bf16[592,128]{1,0:T(8,128)(2,1)S(1)}) custom-call(bf16[4,256,128]{2,1,0:T(8,128)(2,1)} %bitcast.10, bf16[4,256,128]{2,1,0:T(8,128)(2,1)} %bitcast.11, bf16[64,128]{1,0:T(8,128)(2,1)} %bitcast.15, bf16[4,256,128]{2,1,0:T(8,128)(2,1)} %bitcast.12, ...), custom_call_target="tpu_custom_call" | custom-call | tf_op jit(solution)/shard_map/pallas_call | solution.py:490
  2.7 0.0 collective-permute-done.refs_0_
  2.8 0.1 collective-permute-start.8
  2.9 2.9 %collective-permute-start.1 = (bf16[592,128]{1,0:T(8,128)(2,1)S(1)}, bf16[592,128]{1,0:T(8,128)(2,1)S(1)}, u32[]{:S(2)}, u32[]{:S(2)}) collective-permute-start(bf16[592,128]{1,0:T(8,128)(2,1)S(1)} %get-tuple-element.33), channel_id=1, source_target_pairs={{0,2},{1,3},{2,0},{3,1},{4,6},{5,7},{6,4},{7,5},{8,10},{9,11},{10,... | collective-permute-start | bytes 454664 | tf_op jit(solution)/shard_map/ppermute | solution.py:269
  5.8 1.5 %collective-permute-start.2 = (bf16[592,128]{1,0:T(8,128)(2,1)S(1)}, bf16[592,128]{1,0:T(8,128)(2,1)S(1)}, u32[]{:S(2)}, u32[]{:S(2)}) collective-permute-start(bf16[592,128]{1,0:T(8,128)(2,1)S(1)} %get-tuple-element.34), channel_id=1, source_target_pairs={{0,4},{1,5},{2,6},{3,7},{4,0},{5,1},{6,2},{7,3},{8,12},{9,13},{10,... | collective-permute-start | bytes 454664 | tf_op jit(solution)/shard_map/ppermute | solution.py:269
  7.4 0.0 collective-permute-start.3
  7.4 1.6 %shard_map.102.refs_4_ = bf16[512,2048]{1,0:T(8,128)(2,1)S(1)} custom-call(bf16[592,128]{1,0:T(8,128)(2,1)S(1)} %get-tuple-element.32.after_ref.refs_0_, bf16[512,2048]{1,0:T(8,128)(2,1)} %weight_ref.1), custom_call_target="tpu_custom_call" | custom-call | tf_op jit(solution)/shard_map/pallas_call | solution.py:518
  9.0 1.6 %collective-permute-done.1.refs_1_ = bf16[592,128]{1,0:T(8,128)(2,1)S(1)} collective-permute-done((bf16[592,128]{1,0:T(8,128)(2,1)S(1)}, bf16[592,128]{1,0:T(8,128)(2,1)S(1)}, u32[]{:S(2)}, u32[]{:S(2)}) %collective-permute-start.1) | collective-permute-done | bytes 151584 | tf_op jit(solution)/shard_map/ppermute | solution.py:269
  10.6 4.2 %collective-permute-done.2.refs_2_ = bf16[592,128]{1,0:T(8,128)(2,1)S(1)} collective-permute-done((bf16[592,128]{1,0:T(8,128)(2,1)S(1)}, bf16[592,128]{1,0:T(8,128)(2,1)S(1)}, u32[]{:S(2)}, u32[]{:S(2)}) %collective-permute-start.2) | collective-permute-done | bytes 151584 | tf_op jit(solution)/shard_map/ppermute | solution.py:269
  14.7 0.0 collective-permute-done.3.refs_3_
  14.7 0.6 %shard_map.103.refs_0_ = f32[128,256]{1,0:T(8,128)S(1)} custom-call(bf16[592,128]{1,0:T(8,128)(2,1)S(1)} %get-tuple-element.32.after_ref.refs_0_, bf16[592,128]{1,0:T(8,128)(2,1)S(1)} %collective-permute-done.1.refs_1_, bf16[592,128]{1,0:T(8,128)(2,1)S(1)} %collective-permute-done.2.refs_2_, bf16[592,128]{1,0:T(8,128)(2,1)S(1)} %collective-permute-done.3.refs_3_, ...), custom_call_target="tpu_custom_call" | custom-call | tf_op jit(solution)/shard_map/pallas_call | solution.py:531
  15.4 0.1 collective-permute-start.4
  15.4 1.3 %collective-permute-done.4.refs_1_ = f32[128,256]{1,0:T(8,128)S(1)} collective-permute-done((f32[128,256]{1,0:T(8,128)S(1)}, f32[128,256]{1,0:T(8,128)S(1)}, u32[]{:S(2)}, u32[]{:S(2)}) %collective-permute-start.4) | collective-permute-done | bytes 131104 | tf_op jit(solution)/shard_map/ppermute | solution.py:269
  16.8 0.2 shard_map.104
  17.0 2.4 %collective-permute-start.7 = (bf16[8,1024]{1,0:T(8,128)(2,1)S(1)}, bf16[8,1024]{1,0:T(8,128)(2,1)S(1)}, u32[]{:S(2)}, u32[]{:S(2)}) collective-permute-start(bf16[8,1024]{1,0:T(8,128)(2,1)S(1)} %get-tuple-element.37), channel_id=1, source_target_pairs={{0,17},{1,16},{2,19},{3,18},{4,21},{5,20},{6,23},{7,22},{8,25},{9,... | collective-permute-start | bytes 49160 | tf_op jit(solution)/shard_map/ppermute | solution.py:442
  19.4 1.2 %collective-permute-start.6 = (bf16[8,1024]{1,0:T(8,128)(2,1)S(1)}, bf16[8,1024]{1,0:T(8,128)(2,1)S(1)}, u32[]{:S(2)}, u32[]{:S(2)}) collective-permute-start(bf16[8,1024]{1,0:T(8,128)(2,1)S(1)} %get-tuple-element.37), channel_id=1, source_target_pairs={{0,25},{1,24},{2,27},{3,26},{4,29},{5,28},{6,31},{7,30},{8,17},{9,... | collective-permute-start | bytes 49160 | tf_op jit(solution)/shard_map/ppermute | solution.py:442
  20.6 0.4 %collective-permute-start.5 = (bf16[8,1024]{1,0:T(8,128)(2,1)S(1)}, bf16[8,1024]{1,0:T(8,128)(2,1)S(1)}, u32[]{:S(2)}, u32[]{:S(2)}) collective-permute-start(bf16[8,1024]{1,0:T(8,128)(2,1)S(1)} %get-tuple-element.37), channel_id=1, source_target_pairs={{0,9},{1,8},{2,11},{3,10},{4,13},{5,12},{6,15},{7,14},{8,1},{9,0},... | collective-permute-start | bytes 49160 | tf_op jit(solution)/shard_map/ppermute | solution.py:442
  21.0 1.1 %collective-permute-done.7.refs_3_ = bf16[8,1024]{1,0:T(8,128)(2,1)S(1)} collective-permute-done((bf16[8,1024]{1,0:T(8,128)(2,1)S(1)}, bf16[8,1024]{1,0:T(8,128)(2,1)S(1)}, u32[]{:S(2)}, u32[]{:S(2)}) %collective-permute-start.7) | collective-permute-done | bytes 16416 | tf_op jit(solution)/shard_map/ppermute | solution.py:442
  22.0 1.5 %collective-permute-done.6.refs_2_ = bf16[8,1024]{1,0:T(8,128)(2,1)S(1)} collective-permute-done((bf16[8,1024]{1,0:T(8,128)(2,1)S(1)}, bf16[8,1024]{1,0:T(8,128)(2,1)S(1)}, u32[]{:S(2)}, u32[]{:S(2)}) %collective-permute-start.6) | collective-permute-done | bytes 16416 | tf_op jit(solution)/shard_map/ppermute | solution.py:442
  23.5 0.3 collective-permute-done.5.refs_1_
  23.8 0.0 collective-permute-done.8.refs_5_
  23.8 0.8 %shard_map.105 = (f32[8,2048]{1,0:T(8,128)S(1)}, bf16[8,2048]{1,0:T(8,128)(2,1)S(1)}, bf16[8,2048]{1,0:T(8,128)(2,1)S(1)}, bf16[8,2048]{1,0:T(8,128)(2,1)S(1)}) custom-call(bf16[8,1024]{1,0:T(8,128)(2,1)S(1)} %get-tuple-element.36.refs_0_, bf16[8,1024]{1,0:T(8,128)(2,1)S(1)} %collective-permute-done.5.refs_1_, ...), custom_call_target="tpu_custom_call" | custom-call | tf_op jit(solution)/shard_map/pallas_call | solution.py:559
  24.6 1.4 %collective-permute-start.9 = (bf16[8,2048]{1,0:T(8,128)(2,1)S(1)}, bf16[8,2048]{1,0:T(8,128)(2,1)S(1)}, u32[]{:S(2)}, u32[]{:S(2)}) collective-permute-start(bf16[8,2048]{1,0:T(8,128)(2,1)S(1)} %get-tuple-element.40), channel_id=1, source_target_pairs={{0,7},{1,6},{2,5},{3,4},{4,3},{5,2},{6,1},{7,0},{8,15},{9,14},{10,... | collective-permute-start | bytes 98312 | tf_op jit(solution)/shard_map/ppermute | solution.py:269
  25.9 1.1 %collective-permute-start.10 = (bf16[8,2048]{1,0:T(8,128)(2,1)S(1)}, bf16[8,2048]{1,0:T(8,128)(2,1)S(1)}, u32[]{:S(2)}, u32[]{:S(2)}) collective-permute-start(bf16[8,2048]{1,0:T(8,128)(2,1)S(1)} %get-tuple-element.41), channel_id=1, source_target_pairs={{0,5},{1,4},{2,7},{3,6},{4,1},{5,0},{6,3},{7,2},{8,13},{9,12},{10,... | collective-permute-start | bytes 98312 | tf_op jit(solution)/shard_map/ppermute | solution.py:269
  27.0 0.6 %collective-permute-start.11 = (bf16[8,2048]{1,0:T(8,128)(2,1)S(1)}, bf16[8,2048]{1,0:T(8,128)(2,1)S(1)}, u32[]{:S(2)}, u32[]{:S(2)}) collective-permute-start(bf16[8,2048]{1,0:T(8,128)(2,1)S(1)} %get-tuple-element.42), channel_id=1, source_target_pairs={{0,3},{1,2},{2,1},{3,0},{4,7},{5,6},{6,5},{7,4},{8,11},{9,10},{10,... | collective-permute-start | bytes 98312 | tf_op jit(solution)/shard_map/ppermute | solution.py:269
  27.7 1.2 %collective-permute-done.9 = bf16[8,2048]{1,0:T(8,128)(2,1)S(1)} collective-permute-done((bf16[8,2048]{1,0:T(8,128)(2,1)S(1)}, bf16[8,2048]{1,0:T(8,128)(2,1)S(1)}, u32[]{:S(2)}, u32[]{:S(2)}) %collective-permute-start.9) | collective-permute-done | bytes 32800 | tf_op jit(solution)/shard_map/ppermute | solution.py:269
  28.8 1.0 %collective-permute-done.10 = bf16[8,2048]{1,0:T(8,128)(2,1)S(1)} collective-permute-done((bf16[8,2048]{1,0:T(8,128)(2,1)S(1)}, bf16[8,2048]{1,0:T(8,128)(2,1)S(1)}, u32[]{:S(2)}, u32[]{:S(2)}) %collective-permute-start.10) | collective-permute-done | bytes 32800 | tf_op jit(solution)/shard_map/ppermute | solution.py:269
  29.8 0.5 %collective-permute-done.11 = bf16[8,2048]{1,0:T(8,128)(2,1)S(1)} collective-permute-done((bf16[8,2048]{1,0:T(8,128)(2,1)S(1)}, bf16[8,2048]{1,0:T(8,128)(2,1)S(1)}, u32[]{:S(2)}, u32[]{:S(2)}) %collective-permute-start.11) | collective-permute-done | bytes 32800 | tf_op jit(solution)/shard_map/ppermute | solution.py:269
  30.4 0.6 %add_convert_fusion = bf16[8,2048]{1,0:T(8,128)(2,1)} fusion(bf16[8,2048]{1,0:T(8,128)(2,1)S(1)} %collective-permute-done.11, bf16[8,2048]{1,0:T(8,128)(2,1)S(1)} %collective-permute-done.10, f32[8,2048]{1,0:T(8,128)S(1)} %get-tuple-element.39, bf16[8,2048]{1,0:T(8,128)(2,1)S(1)} %collective-permute-done.9), kind=kLoop, calls=%fused_computation | loop fusion | flops 114688 | bytes 196608 | tf_op jit(solution)/shard_map/convert_element_type | solution.py:571
  (1 shorter events, 0.0 us)
Async XLA Ops:
  0.0 2.7 %collective-permute-start = (bf16[64,128]{1,0:T(8,128)(2,1)}, bf16[64,128]{1,0:T(8,128)(2,1)S(1)}, u32[]{:S(2)}, u32[]{:S(2)}) collective-permute-start(bf16[64,128]{1,0:T(8,128)(2,1)} %bitcast.14), channel_id=1, source_target_pairs={{0,1},{1,0},{2,3},{3,2},{4,5},{5,4},{6,7},{7,6},{8,9},{9,8},{10,11... | collective-permute-start | bytes 49160 | tf_op jit(solution)/shard_map/ppermute | solution.py:269
  2.8 21.0 %collective-permute-start.8 = (bf16[512,2048]{1,0:T(8,128)(2,1)}, bf16[512,2048]{1,0:T(8,128)(2,1)S(1)}, u32[]{:S(2)}, u32[]{:S(2)}) collective-permute-start(bf16[512,2048]{1,0:T(8,128)(2,1)} %weight_ref.1), channel_id=1, source_target_pairs={{0,1},{1,0},{2,3},{3,2},{4,5},{5,4},{6,7},{7,6},{8,9},{9,8},{10,11... | collective-permute-start | bytes 6291464 | tf_op jit(solution)/shard_map/ppermute | solution.py:269
  2.9 7.7 %collective-permute-start.1 = (bf16[592,128]{1,0:T(8,128)(2,1)S(1)}, bf16[592,128]{1,0:T(8,128)(2,1)S(1)}, u32[]{:S(2)}, u32[]{:S(2)}) collective-permute-start(bf16[592,128]{1,0:T(8,128)(2,1)S(1)} %get-tuple-element.33), channel_id=1, source_target_pairs={{0,2},{1,3},{2,0},{3,1},{4,6},{5,7},{6,4},{7,5},{8,10},{9,11},{10,... | collective-permute-start | bytes 454664 | tf_op jit(solution)/shard_map/ppermute | solution.py:269
  5.8 8.9 %collective-permute-start.2 = (bf16[592,128]{1,0:T(8,128)(2,1)S(1)}, bf16[592,128]{1,0:T(8,128)(2,1)S(1)}, u32[]{:S(2)}, u32[]{:S(2)}) collective-permute-start(bf16[592,128]{1,0:T(8,128)(2,1)S(1)} %get-tuple-element.34), channel_id=1, source_target_pairs={{0,4},{1,5},{2,6},{3,7},{4,0},{5,1},{6,2},{7,3},{8,12},{9,13},{10,... | collective-permute-start | bytes 454664 | tf_op jit(solution)/shard_map/ppermute | solution.py:269
  7.4 7.4 %collective-permute-start.3 = (bf16[592,128]{1,0:T(8,128)(2,1)S(1)}, bf16[592,128]{1,0:T(8,128)(2,1)S(1)}, u32[]{:S(2)}, u32[]{:S(2)}) collective-permute-start(bf16[592,128]{1,0:T(8,128)(2,1)S(1)} %get-tuple-element.35), channel_id=1, source_target_pairs={{0,6},{1,7},{2,4},{3,5},{4,2},{5,3},{6,0},{7,1},{8,14},{9,15},{10,... | collective-permute-start | bytes 454664 | tf_op jit(solution)/shard_map/ppermute | solution.py:269
  15.4 1.4 %collective-permute-start.4 = (f32[128,256]{1,0:T(8,128)S(1)}, f32[128,256]{1,0:T(8,128)S(1)}, u32[]{:S(2)}, u32[]{:S(2)}) collective-permute-start(f32[128,256]{1,0:T(8,128)S(1)} %shard_map.103.refs_0_), channel_id=1, source_target_pairs={{0,1},{1,0},{2,3},{3,2},{4,5},{5,4},{6,7},{7,6},{8,9},{9,8},{10,11... | collective-permute-start | bytes 393224 | tf_op jit(solution)/shard_map/ppermute | solution.py:269
  17.0 5.0 %collective-permute-start.7 = (bf16[8,1024]{1,0:T(8,128)(2,1)S(1)}, bf16[8,1024]{1,0:T(8,128)(2,1)S(1)}, u32[]{:S(2)}, u32[]{:S(2)}) collective-permute-start(bf16[8,1024]{1,0:T(8,128)(2,1)S(1)} %get-tuple-element.37), channel_id=1, source_target_pairs={{0,17},{1,16},{2,19},{3,18},{4,21},{5,20},{6,23},{7,22},{8,25},{9,... | collective-permute-start | bytes 49160 | tf_op jit(solution)/shard_map/ppermute | solution.py:442
  19.4 4.1 %collective-permute-start.6 = (bf16[8,1024]{1,0:T(8,128)(2,1)S(1)}, bf16[8,1024]{1,0:T(8,128)(2,1)S(1)}, u32[]{:S(2)}, u32[]{:S(2)}) collective-permute-start(bf16[8,1024]{1,0:T(8,128)(2,1)S(1)} %get-tuple-element.37), channel_id=1, source_target_pairs={{0,25},{1,24},{2,27},{3,26},{4,29},{5,28},{6,31},{7,30},{8,17},{9,... | collective-permute-start | bytes 49160 | tf_op jit(solution)/shard_map/ppermute | solution.py:442
  20.6 3.2 %collective-permute-start.5 = (bf16[8,1024]{1,0:T(8,128)(2,1)S(1)}, bf16[8,1024]{1,0:T(8,128)(2,1)S(1)}, u32[]{:S(2)}, u32[]{:S(2)}) collective-permute-start(bf16[8,1024]{1,0:T(8,128)(2,1)S(1)} %get-tuple-element.37), channel_id=1, source_target_pairs={{0,9},{1,8},{2,11},{3,10},{4,13},{5,12},{6,15},{7,14},{8,1},{9,0},... | collective-permute-start | bytes 49160 | tf_op jit(solution)/shard_map/ppermute | solution.py:442
  24.6 4.3 %collective-permute-start.9 = (bf16[8,2048]{1,0:T(8,128)(2,1)S(1)}, bf16[8,2048]{1,0:T(8,128)(2,1)S(1)}, u32[]{:S(2)}, u32[]{:S(2)}) collective-permute-start(bf16[8,2048]{1,0:T(8,128)(2,1)S(1)} %get-tuple-element.40), channel_id=1, source_target_pairs={{0,7},{1,6},{2,5},{3,4},{4,3},{5,2},{6,1},{7,0},{8,15},{9,14},{10,... | collective-permute-start | bytes 98312 | tf_op jit(solution)/shard_map/ppermute | solution.py:269
  25.9 3.9 %collective-permute-start.10 = (bf16[8,2048]{1,0:T(8,128)(2,1)S(1)}, bf16[8,2048]{1,0:T(8,128)(2,1)S(1)}, u32[]{:S(2)}, u32[]{:S(2)}) collective-permute-start(bf16[8,2048]{1,0:T(8,128)(2,1)S(1)} %get-tuple-element.41), channel_id=1, source_target_pairs={{0,5},{1,4},{2,7},{3,6},{4,1},{5,0},{6,3},{7,2},{8,13},{9,12},{10,... | collective-permute-start | bytes 98312 | tf_op jit(solution)/shard_map/ppermute | solution.py:269
  27.0 3.3 %collective-permute-start.11 = (bf16[8,2048]{1,0:T(8,128)(2,1)S(1)}, bf16[8,2048]{1,0:T(8,128)(2,1)S(1)}, u32[]{:S(2)}, u32[]{:S(2)}) collective-permute-start(bf16[8,2048]{1,0:T(8,128)(2,1)S(1)} %get-tuple-element.42), channel_id=1, source_target_pairs={{0,3},{1,2},{2,1},{3,0},{4,7},{5,6},{6,5},{7,4},{8,11},{9,10},{10,... | collective-permute-start | bytes 98312 | tf_op jit(solution)/shard_map/ppermute | solution.py:269

commit v7 on v6

--- a/solution.py
+++ b/solution.py
@@ -226,6 +226,20 @@
     return tuple(tuple(p ^ x for p in range(count)) for x in range(1, count))
 
 
+def chip_targets(count):
+    if count == 4:
+        return ((2, 3, 1, 0), (1, 0, 3, 2), (3, 2, 0, 1))
+    return tuple(tuple(k ^ x for k in range(count)) for x in range(1, count))
+
+
+def slot_of(chip, target, count):
+    slot = 0
+    for i, targets in enumerate(chip_targets(count)):
+        for k, to in enumerate(targets):
+            slot = jnp.where((chip == k) & (target == to), i + 1, slot)
+    return slot
+
+
 def project_kernel(ranks, head_refs, weight_refs, out_refs, all_heads):
     me = lax.axis_index("seq")
     chip, rank = lax.div(me, ranks), lax.rem(me, ranks)
@@ -236,7 +250,7 @@
         if x:
             for p, target in enumerate(prompt_targets(len(head_refs))[x - 1]):
                 sender = jnp.where(prompt == target, p, sender)
-        place = pl.multiple_of((chip ^ sender) * count, count)
+        place = pl.multiple_of(slot_of(chip, sender, len(out_refs)) * count, count)
         all_heads[pl.ds(place, count), :] = ref[...].astype(F32)
     depth = weight_refs[0].shape[0]
     product = 0.0
@@ -566,8 +580,9 @@
         [pltpu.VMEM((prompt_count * count, group * dim), F32)],
     )(*head_outs, weight, *other_weights)
     result = terms[0]
-    for x in reversed(range(1, heads)):
-        result = result + swap(terms[x], "seq", x * ranks + flip).astype(F32)
+    for x, targets in enumerate(chip_targets(heads)):
+        pairs = [(i, targets[i // ranks] * ranks + (i % ranks ^ flip)) for i in range(seq_count)]
+        result = result + lax.ppermute(terms[x + 1], "seq", pairs).astype(F32)
     return result.astype(BF16)
 
 

time: 31.2 us -> 30.8 us (0.987)
  waiting for transfers between devices: 12.6 us -> 11.5 us
  starting transfers between devices: 12.1 us -> 12.8 us
    ppermute x0 -> x3, starting transfers between devices: none -> 3.74 us  [on_device(): result = result + lax.ppermute(terms[x + 1], 'seq', pairs).astype(F32)]
    ppermute x9 -> x6, starting transfers between devices: 8.18 us -> 5.1 us  [swap(): lax.ppermute(x, axis, [(i, i ^ distance) for i in range(lax.axis_size(axi...]
    ppermute x9 -> x6, waiting for transfers between devices: 9.8 us -> 7.1 us  [swap(): lax.ppermute(x, axis, [(i, i ^ distance) for i in range(lax.axis_size(axi...]
    ppermute x0 -> x3, waiting for transfers between devices: none -> 1.6 us  [on_device(): result = result + lax.ppermute(terms[x + 1], 'seq', pairs).astype(F32)]
where the time goes in v7:
time: 30.8 us; the launch traced here: 30.6 us
  starting transfers between devices  12.8 us (42%)
  waiting for transfers between devices  11.5 us (37%)
  Pallas kernels  4.94 us (16%)
  between operations  0.71 us (2%)
  other arithmetic  0.63 us (2%)
    ppermute x6, waiting for transfers between devices, swap(): lax.ppermute(x, axis, [(i, i ^ distance) for i in range(lax.axis_size(axi...  7.1 us
    ppermute x6, starting transfers between devices, swap(): lax.ppermute(x, axis, [(i, i ^ distance) for i in range(lax.axis_size(axi...  5.1 us
    ppermute x3, starting transfers between devices, cross(): return lax.ppermute(x, ('prompt', 'seq'), pairs)  3.95 us
    ppermute x3, starting transfers between devices, on_device(): result = result + lax.ppermute(terms[x + 1], 'seq', pairs).astype(F32)  3.74 us
    ppermute x3, waiting for transfers between devices, cross(): return lax.ppermute(x, ('prompt', 'seq'), pairs)  2.81 us
    pallas_call x1, Pallas kernels, on_device(): call(run_message, [message] * heads, [hbm] * len(sources), [(pltpu.SMEM i...  1.62 us
    pallas_call x1, Pallas kernels, on_device(): call(fetch_kernel, jax.ShapeDtypeStruct(out_weight.shape, BF16), [pl.Bloc...  1.6 us
    ppermute x3, waiting for transfers between devices, on_device(): result = result + lax.ppermute(terms[x + 1], 'seq', pairs).astype(F32)  1.6 us
  transfers between devices with their start and end apart: 12, of which 9 were waited for; matrix products, arithmetic and copies ran while one was open for 0% of the time, Pallas kernels for 13%

profile of v7, /device:TPU:0, one launch (start us, length us, event | category | flops | bytes accessed | tf_op | source)
XLA Modules:
  0.0 30.6 jit_solution(17481554858580255193)
XLA Ops:
  0.0 0.5 %collective-permute-start = (bf16[64,128]{1,0:T(8,128)(2,1)}, bf16[64,128]{1,0:T(8,128)(2,1)S(1)}, u32[]{:S(2)}, u32[]{:S(2)}) collective-permute-start(bf16[64,128]{1,0:T(8,128)(2,1)} %bitcast.14), channel_id=1, source_target_pairs={{0,1},{1,0},{2,3},{3,2},{4,5},{5,4},{6,7},{7,6},{8,9},{9,8},{10,11... | collective-permute-start | bytes 49160 | tf_op jit(solution)/shard_map/ppermute | solution.py:283
  1.1 1.6 %shard_map.100 = (bf16[592,128]{1,0:T(8,128)(2,1)S(1)}, bf16[592,128]{1,0:T(8,128)(2,1)S(1)}, bf16[592,128]{1,0:T(8,128)(2,1)S(1)}, bf16[592,128]{1,0:T(8,128)(2,1)S(1)}) custom-call(bf16[4,256,128]{2,1,0:T(8,128)(2,1)} %bitcast.10, bf16[4,256,128]{2,1,0:T(8,128)(2,1)} %bitcast.11, bf16[64,128]{1,0:T(8,128)(2,1)} %bitcast.15, bf16[4,256,128]{2,1,0:T(8,128)(2,1)} %bitcast.12, ...), custom_call_target="tpu_custom_call" | custom-call | tf_op jit(solution)/shard_map/pallas_call | solution.py:504
  2.7 0.0 collective-permute-done.refs_0_
  2.8 0.1 collective-permute-start.8
  2.9 2.9 %collective-permute-start.1 = (bf16[592,128]{1,0:T(8,128)(2,1)S(1)}, bf16[592,128]{1,0:T(8,128)(2,1)S(1)}, u32[]{:S(2)}, u32[]{:S(2)}) collective-permute-start(bf16[592,128]{1,0:T(8,128)(2,1)S(1)} %get-tuple-element.33), channel_id=1, source_target_pairs={{0,2},{1,3},{2,0},{3,1},{4,6},{5,7},{6,4},{7,5},{8,10},{9,11},{10,... | collective-permute-start | bytes 454664 | tf_op jit(solution)/shard_map/ppermute | solution.py:283
  5.8 1.5 %collective-permute-start.2 = (bf16[592,128]{1,0:T(8,128)(2,1)S(1)}, bf16[592,128]{1,0:T(8,128)(2,1)S(1)}, u32[]{:S(2)}, u32[]{:S(2)}) collective-permute-start(bf16[592,128]{1,0:T(8,128)(2,1)S(1)} %get-tuple-element.34), channel_id=1, source_target_pairs={{0,4},{1,5},{2,6},{3,7},{4,0},{5,1},{6,2},{7,3},{8,12},{9,13},{10,... | collective-permute-start | bytes 454664 | tf_op jit(solution)/shard_map/ppermute | solution.py:283
  7.4 0.0 collective-permute-start.3
  7.4 1.6 %shard_map.102.refs_4_ = bf16[512,2048]{1,0:T(8,128)(2,1)S(1)} custom-call(bf16[592,128]{1,0:T(8,128)(2,1)S(1)} %get-tuple-element.32.after_ref.refs_0_, bf16[512,2048]{1,0:T(8,128)(2,1)} %weight_ref.1), custom_call_target="tpu_custom_call" | custom-call | tf_op jit(solution)/shard_map/pallas_call | solution.py:532
  9.0 1.6 %collective-permute-done.1.refs_1_ = bf16[592,128]{1,0:T(8,128)(2,1)S(1)} collective-permute-done((bf16[592,128]{1,0:T(8,128)(2,1)S(1)}, bf16[592,128]{1,0:T(8,128)(2,1)S(1)}, u32[]{:S(2)}, u32[]{:S(2)}) %collective-permute-start.1) | collective-permute-done | bytes 151584 | tf_op jit(solution)/shard_map/ppermute | solution.py:283
  10.6 4.2 %collective-permute-done.2.refs_2_ = bf16[592,128]{1,0:T(8,128)(2,1)S(1)} collective-permute-done((bf16[592,128]{1,0:T(8,128)(2,1)S(1)}, bf16[592,128]{1,0:T(8,128)(2,1)S(1)}, u32[]{:S(2)}, u32[]{:S(2)}) %collective-permute-start.2) | collective-permute-done | bytes 151584 | tf_op jit(solution)/shard_map/ppermute | solution.py:283
  14.7 0.0 collective-permute-done.3.refs_3_
  14.7 0.6 %shard_map.103.refs_0_ = f32[128,256]{1,0:T(8,128)S(1)} custom-call(bf16[592,128]{1,0:T(8,128)(2,1)S(1)} %get-tuple-element.32.after_ref.refs_0_, bf16[592,128]{1,0:T(8,128)(2,1)S(1)} %collective-permute-done.1.refs_1_, bf16[592,128]{1,0:T(8,128)(2,1)S(1)} %collective-permute-done.2.refs_2_, bf16[592,128]{1,0:T(8,128)(2,1)S(1)} %collective-permute-done.3.refs_3_, ...), custom_call_target="tpu_custom_call" | custom-call | tf_op jit(solution)/shard_map/pallas_call | solution.py:545
  15.4 0.1 collective-permute-start.4
  15.4 1.3 %collective-permute-done.4.refs_1_ = f32[128,256]{1,0:T(8,128)S(1)} collective-permute-done((f32[128,256]{1,0:T(8,128)S(1)}, f32[128,256]{1,0:T(8,128)S(1)}, u32[]{:S(2)}, u32[]{:S(2)}) %collective-permute-start.4) | collective-permute-done | bytes 131104 | tf_op jit(solution)/shard_map/ppermute | solution.py:283
  16.8 0.2 shard_map.104
  17.0 2.4 %collective-permute-start.7 = (bf16[8,1024]{1,0:T(8,128)(2,1)S(1)}, bf16[8,1024]{1,0:T(8,128)(2,1)S(1)}, u32[]{:S(2)}, u32[]{:S(2)}) collective-permute-start(bf16[8,1024]{1,0:T(8,128)(2,1)S(1)} %get-tuple-element.37), channel_id=1, source_target_pairs={{0,17},{1,16},{2,19},{3,18},{4,21},{5,20},{6,23},{7,22},{8,25},{9,... | collective-permute-start | bytes 49160 | tf_op jit(solution)/shard_map/ppermute | solution.py:456
  19.4 1.2 %collective-permute-start.6 = (bf16[8,1024]{1,0:T(8,128)(2,1)S(1)}, bf16[8,1024]{1,0:T(8,128)(2,1)S(1)}, u32[]{:S(2)}, u32[]{:S(2)}) collective-permute-start(bf16[8,1024]{1,0:T(8,128)(2,1)S(1)} %get-tuple-element.37), channel_id=1, source_target_pairs={{0,25},{1,24},{2,27},{3,26},{4,29},{5,28},{6,31},{7,30},{8,17},{9,... | collective-permute-start | bytes 49160 | tf_op jit(solution)/shard_map/ppermute | solution.py:456
  20.6 0.4 %collective-permute-start.5 = (bf16[8,1024]{1,0:T(8,128)(2,1)S(1)}, bf16[8,1024]{1,0:T(8,128)(2,1)S(1)}, u32[]{:S(2)}, u32[]{:S(2)}) collective-permute-start(bf16[8,1024]{1,0:T(8,128)(2,1)S(1)} %get-tuple-element.37), channel_id=1, source_target_pairs={{0,9},{1,8},{2,11},{3,10},{4,13},{5,12},{6,15},{7,14},{8,1},{9,0},... | collective-permute-start | bytes 49160 | tf_op jit(solution)/shard_map/ppermute | solution.py:456
  21.0 1.1 %collective-permute-done.7.refs_3_ = bf16[8,1024]{1,0:T(8,128)(2,1)S(1)} collective-permute-done((bf16[8,1024]{1,0:T(8,128)(2,1)S(1)}, bf16[8,1024]{1,0:T(8,128)(2,1)S(1)}, u32[]{:S(2)}, u32[]{:S(2)}) %collective-permute-start.7) | collective-permute-done | bytes 16416 | tf_op jit(solution)/shard_map/ppermute | solution.py:456
  22.0 1.5 %collective-permute-done.6.refs_2_ = bf16[8,1024]{1,0:T(8,128)(2,1)S(1)} collective-permute-done((bf16[8,1024]{1,0:T(8,128)(2,1)S(1)}, bf16[8,1024]{1,0:T(8,128)(2,1)S(1)}, u32[]{:S(2)}, u32[]{:S(2)}) %collective-permute-start.6) | collective-permute-done | bytes 16416 | tf_op jit(solution)/shard_map/ppermute | solution.py:456
  23.5 0.3 collective-permute-done.5.refs_1_
  23.8 0.0 collective-permute-done.8.refs_5_
  23.8 0.8 %shard_map.105 = (f32[8,2048]{1,0:T(8,128)S(1)}, bf16[8,2048]{1,0:T(8,128)(2,1)S(1)}, bf16[8,2048]{1,0:T(8,128)(2,1)S(1)}, bf16[8,2048]{1,0:T(8,128)(2,1)S(1)}) custom-call(bf16[8,1024]{1,0:T(8,128)(2,1)S(1)} %get-tuple-element.36.refs_0_, bf16[8,1024]{1,0:T(8,128)(2,1)S(1)} %collective-permute-done.5.refs_1_, ...), custom_call_target="tpu_custom_call" | custom-call | tf_op jit(solution)/shard_map/pallas_call | solution.py:573
  24.6 1.4 %collective-permute-start.9 = (bf16[8,2048]{1,0:T(8,128)(2,1)S(1)}, bf16[8,2048]{1,0:T(8,128)(2,1)S(1)}, u32[]{:S(2)}, u32[]{:S(2)}) collective-permute-start(bf16[8,2048]{1,0:T(8,128)(2,1)S(1)} %get-tuple-element.40), channel_id=1, source_target_pairs={{0,5},{1,4},{2,7},{3,6},{4,3},{5,2},{6,1},{7,0},{8,13},{9,12},{10,... | collective-permute-start | bytes 98312 | tf_op jit(solution)/shard_map/ppermute | solution.py:585
  26.0 0.4 %collective-permute-start.10 = (bf16[8,2048]{1,0:T(8,128)(2,1)S(1)}, bf16[8,2048]{1,0:T(8,128)(2,1)S(1)}, u32[]{:S(2)}, u32[]{:S(2)}) collective-permute-start(bf16[8,2048]{1,0:T(8,128)(2,1)S(1)} %get-tuple-element.41), channel_id=1, source_target_pairs={{0,3},{1,2},{2,1},{3,0},{4,7},{5,6},{6,5},{7,4},{8,11},{9,10},{10,... | collective-permute-start | bytes 98312 | tf_op jit(solution)/shard_map/ppermute | solution.py:585
  26.4 1.9 %collective-permute-start.11 = (bf16[8,2048]{1,0:T(8,128)(2,1)S(1)}, bf16[8,2048]{1,0:T(8,128)(2,1)S(1)}, u32[]{:S(2)}, u32[]{:S(2)}) collective-permute-start(bf16[8,2048]{1,0:T(8,128)(2,1)S(1)} %get-tuple-element.42), channel_id=1, source_target_pairs={{0,7},{1,6},{2,5},{3,4},{4,1},{5,0},{6,3},{7,2},{8,15},{9,14},{10,... | collective-permute-start | bytes 98312 | tf_op jit(solution)/shard_map/ppermute | solution.py:585
  28.4 0.5 %collective-permute-done.9 = bf16[8,2048]{1,0:T(8,128)(2,1)S(1)} collective-permute-done((bf16[8,2048]{1,0:T(8,128)(2,1)S(1)}, bf16[8,2048]{1,0:T(8,128)(2,1)S(1)}, u32[]{:S(2)}, u32[]{:S(2)}) %collective-permute-start.9) | collective-permute-done | bytes 32800 | tf_op jit(solution)/shard_map/ppermute | solution.py:585
  28.9 0.5 %collective-permute-done.10 = bf16[8,2048]{1,0:T(8,128)(2,1)S(1)} collective-permute-done((bf16[8,2048]{1,0:T(8,128)(2,1)S(1)}, bf16[8,2048]{1,0:T(8,128)(2,1)S(1)}, u32[]{:S(2)}, u32[]{:S(2)}) %collective-permute-start.10) | collective-permute-done | bytes 32800 | tf_op jit(solution)/shard_map/ppermute | solution.py:585
  29.3 0.6 %collective-permute-done.11 = bf16[8,2048]{1,0:T(8,128)(2,1)S(1)} collective-permute-done((bf16[8,2048]{1,0:T(8,128)(2,1)S(1)}, bf16[8,2048]{1,0:T(8,128)(2,1)S(1)}, u32[]{:S(2)}, u32[]{:S(2)}) %collective-permute-start.11) | collective-permute-done | bytes 32800 | tf_op jit(solution)/shard_map/ppermute | solution.py:585
  30.0 0.6 %add_convert_fusion = bf16[8,2048]{1,0:T(8,128)(2,1)} fusion(bf16[8,2048]{1,0:T(8,128)(2,1)S(1)} %collective-permute-done.11, bf16[8,2048]{1,0:T(8,128)(2,1)S(1)} %collective-permute-done.10, f32[8,2048]{1,0:T(8,128)S(1)} %get-tuple-element.39, bf16[8,2048]{1,0:T(8,128)(2,1)S(1)} %collective-permute-done.9), kind=kLoop, calls=%fused_computation | loop fusion | flops 114688 | bytes 196608 | tf_op jit(solution)/shard_map/convert_element_type | solution.py:586
  (1 shorter events, 0.0 us)
Async XLA Ops:
  0.0 2.7 %collective-permute-start = (bf16[64,128]{1,0:T(8,128)(2,1)}, bf16[64,128]{1,0:T(8,128)(2,1)S(1)}, u32[]{:S(2)}, u32[]{:S(2)}) collective-permute-start(bf16[64,128]{1,0:T(8,128)(2,1)} %bitcast.14), channel_id=1, source_target_pairs={{0,1},{1,0},{2,3},{3,2},{4,5},{5,4},{6,7},{7,6},{8,9},{9,8},{10,11... | collective-permute-start | bytes 49160 | tf_op jit(solution)/shard_map/ppermute | solution.py:283
  2.8 21.0 %collective-permute-start.8 = (bf16[512,2048]{1,0:T(8,128)(2,1)}, bf16[512,2048]{1,0:T(8,128)(2,1)S(1)}, u32[]{:S(2)}, u32[]{:S(2)}) collective-permute-start(bf16[512,2048]{1,0:T(8,128)(2,1)} %weight_ref.1), channel_id=1, source_target_pairs={{0,1},{1,0},{2,3},{3,2},{4,5},{5,4},{6,7},{7,6},{8,9},{9,8},{10,11... | collective-permute-start | bytes 6291464 | tf_op jit(solution)/shard_map/ppermute | solution.py:283
  2.9 7.7 %collective-permute-start.1 = (bf16[592,128]{1,0:T(8,128)(2,1)S(1)}, bf16[592,128]{1,0:T(8,128)(2,1)S(1)}, u32[]{:S(2)}, u32[]{:S(2)}) collective-permute-start(bf16[592,128]{1,0:T(8,128)(2,1)S(1)} %get-tuple-element.33), channel_id=1, source_target_pairs={{0,2},{1,3},{2,0},{3,1},{4,6},{5,7},{6,4},{7,5},{8,10},{9,11},{10,... | collective-permute-start | bytes 454664 | tf_op jit(solution)/shard_map/ppermute | solution.py:283
  5.8 8.9 %collective-permute-start.2 = (bf16[592,128]{1,0:T(8,128)(2,1)S(1)}, bf16[592,128]{1,0:T(8,128)(2,1)S(1)}, u32[]{:S(2)}, u32[]{:S(2)}) collective-permute-start(bf16[592,128]{1,0:T(8,128)(2,1)S(1)} %get-tuple-element.34), channel_id=1, source_target_pairs={{0,4},{1,5},{2,6},{3,7},{4,0},{5,1},{6,2},{7,3},{8,12},{9,13},{10,... | collective-permute-start | bytes 454664 | tf_op jit(solution)/shard_map/ppermute | solution.py:283
  7.4 7.4 %collective-permute-start.3 = (bf16[592,128]{1,0:T(8,128)(2,1)S(1)}, bf16[592,128]{1,0:T(8,128)(2,1)S(1)}, u32[]{:S(2)}, u32[]{:S(2)}) collective-permute-start(bf16[592,128]{1,0:T(8,128)(2,1)S(1)} %get-tuple-element.35), channel_id=1, source_target_pairs={{0,6},{1,7},{2,4},{3,5},{4,2},{5,3},{6,0},{7,1},{8,14},{9,15},{10,... | collective-permute-start | bytes 454664 | tf_op jit(solution)/shard_map/ppermute | solution.py:283
  15.4 1.4 %collective-permute-start.4 = (f32[128,256]{1,0:T(8,128)S(1)}, f32[128,256]{1,0:T(8,128)S(1)}, u32[]{:S(2)}, u32[]{:S(2)}) collective-permute-start(f32[128,256]{1,0:T(8,128)S(1)} %shard_map.103.refs_0_), channel_id=1, source_target_pairs={{0,1},{1,0},{2,3},{3,2},{4,5},{5,4},{6,7},{7,6},{8,9},{9,8},{10,11... | collective-permute-start | bytes 393224 | tf_op jit(solution)/shard_map/ppermute | solution.py:283
  17.0 5.0 %collective-permute-start.7 = (bf16[8,1024]{1,0:T(8,128)(2,1)S(1)}, bf16[8,1024]{1,0:T(8,128)(2,1)S(1)}, u32[]{:S(2)}, u32[]{:S(2)}) collective-permute-start(bf16[8,1024]{1,0:T(8,128)(2,1)S(1)} %get-tuple-element.37), channel_id=1, source_target_pairs={{0,17},{1,16},{2,19},{3,18},{4,21},{5,20},{6,23},{7,22},{8,25},{9,... | collective-permute-start | bytes 49160 | tf_op jit(solution)/shard_map/ppermute | solution.py:456
  19.4 4.1 %collective-permute-start.6 = (bf16[8,1024]{1,0:T(8,128)(2,1)S(1)}, bf16[8,1024]{1,0:T(8,128)(2,1)S(1)}, u32[]{:S(2)}, u32[]{:S(2)}) collective-permute-start(bf16[8,1024]{1,0:T(8,128)(2,1)S(1)} %get-tuple-element.37), channel_id=1, source_target_pairs={{0,25},{1,24},{2,27},{3,26},{4,29},{5,28},{6,31},{7,30},{8,17},{9,... | collective-permute-start | bytes 49160 | tf_op jit(solution)/shard_map/ppermute | solution.py:456
  20.6 3.2 %collective-permute-start.5 = (bf16[8,1024]{1,0:T(8,128)(2,1)S(1)}, bf16[8,1024]{1,0:T(8,128)(2,1)S(1)}, u32[]{:S(2)}, u32[]{:S(2)}) collective-permute-start(bf16[8,1024]{1,0:T(8,128)(2,1)S(1)} %get-tuple-element.37), channel_id=1, source_target_pairs={{0,9},{1,8},{2,11},{3,10},{4,13},{5,12},{6,15},{7,14},{8,1},{9,0},... | collective-permute-start | bytes 49160 | tf_op jit(solution)/shard_map/ppermute | solution.py:456
  24.6 4.3 %collective-permute-start.9 = (bf16[8,2048]{1,0:T(8,128)(2,1)S(1)}, bf16[8,2048]{1,0:T(8,128)(2,1)S(1)}, u32[]{:S(2)}, u32[]{:S(2)}) collective-permute-start(bf16[8,2048]{1,0:T(8,128)(2,1)S(1)} %get-tuple-element.40), channel_id=1, source_target_pairs={{0,5},{1,4},{2,7},{3,6},{4,3},{5,2},{6,1},{7,0},{8,13},{9,12},{10,... | collective-permute-start | bytes 98312 | tf_op jit(solution)/shard_map/ppermute | solution.py:585
  26.0 3.3 %collective-permute-start.10 = (bf16[8,2048]{1,0:T(8,128)(2,1)S(1)}, bf16[8,2048]{1,0:T(8,128)(2,1)S(1)}, u32[]{:S(2)}, u32[]{:S(2)}) collective-permute-start(bf16[8,2048]{1,0:T(8,128)(2,1)S(1)} %get-tuple-element.41), channel_id=1, source_target_pairs={{0,3},{1,2},{2,1},{3,0},{4,7},{5,6},{6,5},{7,4},{8,11},{9,10},{10,... | collective-permute-start | bytes 98312 | tf_op jit(solution)/shard_map/ppermute | solution.py:585
  26.4 3.5 %collective-permute-start.11 = (bf16[8,2048]{1,0:T(8,128)(2,1)S(1)}, bf16[8,2048]{1,0:T(8,128)(2,1)S(1)}, u32[]{:S(2)}, u32[]{:S(2)}) collective-permute-start(bf16[8,2048]{1,0:T(8,128)(2,1)S(1)} %get-tuple-element.42), channel_id=1, source_target_pairs={{0,7},{1,6},{2,5},{3,4},{4,1},{5,0},{6,3},{7,2},{8,15},{9,14},{10,... | collective-permute-start | bytes 98312 | tf_op jit(solution)/shard_map/ppermute | solution.py:585

commit v8 on v7

--- a/solution.py
+++ b/solution.py
@@ -102,14 +102,13 @@
         weight = jnp.exp(score - top)
         total = total + weight
         summed = summed + weight.astype(BF16).astype(F32) * spread(step_values[u])
-    summed_high, summed_rest = in_pieces(summed, 2)
     kept = jnp.concatenate([jnp.full((rows, 1), kept_ref[h].astype(F32)) for h in range(heads)], axis=0)
     stats = lanes_of(all_rows, dim, [*in_pieces(top, 3), *in_pieces(total, 3), kept]).astype(BF16)
-    for i, part in enumerate([summed_high, summed_rest, stats, q_narrow]):
+    for i, part in enumerate([summed.astype(BF16), stats, q_narrow]):
         for h, piece in enumerate(by_head(part)):
             small[h, i * rows : (i + 1) * rows, :] = piece
     for x in range(heads):
-        out_refs[x][2 * chunk : 2 * chunk + 4 * rows, :] = small[chip ^ x]
+        out_refs[x][2 * chunk : 2 * chunk + 3 * rows, :] = small[chip ^ x]
     for copy in copies[len(held) :]:
         copy.wait()
 
@@ -133,7 +132,7 @@
         queries = ref[...].astype(F32)
         for h in range(heads):
             small[h, y * rows : (y + 1) * rows, :] = rows_of_head(queries, shape, h).astype(BF16)
-    start = 2 * chunk + 4 * rows
+    start = 2 * chunk + 3 * rows
     for x in range(heads):
         out_refs[x][start : start + len(q_refs) * rows, :] = small[chip ^ x]
 
@@ -159,13 +158,12 @@
         start = 2 * chunk
         place = pl.multiple_of((base + rank) * rows, rows)
         high = message_refs[x][start : start + rows, :].astype(F32)
-        rest = message_refs[x][start + rows : start + 2 * rows, :].astype(F32)
-        stats = message_refs[x][start + 2 * rows : start + 3 * rows, :].astype(F32)
-        start += 3 * rows
+        stats = message_refs[x][start + rows : start + 2 * rows, :].astype(F32)
+        start += 2 * rows
         for y in range(ranks):
             row = pl.multiple_of((base + (rank ^ y)) * rows, rows)
             q_all[pl.ds(row, rows), :] = message_refs[x][start + y * rows : start + (y + 1) * rows, :]
-        tails[pl.ds(place, rows), 0:dim] = high + rest
+        tails[pl.ds(place, rows), 0:dim] = high
         tail_top = stats[:, 0:1] + stats[:, 1:2] + stats[:, 2:3]
         total = stats[:, 3:4] + stats[:, 4:5] + stats[:, 5:6]
         tails[pl.ds(place, rows), dim:] = lanes_of(rows, dim, [tail_top, total])
@@ -495,7 +493,7 @@
         suffix_len.reshape(1),
     ]
     sources = [prompt_key_cache[0], prompt_value_cache[0], *fetched]
-    message = jax.ShapeDtypeStruct((2 * chunk + (ranks + 3) * rows, dim), BF16)
+    message = jax.ShapeDtypeStruct((2 * chunk + (ranks + 2) * rows, dim), BF16)
 
     def run_message(*refs):
         n, m = len(sources), len(sources) + heads
@@ -510,7 +508,7 @@
             for x in fetched
         ]
         + [
-            pltpu.VMEM((heads, 4 * rows, dim), BF16),
+            pltpu.VMEM((heads, 3 * rows, dim), BF16),
             pltpu.SemaphoreType.DMA((len(fetched) + 2 * heads,)),
         ],
     )(*[x if x.size == 1 else in_hbm(x) for x in sources])

time: 30.8 us -> 30.6 us (level)
  no operation moved by 1% of the time
where the time goes in v8:
time: 30.6 us; the launch traced here: 30.4 us
  starting transfers between devices  12.8 us (42%)
  waiting for transfers between devices  11.3 us (37%)
  Pallas kernels  4.94 us (16%)
  between operations  0.71 us (2%)
  other arithmetic  0.63 us (2%)
    ppermute x6, waiting for transfers between devices, swap(): lax.ppermute(x, axis, [(i, i ^ distance) for i in range(lax.axis_size(axi...  6.92 us
    ppermute x6, starting transfers between devices, swap(): lax.ppermute(x, axis, [(i, i ^ distance) for i in range(lax.axis_size(axi...  5.1 us
    ppermute x3, starting transfers between devices, cross(): return lax.ppermute(x, ('prompt', 'seq'), pairs)  3.94 us
    ppermute x3, starting transfers between devices, on_device(): result = result + lax.ppermute(terms[x + 1], 'seq', pairs).astype(F32)  3.74 us
    ppermute x3, waiting for transfers between devices, cross(): return lax.ppermute(x, ('prompt', 'seq'), pairs)  2.81 us
    pallas_call x1, Pallas kernels, on_device(): call(run_message, [message] * heads, [hbm] * len(sources), [(pltpu.SMEM i...  1.61 us
    pallas_call x1, Pallas kernels, on_device(): call(fetch_kernel, jax.ShapeDtypeStruct(out_weight.shape, BF16), [pl.Bloc...  1.6 us
    ppermute x3, waiting for transfers between devices, on_device(): result = result + lax.ppermute(terms[x + 1], 'seq', pairs).astype(F32)  1.6 us
  transfers between devices with their start and end apart: 12, of which 9 were waited for; matrix products, arithmetic and copies ran while one was open for 0% of the time, Pallas kernels for 13%

profile of v8, /device:TPU:0, one launch (start us, length us, event | category | flops | bytes accessed | tf_op | source)
XLA Modules:
  0.0 30.4 jit_solution(5354515300982819650)
XLA Ops:
  0.0 0.5 %collective-permute-start = (bf16[64,128]{1,0:T(8,128)(2,1)}, bf16[64,128]{1,0:T(8,128)(2,1)S(1)}, u32[]{:S(2)}, u32[]{:S(2)}) collective-permute-start(bf16[64,128]{1,0:T(8,128)(2,1)} %bitcast.14), channel_id=1, source_target_pairs={{0,1},{1,0},{2,3},{3,2},{4,5},{5,4},{6,7},{7,6},{8,9},{9,8},{10,11... | collective-permute-start | bytes 49160 | tf_op jit(solution)/shard_map/ppermute | solution.py:281
  1.1 1.6 %shard_map.100 = (bf16[576,128]{1,0:T(8,128)(2,1)S(1)}, bf16[576,128]{1,0:T(8,128)(2,1)S(1)}, bf16[576,128]{1,0:T(8,128)(2,1)S(1)}, bf16[576,128]{1,0:T(8,128)(2,1)S(1)}) custom-call(bf16[4,256,128]{2,1,0:T(8,128)(2,1)} %bitcast.10, bf16[4,256,128]{2,1,0:T(8,128)(2,1)} %bitcast.11, bf16[64,128]{1,0:T(8,128)(2,1)} %bitcast.15, bf16[4,256,128]{2,1,0:T(8,128)(2,1)} %bitcast.12, ...), custom_call_target="tpu_custom_call" | custom-call | tf_op jit(solution)/shard_map/pallas_call | solution.py:502
  2.7 0.0 collective-permute-done.refs_0_
  2.8 0.1 collective-permute-start.8
  2.9 2.9 %collective-permute-start.1 = (bf16[576,128]{1,0:T(8,128)(2,1)S(1)}, bf16[576,128]{1,0:T(8,128)(2,1)S(1)}, u32[]{:S(2)}, u32[]{:S(2)}) collective-permute-start(bf16[576,128]{1,0:T(8,128)(2,1)S(1)} %get-tuple-element.33), channel_id=1, source_target_pairs={{0,2},{1,3},{2,0},{3,1},{4,6},{5,7},{6,4},{7,5},{8,10},{9,11},{10,... | collective-permute-start | bytes 442376 | tf_op jit(solution)/shard_map/ppermute | solution.py:281
  5.8 1.5 %collective-permute-start.2 = (bf16[576,128]{1,0:T(8,128)(2,1)S(1)}, bf16[576,128]{1,0:T(8,128)(2,1)S(1)}, u32[]{:S(2)}, u32[]{:S(2)}) collective-permute-start(bf16[576,128]{1,0:T(8,128)(2,1)S(1)} %get-tuple-element.34), channel_id=1, source_target_pairs={{0,4},{1,5},{2,6},{3,7},{4,0},{5,1},{6,2},{7,3},{8,12},{9,13},{10,... | collective-permute-start | bytes 442376 | tf_op jit(solution)/shard_map/ppermute | solution.py:281
  7.3 0.0 collective-permute-start.3
  7.3 1.6 %shard_map.102.refs_4_ = bf16[512,2048]{1,0:T(8,128)(2,1)S(1)} custom-call(bf16[576,128]{1,0:T(8,128)(2,1)S(1)} %get-tuple-element.32.after_ref.refs_0_, bf16[512,2048]{1,0:T(8,128)(2,1)} %weight_ref.1), custom_call_target="tpu_custom_call" | custom-call | tf_op jit(solution)/shard_map/pallas_call | solution.py:530
  9.0 1.4 %collective-permute-done.1.refs_1_ = bf16[576,128]{1,0:T(8,128)(2,1)S(1)} collective-permute-done((bf16[576,128]{1,0:T(8,128)(2,1)S(1)}, bf16[576,128]{1,0:T(8,128)(2,1)S(1)}, u32[]{:S(2)}, u32[]{:S(2)}) %collective-permute-start.1) | collective-permute-done | bytes 147488 | tf_op jit(solution)/shard_map/ppermute | solution.py:281
  10.4 4.2 %collective-permute-done.2.refs_2_ = bf16[576,128]{1,0:T(8,128)(2,1)S(1)} collective-permute-done((bf16[576,128]{1,0:T(8,128)(2,1)S(1)}, bf16[576,128]{1,0:T(8,128)(2,1)S(1)}, u32[]{:S(2)}, u32[]{:S(2)}) %collective-permute-start.2) | collective-permute-done | bytes 147488 | tf_op jit(solution)/shard_map/ppermute | solution.py:281
  14.5 0.0 collective-permute-done.3.refs_3_
  14.5 0.6 %shard_map.103.refs_0_ = f32[128,256]{1,0:T(8,128)S(1)} custom-call(bf16[576,128]{1,0:T(8,128)(2,1)S(1)} %get-tuple-element.32.after_ref.refs_0_, bf16[576,128]{1,0:T(8,128)(2,1)S(1)} %collective-permute-done.1.refs_1_, bf16[576,128]{1,0:T(8,128)(2,1)S(1)} %collective-permute-done.2.refs_2_, bf16[576,128]{1,0:T(8,128)(2,1)S(1)} %collective-permute-done.3.refs_3_, ...), custom_call_target="tpu_custom_call" | custom-call | tf_op jit(solution)/shard_map/pallas_call | solution.py:543
  15.2 0.1 collective-permute-start.4
  15.3 1.3 %collective-permute-done.4.refs_1_ = f32[128,256]{1,0:T(8,128)S(1)} collective-permute-done((f32[128,256]{1,0:T(8,128)S(1)}, f32[128,256]{1,0:T(8,128)S(1)}, u32[]{:S(2)}, u32[]{:S(2)}) %collective-permute-start.4) | collective-permute-done | bytes 131104 | tf_op jit(solution)/shard_map/ppermute | solution.py:281
  16.6 0.2 shard_map.104
  16.8 2.4 %collective-permute-start.7 = (bf16[8,1024]{1,0:T(8,128)(2,1)S(1)}, bf16[8,1024]{1,0:T(8,128)(2,1)S(1)}, u32[]{:S(2)}, u32[]{:S(2)}) collective-permute-start(bf16[8,1024]{1,0:T(8,128)(2,1)S(1)} %get-tuple-element.37), channel_id=1, source_target_pairs={{0,17},{1,16},{2,19},{3,18},{4,21},{5,20},{6,23},{7,22},{8,25},{9,... | collective-permute-start | bytes 49160 | tf_op jit(solution)/shard_map/ppermute | solution.py:454
  19.2 1.2 %collective-permute-start.6 = (bf16[8,1024]{1,0:T(8,128)(2,1)S(1)}, bf16[8,1024]{1,0:T(8,128)(2,1)S(1)}, u32[]{:S(2)}, u32[]{:S(2)}) collective-permute-start(bf16[8,1024]{1,0:T(8,128)(2,1)S(1)} %get-tuple-element.37), channel_id=1, source_target_pairs={{0,25},{1,24},{2,27},{3,26},{4,29},{5,28},{6,31},{7,30},{8,17},{9,... | collective-permute-start | bytes 49160 | tf_op jit(solution)/shard_map/ppermute | solution.py:454
  20.4 0.3 %collective-permute-start.5 = (bf16[8,1024]{1,0:T(8,128)(2,1)S(1)}, bf16[8,1024]{1,0:T(8,128)(2,1)S(1)}, u32[]{:S(2)}, u32[]{:S(2)}) collective-permute-start(bf16[8,1024]{1,0:T(8,128)(2,1)S(1)} %get-tuple-element.37), channel_id=1, source_target_pairs={{0,9},{1,8},{2,11},{3,10},{4,13},{5,12},{6,15},{7,14},{8,1},{9,0},... | collective-permute-start | bytes 49160 | tf_op jit(solution)/shard_map/ppermute | solution.py:454
  20.8 1.1 %collective-permute-done.7.refs_3_ = bf16[8,1024]{1,0:T(8,128)(2,1)S(1)} collective-permute-done((bf16[8,1024]{1,0:T(8,128)(2,1)S(1)}, bf16[8,1024]{1,0:T(8,128)(2,1)S(1)}, u32[]{:S(2)}, u32[]{:S(2)}) %collective-permute-start.7) | collective-permute-done | bytes 16416 | tf_op jit(solution)/shard_map/ppermute | solution.py:454
  21.8 1.5 %collective-permute-done.6.refs_2_ = bf16[8,1024]{1,0:T(8,128)(2,1)S(1)} collective-permute-done((bf16[8,1024]{1,0:T(8,128)(2,1)S(1)}, bf16[8,1024]{1,0:T(8,128)(2,1)S(1)}, u32[]{:S(2)}, u32[]{:S(2)}) %collective-permute-start.6) | collective-permute-done | bytes 16416 | tf_op jit(solution)/shard_map/ppermute | solution.py:454
  23.3 0.3 collective-permute-done.5.refs_1_
  23.6 0.0 collective-permute-done.8.refs_5_
  23.6 0.8 %shard_map.105 = (f32[8,2048]{1,0:T(8,128)S(1)}, bf16[8,2048]{1,0:T(8,128)(2,1)S(1)}, bf16[8,2048]{1,0:T(8,128)(2,1)S(1)}, bf16[8,2048]{1,0:T(8,128)(2,1)S(1)}) custom-call(bf16[8,1024]{1,0:T(8,128)(2,1)S(1)} %get-tuple-element.36.refs_0_, bf16[8,1024]{1,0:T(8,128)(2,1)S(1)} %collective-permute-done.5.refs_1_, ...), custom_call_target="tpu_custom_call" | custom-call | tf_op jit(solution)/shard_map/pallas_call | solution.py:571
  24.4 1.4 %collective-permute-start.9 = (bf16[8,2048]{1,0:T(8,128)(2,1)S(1)}, bf16[8,2048]{1,0:T(8,128)(2,1)S(1)}, u32[]{:S(2)}, u32[]{:S(2)}) collective-permute-start(bf16[8,2048]{1,0:T(8,128)(2,1)S(1)} %get-tuple-element.40), channel_id=1, source_target_pairs={{0,5},{1,4},{2,7},{3,6},{4,3},{5,2},{6,1},{7,0},{8,13},{9,12},{10,... | collective-permute-start | bytes 98312 | tf_op jit(solution)/shard_map/ppermute | solution.py:583
  25.8 0.4 %collective-permute-start.10 = (bf16[8,2048]{1,0:T(8,128)(2,1)S(1)}, bf16[8,2048]{1,0:T(8,128)(2,1)S(1)}, u32[]{:S(2)}, u32[]{:S(2)}) collective-permute-start(bf16[8,2048]{1,0:T(8,128)(2,1)S(1)} %get-tuple-element.41), channel_id=1, source_target_pairs={{0,3},{1,2},{2,1},{3,0},{4,7},{5,6},{6,5},{7,4},{8,11},{9,10},{10,... | collective-permute-start | bytes 98312 | tf_op jit(solution)/shard_map/ppermute | solution.py:583
  26.2 1.9 %collective-permute-start.11 = (bf16[8,2048]{1,0:T(8,128)(2,1)S(1)}, bf16[8,2048]{1,0:T(8,128)(2,1)S(1)}, u32[]{:S(2)}, u32[]{:S(2)}) collective-permute-start(bf16[8,2048]{1,0:T(8,128)(2,1)S(1)} %get-tuple-element.42), channel_id=1, source_target_pairs={{0,7},{1,6},{2,5},{3,4},{4,1},{5,0},{6,3},{7,2},{8,15},{9,14},{10,... | collective-permute-start | bytes 98312 | tf_op jit(solution)/shard_map/ppermute | solution.py:583
  28.2 0.5 %collective-permute-done.9 = bf16[8,2048]{1,0:T(8,128)(2,1)S(1)} collective-permute-done((bf16[8,2048]{1,0:T(8,128)(2,1)S(1)}, bf16[8,2048]{1,0:T(8,128)(2,1)S(1)}, u32[]{:S(2)}, u32[]{:S(2)}) %collective-permute-start.9) | collective-permute-done | bytes 32800 | tf_op jit(solution)/shard_map/ppermute | solution.py:583
  28.7 0.5 %collective-permute-done.10 = bf16[8,2048]{1,0:T(8,128)(2,1)S(1)} collective-permute-done((bf16[8,2048]{1,0:T(8,128)(2,1)S(1)}, bf16[8,2048]{1,0:T(8,128)(2,1)S(1)}, u32[]{:S(2)}, u32[]{:S(2)}) %collective-permute-start.10) | collective-permute-done | bytes 32800 | tf_op jit(solution)/shard_map/ppermute | solution.py:583
  29.2 0.6 %collective-permute-done.11 = bf16[8,2048]{1,0:T(8,128)(2,1)S(1)} collective-permute-done((bf16[8,2048]{1,0:T(8,128)(2,1)S(1)}, bf16[8,2048]{1,0:T(8,128)(2,1)S(1)}, u32[]{:S(2)}, u32[]{:S(2)}) %collective-permute-start.11) | collective-permute-done | bytes 32800 | tf_op jit(solution)/shard_map/ppermute | solution.py:583
  29.8 0.6 %add_convert_fusion = bf16[8,2048]{1,0:T(8,128)(2,1)} fusion(bf16[8,2048]{1,0:T(8,128)(2,1)S(1)} %collective-permute-done.11, bf16[8,2048]{1,0:T(8,128)(2,1)S(1)} %collective-permute-done.10, f32[8,2048]{1,0:T(8,128)S(1)} %get-tuple-element.39, bf16[8,2048]{1,0:T(8,128)(2,1)S(1)} %collective-permute-done.9), kind=kLoop, calls=%fused_computation | loop fusion | flops 114688 | bytes 196608 | tf_op jit(solution)/shard_map/convert_element_type | solution.py:584
  (1 shorter events, 0.0 us)
Async XLA Ops:
  0.0 2.7 %collective-permute-start = (bf16[64,128]{1,0:T(8,128)(2,1)}, bf16[64,128]{1,0:T(8,128)(2,1)S(1)}, u32[]{:S(2)}, u32[]{:S(2)}) collective-permute-start(bf16[64,128]{1,0:T(8,128)(2,1)} %bitcast.14), channel_id=1, source_target_pairs={{0,1},{1,0},{2,3},{3,2},{4,5},{5,4},{6,7},{7,6},{8,9},{9,8},{10,11... | collective-permute-start | bytes 49160 | tf_op jit(solution)/shard_map/ppermute | solution.py:281
  2.8 20.8 %collective-permute-start.8 = (bf16[512,2048]{1,0:T(8,128)(2,1)}, bf16[512,2048]{1,0:T(8,128)(2,1)S(1)}, u32[]{:S(2)}, u32[]{:S(2)}) collective-permute-start(bf16[512,2048]{1,0:T(8,128)(2,1)} %weight_ref.1), channel_id=1, source_target_pairs={{0,1},{1,0},{2,3},{3,2},{4,5},{5,4},{6,7},{7,6},{8,9},{9,8},{10,11... | collective-permute-start | bytes 6291464 | tf_op jit(solution)/shard_map/ppermute | solution.py:281
  2.9 7.5 %collective-permute-start.1 = (bf16[576,128]{1,0:T(8,128)(2,1)S(1)}, bf16[576,128]{1,0:T(8,128)(2,1)S(1)}, u32[]{:S(2)}, u32[]{:S(2)}) collective-permute-start(bf16[576,128]{1,0:T(8,128)(2,1)S(1)} %get-tuple-element.33), channel_id=1, source_target_pairs={{0,2},{1,3},{2,0},{3,1},{4,6},{5,7},{6,4},{7,5},{8,10},{9,11},{10,... | collective-permute-start | bytes 442376 | tf_op jit(solution)/shard_map/ppermute | solution.py:281
  5.8 8.7 %collective-permute-start.2 = (bf16[576,128]{1,0:T(8,128)(2,1)S(1)}, bf16[576,128]{1,0:T(8,128)(2,1)S(1)}, u32[]{:S(2)}, u32[]{:S(2)}) collective-permute-start(bf16[576,128]{1,0:T(8,128)(2,1)S(1)} %get-tuple-element.34), channel_id=1, source_target_pairs={{0,4},{1,5},{2,6},{3,7},{4,0},{5,1},{6,2},{7,3},{8,12},{9,13},{10,... | collective-permute-start | bytes 442376 | tf_op jit(solution)/shard_map/ppermute | solution.py:281
  7.3 7.2 %collective-permute-start.3 = (bf16[576,128]{1,0:T(8,128)(2,1)S(1)}, bf16[576,128]{1,0:T(8,128)(2,1)S(1)}, u32[]{:S(2)}, u32[]{:S(2)}) collective-permute-start(bf16[576,128]{1,0:T(8,128)(2,1)S(1)} %get-tuple-element.35), channel_id=1, source_target_pairs={{0,6},{1,7},{2,4},{3,5},{4,2},{5,3},{6,0},{7,1},{8,14},{9,15},{10,... | collective-permute-start | bytes 442376 | tf_op jit(solution)/shard_map/ppermute | solution.py:281
  15.2 1.4 %collective-permute-start.4 = (f32[128,256]{1,0:T(8,128)S(1)}, f32[128,256]{1,0:T(8,128)S(1)}, u32[]{:S(2)}, u32[]{:S(2)}) collective-permute-start(f32[128,256]{1,0:T(8,128)S(1)} %shard_map.103.refs_0_), channel_id=1, source_target_pairs={{0,1},{1,0},{2,3},{3,2},{4,5},{5,4},{6,7},{7,6},{8,9},{9,8},{10,11... | collective-permute-start | bytes 393224 | tf_op jit(solution)/shard_map/ppermute | solution.py:281
  16.8 5.0 %collective-permute-start.7 = (bf16[8,1024]{1,0:T(8,128)(2,1)S(1)}, bf16[8,1024]{1,0:T(8,128)(2,1)S(1)}, u32[]{:S(2)}, u32[]{:S(2)}) collective-permute-start(bf16[8,1024]{1,0:T(8,128)(2,1)S(1)} %get-tuple-element.37), channel_id=1, source_target_pairs={{0,17},{1,16},{2,19},{3,18},{4,21},{5,20},{6,23},{7,22},{8,25},{9,... | collective-permute-start | bytes 49160 | tf_op jit(solution)/shard_map/ppermute | solution.py:454
  19.2 4.1 %collective-permute-start.6 = (bf16[8,1024]{1,0:T(8,128)(2,1)S(1)}, bf16[8,1024]{1,0:T(8,128)(2,1)S(1)}, u32[]{:S(2)}, u32[]{:S(2)}) collective-permute-start(bf16[8,1024]{1,0:T(8,128)(2,1)S(1)} %get-tuple-element.37), channel_id=1, source_target_pairs={{0,25},{1,24},{2,27},{3,26},{4,29},{5,28},{6,31},{7,30},{8,17},{9,... | collective-permute-start | bytes 49160 | tf_op jit(solution)/shard_map/ppermute | solution.py:454
  20.4 3.2 %collective-permute-start.5 = (bf16[8,1024]{1,0:T(8,128)(2,1)S(1)}, bf16[8,1024]{1,0:T(8,128)(2,1)S(1)}, u32[]{:S(2)}, u32[]{:S(2)}) collective-permute-start(bf16[8,1024]{1,0:T(8,128)(2,1)S(1)} %get-tuple-element.37), channel_id=1, source_target_pairs={{0,9},{1,8},{2,11},{3,10},{4,13},{5,12},{6,15},{7,14},{8,1},{9,0},... | collective-permute-start | bytes 49160 | tf_op jit(solution)/shard_map/ppermute | solution.py:454
  24.4 4.3 %collective-permute-start.9 = (bf16[8,2048]{1,0:T(8,128)(2,1)S(1)}, bf16[8,2048]{1,0:T(8,128)(2,1)S(1)}, u32[]{:S(2)}, u32[]{:S(2)}) collective-permute-start(bf16[8,2048]{1,0:T(8,128)(2,1)S(1)} %get-tuple-element.40), channel_id=1, source_target_pairs={{0,5},{1,4},{2,7},{3,6},{4,3},{5,2},{6,1},{7,0},{8,13},{9,12},{10,... | collective-permute-start | bytes 98312 | tf_op jit(solution)/shard_map/ppermute | solution.py:583
  25.8 3.3 %collective-permute-start.10 = (bf16[8,2048]{1,0:T(8,128)(2,1)S(1)}, bf16[8,2048]{1,0:T(8,128)(2,1)S(1)}, u32[]{:S(2)}, u32[]{:S(2)}) collective-permute-start(bf16[8,2048]{1,0:T(8,128)(2,1)S(1)} %get-tuple-element.41), channel_id=1, source_target_pairs={{0,3},{1,2},{2,1},{3,0},{4,7},{5,6},{6,5},{7,4},{8,11},{9,10},{10,... | collective-permute-start | bytes 98312 | tf_op jit(solution)/shard_map/ppermute | solution.py:583
  26.2 3.5 %collective-permute-start.11 = (bf16[8,2048]{1,0:T(8,128)(2,1)S(1)}, bf16[8,2048]{1,0:T(8,128)(2,1)S(1)}, u32[]{:S(2)}, u32[]{:S(2)}) collective-permute-start(bf16[8,2048]{1,0:T(8,128)(2,1)S(1)} %get-tuple-element.42), channel_id=1, source_target_pairs={{0,7},{1,6},{2,5},{3,4},{4,1},{5,0},{6,3},{7,2},{8,15},{9,14},{10,... | collective-permute-start | bytes 98312 | tf_op jit(solution)/shard_map/ppermute | solution.py:583
